TPU v7x, 32 devices: a whole 2x2x4 slice. The times are simulated.
32 devices in a mesh: grp: 2 (over y), mom: 4 (over z), orb: 2 (over x), ff: 2 (over core).
Axes of the slice: x: 2, y: 2, z: 4, core: 2. Of those that a mesh axis runs over, the one named last changes fastest.
Arguments:
- vertex_own: bfloat16 [64, 468, 468], P(('grp', 'mom'), 'orb', 'ff'), parts along dimension 0, may hold values from -6 to 6
- vertex_cross: bfloat16 [64, 468, 468], P(('grp', 'mom'), 'orb', 'ff'), parts along dimension 0, may hold values from -6 to 6
- project_coeff: bfloat16 [32, 32, 13, 13], P('mom'), may hold values from -0.3125 to 0.3125
- green_left: float32 [72, 2304], P('grp'), parts along dimension 0, may hold values from -6 to 6
- green_right: float32 [72, 2304], P('grp'), parts along dimension 0, may hold values from -0.30769232 to 0.30769232
- window: int32 [32], replicated, may hold values from 0 to 2303, as said below
- shifts: int32 [13, 2], replicated, may hold values from -3 to 3, as said below
Outputs:
- new_vertex: bfloat16 [64, 468, 468], P(('grp', 'mom'), 'orb', 'ff'), parts along dimension 0
There are 2 independent parts, one for each index of `grp`. A program takes and returns all parts, laid end to end along the dimension named above; an argument that names none is the same for every part. Nothing has to cross between parts.
Inputs may be any that keep to these rules, and one draw needn't show every extreme that they name: `window`: 32 distinct lattice indices kx * 48 + ky. `shifts`: 13 distinct vectors (x, y) with x > 0, or x = 0 and y >= 0.
All inputs are finite; a program needn't handle non-finite values.
Results may differ from a plain program's by a relative error of at most 0.0066.
Values may be sent and summed in bfloat16 or wider, within the bound.
A program may use at most 128 MiB of HBM per device.

v0:
```python
import math

import jax
import jax.numpy as jnp
from jax import lax
from jax.sharding import PartitionSpec as P

LX = 48


def form_factors(shifts, momenta):
    row_x = momenta // LX
    row_y = momenta % LX
    turn_count = (shifts[:, 0:1] * row_x[None, :] + shifts[:, 1:2] * row_y[None, :]) % LX
    phases = turn_count.astype(jnp.float32) * (2.0 * math.pi / LX)
    anchor = (shifts[:, 0] == 0) & (shifts[:, 1] == 0)
    weight = jnp.where(anchor, 1.0, math.sqrt(2.0)).astype(jnp.float32)
    return weight[:, None] * jnp.cos(phases)


def folded_all(momenta, qpoints):
    row_x = (momenta[None, :] // LX + qpoints[:, None] // LX) % LX
    row_y = (momenta[None, :] % LX + qpoints[:, None] % LX) % LX
    return row_x * LX + row_y


def loop_left(green_part, form_table):
    loop_rows = green_part[:, None, :] * form_table[None, :, :]
    return loop_rows.reshape(-1, form_table.shape[1]).astype(jnp.bfloat16)


def loop_right_all(green_right, form_table, momenta, qpoints, total_count):
    picked = jnp.take(green_right, folded_all(momenta, qpoints), axis=1)
    picked = jnp.transpose(picked, (1, 0, 2))
    loop_rows = picked[:, :, None, :] * form_table[None, None, :, :] * (1.0 / total_count)
    return loop_rows.reshape(qpoints.shape[0], -1, momenta.shape[0]).astype(jnp.bfloat16)


def bubble_change(row_block, column_block, left_loop, right_loop):
    carried = jnp.einsum(
        "qrj,jk->qrk", row_block, left_loop, preferred_element_type=jnp.float32
    ).astype(jnp.bfloat16)
    returned = jnp.einsum(
        "qjk,qjc->qkc", right_loop, column_block, preferred_element_type=jnp.float32
    ).astype(jnp.bfloat16)
    return jnp.einsum("qrk,qkc->qrc", carried, returned, preferred_element_type=jnp.float32)


def body(vertex_own, vertex_cross, project_coeff, green_left, green_right, window, shifts):
    points, row_count, col_count = vertex_own.shape
    form_count = shifts.shape[0]
    pair_rows = row_count // form_count
    total_k = green_left.shape[1]
    my_start = lax.axis_index("mom") * points
    my_window = lax.dynamic_slice_in_dim(window, my_start, points, 0)
    arrived = lax.all_gather(vertex_cross, "mom", axis=0, tiled=True)
    count = arrived.shape[0]
    tiles = arrived.reshape(count, pair_rows, form_count, col_count)
    projected = jnp.einsum(
        "qplm,pamc->qalc", project_coeff, tiles, preferred_element_type=jnp.float32
    )
    merged = (
        vertex_own.astype(jnp.float32) + projected.reshape(points, row_count, col_count)
    ).astype(jnp.bfloat16)
    wide_block = lax.all_gather(merged, "ff", axis=2, tiled=True)
    col_start = lax.axis_index("ff") * col_count
    full_block = lax.all_gather(wide_block, "orb", axis=1, tiled=True)
    part_k = total_k // lax.axis_size("orb")
    k_start = lax.axis_index("orb") * part_k
    loop_index = k_start + jnp.arange(part_k, dtype=jnp.int32)
    form_table = form_factors(shifts, loop_index)
    left_loop = loop_left(lax.dynamic_slice_in_dim(green_left, k_start, part_k, 1), form_table)
    right_loop = loop_right_all(green_right, form_table, loop_index, my_window, total_k)
    tall_block = lax.dynamic_slice_in_dim(full_block, col_start, col_count, 2)
    partial_value = bubble_change(full_block, tall_block, left_loop, right_loop)
    change = lax.psum_scatter(partial_value, "orb", scatter_dimension=1, tiled=True)
    return (merged.astype(jnp.float32) + change).astype(jnp.bfloat16)


def solution(mesh):
    return jax.shard_map(
        body,
        mesh=mesh,
        in_specs=(
            P(("grp", "mom"), "orb", "ff"),
            P(("grp", "mom"), "orb", "ff"),
            P("mom", None, None, None),
            P("grp", None),
            P("grp", None),
            P(),
            P(),
        ),
        out_specs=P(("grp", "mom"), "orb", "ff"),
        check_vma=False,
    )
```

profile of v0, /device:TPU:0, one launch (start us, length us, event | category | flops | bytes accessed | tf_op | source)
XLA Modules:
  0.0 266.8 jit_solution(14398249234729252671)
XLA Ops:
  6.5 0.7 all-gather.4.cloned.1.call-update
  7.3 0.0 all-gather.6.cloned.1.call-start
  7.3 79.0 %all-gather.4.cloned.1.call-done = bf16[32,234,234]{2,0,1:T(8,128)(2,1)} async-done(((bf16[8,234,234]{2,0,1:T(8,128)(2,1)}), bf16[32,234,234]{2,0,1:T(8,128)(2,1)}) %all-gather.4.cloned.1.call-update) | async-done | bytes 3504400 | tf_op jit(solution)/shard_map/all_gather | solution.py:56
  86.3 3.0 %convolution_bitcast_fusion = f32[8,18,13,234]{3,2,0,1:T(8,128)S(1)} fusion(bf16[32,18,13,234,1]{3,0,2,4,1:T(8,128)(2,1)} %bitcast.40, bf16[8,32,13,13]{1,0,3,2:T(8,128)(2,1)} %param.9), kind=kOutput, calls=%fused_computation.16 | convolution fusion | flops 364455936 | bytes 5343104 | tf_op jit(solution)/shard_map/qplm,pamc->qalc/dot_general | solution.py:59
  89.3 1.6 copy.21
  90.9 0.2 fusion.14
  91.1 2.2 copy.22
  93.3 0.0 all-gather.6.cloned.1.call-update
  93.3 0.0 all-gather.8.cloned.1.call-start
  93.4 8.6 %all-gather.6.cloned.1.call-done = bf16[8,234,468]{1,0,2:T(8,128)(2,1)} async-done(((bf16[8,234,234]{1,0,2:T(8,128)(2,1)}), bf16[8,234,468]{1,0,2:T(8,128)(2,1)}) %all-gather.6.cloned.1.call-update) | async-done | bytes 1752208 | tf_op jit(solution)/shard_map/all_gather | solution.py:65
  102.0 4.8 %copy.23 = bf16[8,234,468]{2,0,1:T(8,128)(2,1)} copy(bf16[8,234,468]{1,0,2:T(8,128)(2,1)} %all-gather.6.cloned.1.call-done) | data formatting | bytes 3504384 | tf_op jit(solution)/shard_map/all_gather | solution.py:65
  106.8 0.0 all-gather.8.cloned.1.call-update
  106.9 0.0 reduce-scatter.2.cloned.1.call-start
  106.9 0.1 and_select_fusion.1
  107.0 0.1 compare_select_fusion
  107.2 0.4 copy.25
  107.6 1.7 mul.144
  109.3 3.4 %mul.145 = f32[468,1152]{1,0:T(8,128)} reshape(f32[36,13,1152]{2,1,0:T(8,128)} %mul.144) | data formatting | bytes 4313088 | tf_op jit(solution)/shard_map/mul | solution.py:28
  112.7 0.4 fusion.22
  113.1 1.7 mul.159
  114.8 3.6 %mul.160 = f32[468,1152]{1,0:T(8,128)} reshape(f32[36,13,1152]{2,1,0:T(8,128)} %mul.159) | data formatting | bytes 4313088 | tf_op jit(solution)/shard_map/mul | solution.py:28
  118.4 31.2 %gather_fusion = f32[9216,36]{1,0:T(8,128)} fusion(f32[36,2304]{0,1:T(8,128)S(1)} %copy.25, s32[9216]{0:T(1024)S(1)} %broadcast_clamp_fusion), kind=kCustom, calls=%fused_computation | custom fusion | bytes 2691072 | tf_op jit(solution)/shard_map/jit(_take)/gather | solution.py:33
  149.6 0.1 compare_and_fusion
  149.7 6.7 %select_bitcast_fusion = f32[8,36,1152]{1,2,0:T(8,128)} fusion(f32[8,1152,36]{2,1,0:T(8,128)} %bitcast.39, pred[8,1152]{1,0:T(8,128)(4,1)S(1)} %compare_and_fusion), kind=kLoop, calls=%fused_computation.8 | loop fusion | flops 331776 | bytes 2663424 | tf_op jit(solution)/shard_map/jit(_take)/select_n | solution.py:33
  156.4 5.1 %copy.26 = f32[8,36,1152]{2,0,1:T(8,128)} copy(f32[8,36,1152]{1,2,0:T(8,128)} %select_bitcast_fusion) | data formatting | bytes 2654208 | tf_op jit(solution)/shard_map/jit(_take)/select_n | solution.py:33
  161.5 6.9 %fusion.1 = bf16[8,468,1152]{2,0,1:T(8,128)(2,1)} fusion(f32[468,1152]{1,0:T(8,128)S(1)} %copy-done.2, f32[8,36,1152]{2,0,1:T(8,128)} %copy.26), kind=kLoop, calls=%fused_computation.3 | loop fusion | flops 12939264 | bytes 12109824 | tf_op jit(solution)/shard_map/convert_element_type | solution.py:36
  168.4 4.3 %constant_dynamic-slice_fusion = bf16[8,468,234]{2,0,1:T(8,128)(2,1)} fusion(bf16[8,468,468]{2,0,1:T(8,128)(2,1)} %all-gather.8.cloned.1.call-done, s32[]{:T(128)S(6)} %select_n.144), kind=kLoop, calls=%fused_computation.69 | loop fusion | bytes 3504388 | tf_op jit(solution)/shard_map/dynamic_slice | solution.py:74
  172.7 12.3 %convolution_convert_fusion = bf16[8,468,1152]{2,1,0:T(8,128)(2,1)} fusion(bf16[8,468,468]{2,0,1:T(8,128)(2,1)} %all-gather.8.cloned.1.call-done, f32[468,1152]{1,0:T(8,128)S(1)} %copy-done.3, f32[468,1152]{1,0:T(8,128)S(1)} %copy-done.2), kind=kOutput, calls=%fused_computation.4 | convolution fusion | flops 4042441728 | bytes 16443648 | tf_op jit(solution)/shard_map/qrj,jk->qrk/dot_general | solution.py:40
  185.0 15.0 %fusion.11 = f32[8,468,234]{2,1,0:T(8,128)} fusion(bf16[8,468,1152]{2,1,0:T(8,128)(2,1)} %convolution_convert_fusion, bf16[8,468,1152]{2,0,1:T(8,128)(2,1)} %fusion.1, bf16[8,468,234]{2,0,1:T(8,128)(2,1)} %constant_dynamic-slice_fusion), kind=kOutput, calls=%fused_computation.12 | convolution fusion | flops 4039206912 | bytes 22508928 | tf_op jit(solution)/shard_map/qrk,qkc->qrc/dot_general | solution.py:46
  200.0 5.1 %copy.29 = f32[8,468,234]{2,0,1:T(8,128)} copy(f32[8,468,234]{2,1,0:T(8,128)} %fusion.11) | data formatting | bytes 7008768 | tf_op jit(solution)/shard_map/qrk,qkc->qrc/dot_general | solution.py:46
  205.2 52.3 %reduce-scatter.2.cloned.1.call-done = f32[8,234,234]{2,0,1:T(8,128)} async-done(((f32[8,468,234]{2,0,1:T(8,128)}), f32[8,234,234]{2,0,1:T(8,128)}) %reduce-scatter.2.cloned.1.call-update) | async-done | bytes 1752208 | tf_op jit(solution)/shard_map/reduce_scatter | solution.py:76
  257.5 2.7 %add_convert_fusion = bf16[8,234,234]{2,0,1:T(8,128)(2,1)} fusion(f32[8,234,234]{2,0,1:T(8,128)} %reduce-scatter.2.cloned.1.call-done, bf16[8,234,234]{2,0,1:T(8,128)(2,1)S(1)} %fusion.14), kind=kLoop, calls=%fused_computation.15 | loop fusion | flops 1314144 | bytes 3504384 | tf_op jit(solution)/shard_map/convert_element_type | solution.py:77
  (25 shorter events, 0.1 us)
Async XLA Ops:
  6.5 101.0 %copy-start = (f32[36,2304]{1,0:T(8,128)S(1)}, f32[36,2304]{1,0:T(8,128)}, u32[]{:S(2)}) copy-start(f32[36,2304]{1,0:T(8,128)} %param.10) | copy-start | bytes 995332
  6.5 79.8 %all-gather.4.cloned.1.call-start = ((), (), s32[]{:S(2)}) async-start(), calls=%async_computation.1 | async-start | bytes 4792320 | tf_op jit(solution)/shard_map/all_gather | solution.py:56
  7.3 94.7 %all-gather.6.cloned.1.call-start = ((), (), s32[]{:S(2)}) async-start(), calls=%async_computation.2 | async-start | bytes 2875392 | tf_op jit(solution)/shard_map/all_gather | solution.py:65
  89.3 1.6 copy-start.4
  93.3 13.6 %copy-start.7 = (s32[32]{0:T(128)S(1)}, s32[32]{0:T(128)}, u32[]{:S(2)}) copy-start(s32[32]{0:T(128)} %param.12) | copy-start | bytes 388
  93.3 13.9 %copy-start.5 = (f32[36,2304]{1,0:T(8,128)S(1)}, f32[36,2304]{1,0:T(8,128)}, u32[]{:S(2)}) copy-start(f32[36,2304]{1,0:T(8,128)} %param.11) | copy-start | bytes 995332
  93.3 75.1 %all-gather.8.cloned.1.call-start = ((), (), s32[]{:S(2)}) async-start(), calls=%async_computation.3 | async-start | bytes 5750784 | tf_op jit(solution)/shard_map/all_gather | solution.py:67
  106.9 150.6 %reduce-scatter.2.cloned.1.call-start = ((), (), s32[]{:S(2)}) async-start(), calls=%async_computation.4 | async-start | bytes 5750784 | tf_op jit(solution)/shard_map/reduce_scatter | solution.py:76
  107.6 5.1 %copy-start.6 = (s32[13,2]{0,1:T(2,128)S(1)}, s32[13,2]{0,1:T(2,128)}, u32[]{:S(2)}) copy-start(s32[13,2]{0,1:T(2,128)} %param.13) | copy-start | bytes 316
  156.4 5.1 %copy-start.2 = (f32[468,1152]{1,0:T(8,128)S(1)}, f32[468,1152]{1,0:T(8,128)}, u32[]{:S(2)}) copy-start(f32[468,1152]{1,0:T(8,128)} %mul.160) | copy-start | bytes 6469636
  168.4 4.3 %copy-start.3 = (f32[468,1152]{1,0:T(8,128)S(1)}, f32[468,1152]{1,0:T(8,128)}, u32[]{:S(2)}) copy-start(f32[468,1152]{1,0:T(8,128)} %mul.145) | copy-start | bytes 6469636
  205.2 55.1 %copy-start.1 = (f32[36,2304]{1,0:T(8,128)S(1)}, f32[36,2304]{1,0:T(8,128)}, u32[]{:S(2)}) copy-start(f32[36,2304]{1,0:T(8,128)} %param.10) | copy-start | bytes 995332
Sparse Core Ops, SparseCore 0:
  8.9 77.3 all-gather.3
  93.5 8.4 all-gather.5
  107.0 53.8 all-gather.7
  205.3 52.1 reduce-scatter.1
where the time goes:
time: 267 us
  waiting for transfers between devices  141 us (53%)
  local copies, waits for them, and re-layouts  65.1 us (24%)
  matrix products  30.3 us (11%)
  other arithmetic  17.3 us (6%)
  between operations  13.3 us (5%)
    all_gather x1, waiting for transfers between devices, body(): arrived = lax.all_gather(vertex_cross, 'mom', axis=0, tiled=True)  79 us
    reduce_scatter x1, waiting for transfers between devices, body(): lax.psum_scatter(partial_value, 'orb', scatter_dimension=1, tiled=True)  52.3 us
    gather x1, local copies, waits for them, and re-layouts, loop_right_all(): picked = jnp.take(green_right, folded_all(momenta, qpoints), axis=1)  31.2 us
    dot_general x1, matrix products, bubble_change(): jnp.einsum('qrk,qkc->qrc', carried, returned, preferred_element_type=jnp....  15 us
    dot_general x1, matrix products, bubble_change(): jnp.einsum('qrj,jk->qrk', row_block, left_loop, preferred_element_type=jn...  12.3 us
    mul x4, local copies, waits for them, and re-layouts, loop_left(): loop_rows = green_part[:, None, :] * form_table[None, :, :]  10.4 us
    all_gather x1, waiting for transfers between devices, body(): wide_block = lax.all_gather(merged, 'ff', axis=2, tiled=True)  8.6 us
    convert_element_type x1, other arithmetic, loop_right_all(): loop_rows.reshape(qpoints.shape[0], -1, momenta.shape[0])  6.94 us
  transfers between devices with their start and end apart: 4, of which 3 were waited for; matrix products, arithmetic and copies ran while one was open for 23% of the time, Pallas kernels for 0%

commit v1 on v0

v1 whole, which is shorter than its diff:
```python
import math

import jax
import jax.numpy as jnp
from jax import lax
from jax.sharding import PartitionSpec as P

LX = 48


def form_factors(shifts, momenta):
    row_x = momenta // LX
    row_y = momenta % LX
    turn_count = (shifts[:, 0:1] * row_x[None, :] + shifts[:, 1:2] * row_y[None, :]) % LX
    phases = turn_count.astype(jnp.float32) * (2.0 * math.pi / LX)
    anchor = (shifts[:, 0] == 0) & (shifts[:, 1] == 0)
    weight = jnp.where(anchor, 1.0, math.sqrt(2.0)).astype(jnp.float32)
    return weight[:, None] * jnp.cos(phases)


def loop_left(green_part, form_table):
    loop_rows = green_part[:, None, :] * form_table[None, :, :]
    return loop_rows.reshape(-1, form_table.shape[1]).astype(jnp.bfloat16)


def shifted(doubled, momenta, qpoint, total_count):
    pairs = doubled.shape[0]
    step_y = qpoint % LX
    straight = lax.dynamic_slice(doubled, (0, qpoint), (pairs, total_count))
    back = (qpoint - LX + total_count) % total_count
    wrapped = lax.dynamic_slice(doubled, (0, back), (pairs, total_count))
    return jnp.where(momenta[None, :] % LX + step_y < LX, straight, wrapped)


def loop_right_all(green_right, form_table, momenta, qpoints, total_count):
    doubled = jnp.concatenate([green_right, green_right], axis=1)
    picked = jnp.stack(
        [shifted(doubled, momenta, qpoints[i], total_count) for i in range(qpoints.shape[0])]
    )
    loop_rows = picked[:, :, None, :] * form_table[None, None, :, :] * (1.0 / total_count)
    return loop_rows.reshape(qpoints.shape[0], -1, momenta.shape[0]).astype(jnp.bfloat16)


def body(vertex_own, vertex_cross, project_coeff, green_left, green_right, window, shifts):
    points, row_count, col_count = vertex_own.shape
    form_count = shifts.shape[0]
    pair_rows = row_count // form_count
    total_k = green_left.shape[1]
    my_start = lax.axis_index("mom") * points
    my_window = lax.dynamic_slice_in_dim(window, my_start, points, 0)
    arrived = lax.all_gather(vertex_cross, "mom", axis=0, tiled=True)
    momenta = jnp.arange(total_k, dtype=jnp.int32)
    form_table = form_factors(shifts, momenta)
    left_loop = loop_left(green_left, form_table)
    right_loop = loop_right_all(green_right, form_table, momenta, my_window, total_k)
    bubble = jnp.einsum(
        "jk,qik->qji", left_loop, right_loop, preferred_element_type=jnp.float32
    ).astype(jnp.bfloat16)
    count = arrived.shape[0]
    tiles = arrived.reshape(count, pair_rows, form_count, col_count)
    projected = jnp.einsum(
        "qplm,pamc->qalc", project_coeff, tiles, preferred_element_type=jnp.float32
    )
    merged = (
        vertex_own.astype(jnp.float32) + projected.reshape(points, row_count, col_count)
    ).astype(jnp.bfloat16)
    tall_block = lax.all_gather(merged, "orb", axis=1, tiled=True)
    wide_block = lax.all_gather(merged, "ff", axis=2, tiled=True)
    half = jnp.einsum(
        "qrj,qji->qri", wide_block, bubble, preferred_element_type=jnp.float32
    ).astype(jnp.bfloat16)
    change = jnp.einsum("qri,qic->qrc", half, tall_block, preferred_element_type=jnp.float32)
    return (merged.astype(jnp.float32) + change).astype(jnp.bfloat16)


def solution(mesh):
    return jax.shard_map(
        body,
        mesh=mesh,
        in_specs=(
            P(("grp", "mom"), "orb", "ff"),
            P(("grp", "mom"), "orb", "ff"),
            P("mom", None, None, None),
            P("grp", None),
            P("grp", None),
            P(),
            P(),
        ),
        out_specs=P(("grp", "mom"), "orb", "ff"),
        check_vma=False,
    )
```

time: 267 us -> 151 us (0.57)
  waiting for transfers between devices: 141 us -> 62.9 us
  local copies, waits for them, and re-layouts: 65.1 us -> 11.7 us
  between operations: 13.3 us -> 38.8 us
  matrix products: 30.3 us -> 22.5 us
  other arithmetic: 17.3 us -> 13.8 us
    reduce_scatter x1 -> x0, waiting for transfers between devices: 52.3 us -> none  [body(): lax.psum_scatter(partial_value, 'orb', scatter_dimension=1, tiled=True)]
    all_gather x1, waiting for transfers between devices: 79 us -> 42.3 us  [body(): arrived = lax.all_gather(vertex_cross, 'mom', axis=0, tiled=True)]
    gather x1 -> x0, local copies, waits for them, and re-layouts: 31.2 us -> none  [loop_right_all(): picked = jnp.take(green_right, folded_all(momenta, qpoints), axis=1)]
    all_gather x1, waiting for transfers between devices: 0.01 us -> 19.9 us  [body(): tall_block = lax.all_gather(merged, 'orb', axis=1, tiled=True)]
    mul x4 -> x0, local copies, waits for them, and re-layouts: 10.4 us -> none  [loop_left(): loop_rows = green_part[:, None, :] * form_table[None, :, :]]
    all_gather x1, waiting for transfers between devices: 8.6 us -> 0.01 us  [body(): wide_block = lax.all_gather(merged, 'ff', axis=2, tiled=True)]
    dot_general x2, matrix products: 27.4 us -> 19.6 us  [the longest x1 14.1 us: body(): jnp.einsum('jk,qik->qji', left_loop, right_loop, preferred_element_type=j...]
    select_n x4 -> x1, other arithmetic: 6.91 us -> 0.01 us  [form_factors(): row_x = momenta // LX]
  transfers between devices with their start and end apart: 4 -> 3, of which waited for: 3 -> 2; matrix products, arithmetic and copies ran while one was open for 23% -> 22% of each run, Pallas kernels for 0% -> 0%
where the time goes in v1:
time: 151 us; the launch traced here: 150 us
  waiting for transfers between devices  62.9 us (42%)
  between operations  38.8 us (26%)
  matrix products  22.5 us (15%)
  other arithmetic  13.8 us (9%)
  local copies, waits for them, and re-layouts  11.7 us (8%)
    all_gather x1, waiting for transfers between devices, body(): arrived = lax.all_gather(vertex_cross, 'mom', axis=0, tiled=True)  42.3 us
    all_gather x1, waiting for transfers between devices, body(): tall_block = lax.all_gather(merged, 'orb', axis=1, tiled=True)  19.9 us
    dot_general x1, matrix products, body(): jnp.einsum('jk,qik->qji', left_loop, right_loop, preferred_element_type=j...  14.1 us
    convert_element_type x1, other arithmetic, loop_right_all(): loop_rows.reshape(qpoints.shape[0], -1, momenta.shape[0])  8.23 us
    dot_general x1, matrix products, body(): jnp.einsum('qri,qic->qrc', half, tall_block, preferred_element_type=jnp.f...  5.46 us
  transfers between devices with their start and end apart: 3, of which 2 were waited for; matrix products, arithmetic and copies ran while one was open for 22% of the time, Pallas kernels for 0%

profile of v1, /device:TPU:0, one launch (start us, length us, event | category | flops | bytes accessed | tf_op | source)
XLA Modules:
  0.0 149.9 jit_solution(9991153295831021083)
XLA Ops:
  6.5 0.7 all-gather.4.cloned.1.call-update
  7.3 0.0 all-gather.6.cloned.1.call-start
  7.3 0.7 dynamic_slice.51
  8.0 0.7 fusion.31
  29.1 1.0 constant_dynamic-update-slice_fusion.1
  30.1 1.0 constant_dynamic-update-slice_fusion
  36.4 0.3 bitcast_dynamic-update-slice_fusion.7
  36.6 0.3 bitcast_dynamic-update-slice_fusion.6
  36.9 0.3 bitcast_dynamic-update-slice_fusion.5
  37.2 0.3 bitcast_dynamic-update-slice_fusion.4
  37.4 0.3 bitcast_dynamic-update-slice_fusion.3
  37.7 0.3 bitcast_dynamic-update-slice_fusion.2
  38.0 0.3 bitcast_dynamic-update-slice_fusion.1
  38.3 0.3 bitcast_dynamic-update-slice_fusion
  38.5 0.0 copy-start.5
  38.6 2.3 %copy.31 = f32[8,36,2304]{2,0,1:T(8,128)} copy(f32[8,36,2304]{2,1,0:T(8,128)S(1)} %bitcast_dynamic-update-slice_fusion) | data formatting | bytes 5308416 | tf_op jit(solution)/shard_map/stack | solution.py:37
  40.9 0.7 fusion.21
  41.6 0.3 multiply_convert_fusion.1
  42.0 2.1 %reshape.274 = bf16[468,2304,1]{1,0,2:T(8,128)(2,1)} reshape(bf16[36,13,2304]{2,1,0:T(8,128)(2,1)S(1)} %multiply_convert_fusion.1) | data formatting | bytes 4313088 | tf_op jit(solution)/shard_map/convert_element_type | solution.py:23
  44.1 42.3 %all-gather.4.cloned.1.call-done = bf16[32,234,234]{2,0,1:T(8,128)(2,1)} async-done(((bf16[8,234,234]{2,0,1:T(8,128)(2,1)}), bf16[32,234,234]{2,0,1:T(8,128)(2,1)}) %all-gather.4.cloned.1.call-update) | async-done | bytes 3504400 | tf_op jit(solution)/shard_map/all_gather | solution.py:51
  86.3 2.9 %convolution_bitcast_fusion = f32[8,18,13,234]{3,2,0,1:T(8,128)S(1)} fusion(bf16[32,18,13,234,1]{3,0,2,4,1:T(8,128)(2,1)} %bitcast.52, bf16[8,32,13,13]{1,0,3,2:T(8,128)(2,1)S(1)} %copy-done.6), kind=kOutput, calls=%fused_computation.13 | convolution fusion | flops 364455936 | bytes 5343104 | tf_op jit(solution)/shard_map/qplm,pamc->qalc/dot_general | solution.py:61
  89.3 1.6 %copy.29 = f32[8,18,13,234]{3,0,2,1:T(8,128)S(1)} copy(f32[8,18,13,234]{3,2,0,1:T(8,128)S(1)} %convolution_bitcast_fusion) | data formatting | bytes 3504384 | tf_op jit(solution)/shard_map/qplm,pamc->qalc/transpose | solution.py:61
  90.8 0.3 fusion.6
  91.1 2.3 %copy.30 = bf16[8,234,234]{1,0,2:T(8,128)(2,1)} copy(bf16[8,234,234]{2,0,1:T(8,128)(2,1)S(1)} %fusion.6) | data formatting | bytes 1752192 | tf_op jit(solution)/shard_map/convert_element_type | solution.py:66
  93.4 0.0 all-gather.6.cloned.1.call-update
  93.4 0.2 all-gather.8.cloned.1.call-start
  93.6 8.2 %multiply_convert_fusion = bf16[8,36,13,2304]{3,0,2,1:T(8,128)(2,1)} fusion(f32[13,2304]{1,0:T(8,128)S(1)} %fusion.21, f32[8,36,2304]{2,0,1:T(8,128)} %copy.31), kind=kLoop, calls=%fused_computation | loop fusion | flops 25878528 | bytes 20026368 | tf_op jit(solution)/shard_map/convert_element_type | solution.py:41
  101.9 0.0 all-gather.8.cloned.1.call-update
  101.9 14.1 %convolution_convert_fusion = bf16[8,468,468]{2,0,1:T(8,128)(2,1)} fusion(bf16[8,468,2304]{2,0,1:T(8,128)(2,1)} %bitcast.51, bf16[468,2304,1]{1,0,2:T(8,128)(2,1)S(1)} %copy-done.2), kind=kOutput, calls=%fused_computation.4 | convolution fusion | flops 8075852800 | bytes 22913280 | tf_op jit(solution)/shard_map/jk,qik->qji/dot_general | solution.py:56
  116.0 19.9 %all-gather.8.cloned.1.call-done = bf16[8,468,234]{2,0,1:T(8,128)(2,1)} async-done(((bf16[8,234,234]{2,0,1:T(8,128)(2,1)}), bf16[8,468,234]{2,0,1:T(8,128)(2,1)}) %all-gather.8.cloned.1.call-update) | async-done | bytes 1752208 | tf_op jit(solution)/shard_map/all_gather | solution.py:67
  135.9 5.5 %fusion.2 = f32[8,234,234]{2,1,0:T(8,128)S(1)} fusion(bf16[8,468,234]{2,0,1:T(8,128)(2,1)} %all-gather.8.cloned.1.call-done, bf16[8,468,468]{2,0,1:T(8,128)(2,1)} %convolution_convert_fusion, bf16[8,234,468]{1,0,2:T(8,128)(2,1)} %all-gather.6.cloned.1.call-done), kind=kOutput, calls=%fused_computation.5 | convolution fusion | flops 1230914816 | bytes 8760960 | tf_op jit(solution)/shard_map/qri,qic->qrc/dot_general | solution.py:72
  141.4 2.0 %fusion.7 = bf16[8,234,234]{2,0,1:T(8,128)(2,1)} fusion(f32[8,234,234]{2,1,0:T(8,128)S(1)} %fusion.2, bf16[8,234,234]{2,0,1:T(8,128)(2,1)S(1)} %copy-done.1), kind=kLoop, calls=%fused_computation.12 | loop fusion | flops 1314144 | bytes 3504384 | tf_op jit(solution)/shard_map/convert_element_type | solution.py:73
  (26 shorter events, 0.2 us)
Async XLA Ops:
  6.5 79.8 %all-gather.4.cloned.1.call-start = ((), (), s32[]{:S(2)}) async-start(), calls=%async_computation | async-start | bytes 4792320 | tf_op jit(solution)/shard_map/all_gather | solution.py:51
  7.3 108.8 %all-gather.6.cloned.1.call-start = ((), (), s32[]{:S(2)}) async-start(), calls=%async_computation.1 | async-start | bytes 2875392 | tf_op jit(solution)/shard_map/all_gather | solution.py:68
  38.5 2.4 %copy-start.5 = (s32[13,2]{0,1:T(2,128)S(1)}, s32[13,2]{0,1:T(2,128)}, u32[]{:S(2)}) copy-start(s32[13,2]{0,1:T(2,128)} %param.13) | copy-start | bytes 316
  38.5 3.0 %copy-start.4 = (f32[36,2304]{1,0:T(8,128)S(1)}, f32[36,2304]{1,0:T(8,128)}, u32[]{:S(2)}) copy-start(f32[36,2304]{1,0:T(8,128)} %param.10) | copy-start | bytes 995332
  41.9 44.4 %copy-start.6 = (bf16[8,32,13,13]{1,0,3,2:T(8,128)(2,1)S(1)}, bf16[8,32,13,13]{1,0,3,2:T(8,128)(2,1)}, u32[]{:S(2)}) copy-start(bf16[8,32,13,13]{1,0,3,2:T(8,128)(2,1)} %param.9) | copy-start | bytes 259588
  89.2 1.6 %copy-start.3 = (bf16[8,234,234]{2,0,1:T(8,128)(2,1)S(1)}, bf16[8,234,234]{2,0,1:T(8,128)(2,1)}, u32[]{:S(2)}) copy-start(bf16[8,234,234]{2,0,1:T(8,128)(2,1)} %param.7) | copy-start | bytes 2628292
  91.1 10.8 %copy-start = (bf16[8,234,234]{2,0,1:T(8,128)(2,1)}, bf16[8,234,234]{2,0,1:T(8,128)(2,1)S(1)}, u32[]{:S(2)}) copy-start(bf16[8,234,234]{2,0,1:T(8,128)(2,1)S(1)} %fusion.6) | copy-start | bytes 2628292
  93.4 8.5 %copy-start.2 = (bf16[468,2304,1]{1,0,2:T(8,128)(2,1)S(1)}, bf16[468,2304,1]{1,0,2:T(8,128)(2,1)}, u32[]{:S(2)}) copy-start(bf16[468,2304,1]{1,0,2:T(8,128)(2,1)} %reshape.274) | copy-start | bytes 6469636
  93.4 42.5 %all-gather.8.cloned.1.call-start = ((), (), s32[]{:S(2)}) async-start(), calls=%async_computation.2 | async-start | bytes 2875392 | tf_op jit(solution)/shard_map/all_gather | solution.py:67
  116.0 25.4 %copy-start.1 = (bf16[8,234,234]{2,0,1:T(8,128)(2,1)S(1)}, bf16[8,234,234]{2,0,1:T(8,128)(2,1)}, u32[]{:S(2)}) copy-start(bf16[8,234,234]{2,0,1:T(8,128)(2,1)} %copy-done) | copy-start | bytes 2628292
Sparse Core Ops, SparseCore 0:
  8.9 77.3 all-gather.3
  93.5 8.4 all-gather.5
  103.6 32.2 all-gather.7

commit v2 on v1

--- a/solution.py
+++ b/solution.py
@@ -41,7 +41,7 @@
     return loop_rows.reshape(qpoints.shape[0], -1, momenta.shape[0]).astype(jnp.bfloat16)
 
 
-def body(vertex_own, vertex_cross, project_coeff, green_left, green_right, window, shifts):
+def body_gathered(vertex_own, vertex_cross, project_coeff, green_left, green_right, window, shifts):
     points, row_count, col_count = vertex_own.shape
     form_count = shifts.shape[0]
     pair_rows = row_count // form_count
@@ -73,9 +73,88 @@
     return (merged.astype(jnp.float32) + change).astype(jnp.bfloat16)
 
 
+CHUNKS = 2
+ENDS = 4
+
+
+def body_line(vertex_own, vertex_cross, project_coeff, green_left, green_right, window, shifts):
+    points, row_count, col_count = vertex_own.shape
+    form_count = shifts.shape[0]
+    pair_rows = row_count // form_count
+    total_k = green_left.shape[1]
+    place = lax.axis_index("mom")
+    chunk_pairs = pair_rows // CHUNKS
+    chunk_rows = chunk_pairs * form_count
+
+    padded = jnp.pad(project_coeff, ((0, 0), (2 * points, 2 * points), (0, 0), (0, 0)))
+    padded = padded.transpose(0, 2, 1, 3).reshape(points * form_count, -1)
+    wide = points * form_count
+    own_coeff = lax.dynamic_slice_in_dim(padded, place * wide, 5 * wide, 1)
+    straight = padded[:, 2 * wide : 6 * wide]
+    zero = jnp.zeros((wide, wide), straight.dtype)
+    to_two = jnp.concatenate([straight[:, : 2 * wide], zero, zero, zero], axis=1)
+    to_one = jnp.concatenate([zero, zero, zero, straight[:, 2 * wide :]], axis=1)
+    end_coeff = lax.ppermute(jnp.where(place == 3, to_two, to_one), "mom", [(3, 2), (0, 1)])
+    weights = jnp.concatenate([own_coeff, end_coeff], axis=0)
+    weights = weights.reshape(2 * points, form_count, 5 * points, form_count)
+
+    up = [(i, i + 1) for i in range(ENDS - 1)]
+    down = [(i + 1, i) for i in range(ENDS - 1)]
+    pieces = [
+        vertex_cross[:, i * chunk_rows : (i + 1) * chunk_rows] for i in range(CHUNKS)
+    ]
+    below = [lax.ppermute(piece, "mom", up) for piece in pieces]
+    above = [lax.ppermute(piece, "mom", down) for piece in pieces]
+    far_below = [lax.ppermute(piece, "mom", [(1, 2)]) for piece in below]
+    far_above = [lax.ppermute(piece, "mom", [(2, 1)]) for piece in above]
+
+    my_window = lax.dynamic_slice_in_dim(window, place * points, points, 0)
+    momenta = jnp.arange(total_k, dtype=jnp.int32)
+    form_table = form_factors(shifts, momenta)
+    half_pairs = green_left.shape[0] // 2
+    first_left = jnp.where(
+        lax.axis_index("ff") == 0, green_left, jnp.roll(green_left, half_pairs, axis=0)
+    )
+    first_right = jnp.where(
+        lax.axis_index("orb") == 0, green_right, jnp.roll(green_right, half_pairs, axis=0)
+    )
+    left_loop = loop_left(first_left, form_table)
+    right_loop = loop_right_all(first_right, form_table, momenta, my_window, total_k)
+    bubble = jnp.einsum(
+        "jk,qik->qji", left_loop, right_loop, preferred_element_type=jnp.float32
+    ).astype(jnp.bfloat16)
+
+    merged, halves, across = [], [], []
+    swap = [(0, 1), (1, 0)]
+    for i in range(CHUNKS):
+        stack = jnp.concatenate([far_below[i], below[i], pieces[i], above[i], far_above[i]], axis=0)
+        tiles = stack.reshape(5 * points, chunk_pairs, form_count, col_count)
+        sums = jnp.einsum("qlpm,pamc->qalc", weights, tiles, preferred_element_type=jnp.float32)
+        sums = sums.reshape(2 * points, chunk_rows, col_count)
+        outer = lax.ppermute(sums[points:].astype(jnp.bfloat16), "mom", [(2, 3), (1, 0)])
+        mine = vertex_own[:, i * chunk_rows : (i + 1) * chunk_rows].astype(jnp.float32)
+        mine = (mine + sums[:points] + outer.astype(jnp.float32)).astype(jnp.bfloat16)
+        merged.append(mine)
+        across.append(lax.ppermute(mine, "orb", swap))
+        beside = lax.ppermute(mine, "ff", swap)
+        rows = jnp.concatenate([mine, beside], axis=2)
+        halves.append(
+            jnp.einsum(
+                "qrj,qji->qri", rows, bubble, preferred_element_type=jnp.float32
+            ).astype(jnp.bfloat16)
+        )
+    half = jnp.concatenate(halves, axis=1)
+    tall = jnp.concatenate(merged + across, axis=1)
+    change = jnp.einsum("qri,qic->qrc", half, tall, preferred_element_type=jnp.float32)
+    total = jnp.concatenate(merged, axis=1).astype(jnp.float32) + change
+    return total.astype(jnp.bfloat16)
+
+
 def solution(mesh):
+    sizes = dict(mesh.shape)
+    in_line = sizes["mom"] == ENDS and sizes["orb"] == 2 and sizes["ff"] == 2
     return jax.shard_map(
-        body,
+        body_line if in_line else body_gathered,
         mesh=mesh,
         in_specs=(
             P(("grp", "mom"), "orb", "ff"),

time: 151 us -> 155 us (1.026)
  starting transfers between devices: 0.26 us -> 27.7 us
  waiting for transfers between devices: 62.9 us -> 43.6 us
  between operations: 38.8 us -> 26.5 us
  local copies, waits for them, and re-layouts: 11.7 us -> 23.5 us
  matrix products: 22.5 us -> 20.1 us
  other arithmetic: 13.8 us -> 12.2 us
    all_gather x3 -> x0, waiting for transfers between devices: 62.1 us -> none  [the longest x1 42.3 us: body(): arrived = lax.all_gather(vertex_cross, 'mom', axis=0, tiled=True)]
    ppermute x0 -> x15, waiting for transfers between devices: none -> 43.6 us  [the longest x2 24.5 us: body_line(): lax.ppermute(sums[points:].astype(jnp.bfloat16), 'mom', [(2, 3), (1, 0)])]
    ppermute x0 -> x15, starting transfers between devices: none -> 27.7 us  [the longest x2 11 us: body_line(): below = [lax.ppermute(piece, 'mom', up) for piece in pieces]]
    reshape x0 -> x3, local copies, waits for them, and re-layouts: none -> 6.29 us  [the longest x2 3.3 us: body_line(): weights = weights.reshape(2 * points, form_count, 5 * points, form_count)]
    unnamed x15 -> x25, local copies, waits for them, and re-layouts: 1.05 us -> 6.71 us
    slice x0 -> x11, local copies, waits for them, and re-layouts: none -> 2.53 us  [the longest x1 2.16 us: body_line(): vertex_cross[:, i * chunk_rows:(i + 1) * chunk_rows]]
    dot_general x3 -> x6, matrix products: 22.5 us -> 20.1 us  [the longest x1 12.9 us: body_line(): jnp.einsum('jk,qik->qji', left_loop, right_loop, preferred_element_type=j...]
    convert_element_type x1, other arithmetic: 8.23 us -> 6.36 us  [loop_right_all(): loop_rows.reshape(qpoints.shape[0], -1, momenta.shape[0])]
  transfers between devices with their start and end apart: 3 -> 15, of which waited for: 2 -> 4; matrix products, arithmetic and copies ran while one was open for 22% -> 33% of each run, Pallas kernels for 0% -> 0%
where the time goes in v2:
time: 155 us; the launch traced here: 154 us
  waiting for transfers between devices  43.6 us (28%)
  starting transfers between devices  27.7 us (18%)
  between operations  26.5 us (17%)
  local copies, waits for them, and re-layouts  23.5 us (15%)
  matrix products  20.1 us (13%)
  other arithmetic  12.2 us (8%)
    ppermute x2, waiting for transfers between devices, body_line(): lax.ppermute(sums[points:].astype(jnp.bfloat16), 'mom', [(2, 3), (1, 0)])  24.5 us
    ppermute x2, waiting for transfers between devices, body_line(): across.append(lax.ppermute(mine, 'orb', swap))  19.1 us
    dot_general x1, matrix products, body_line(): jnp.einsum('jk,qik->qji', left_loop, right_loop, preferred_element_type=j...  12.9 us
    ppermute x2, starting transfers between devices, body_line(): below = [lax.ppermute(piece, 'mom', up) for piece in pieces]  11 us
    unnamed x25, local copies, waits for them, and re-layouts  6.71 us
    convert_element_type x1, other arithmetic, loop_right_all(): loop_rows.reshape(qpoints.shape[0], -1, momenta.shape[0])  6.36 us
    ppermute x1, starting transfers between devices, body_line(): lax.ppermute(jnp.where(place == 3, to_two, to_one), 'mom', [(3, 2), (0, 1)])  4.56 us
    reshape x2, local copies, waits for them, and re-layouts, body_line(): weights = weights.reshape(2 * points, form_count, 5 * points, form_count)  3.3 us
  transfers between devices with their start and end apart: 15, of which 4 were waited for; matrix products, arithmetic and copies ran while one was open for 33% of the time, Pallas kernels for 0%

profile of v2, /device:TPU:0, one launch (start us, length us, event | category | flops | bytes accessed | tf_op | source)
XLA Modules:
  0.0 153.5 jit_solution(11402662611792849249)
XLA Ops:
  0.0 2.2 %fusion.88 = (bf16[8,117,234]{2,0,1:T(8,128)(2,1)}, bf16[8,117,234]{2,0,1:T(8,128)(2,1)}) fusion(bf16[8,234,234]{2,0,1:T(8,128)(2,1)} %param.8), kind=kLoop, calls=%fused_computation.160 | loop fusion | bytes 1752192 | tf_op jit(solution)/shard_map/slice | solution.py:104
  2.2 5.7 %collective-permute-start = (bf16[8,117,234]{2,0,1:T(8,128)(2,1)}, bf16[8,117,234]{2,0,1:T(8,128)(2,1)}, u32[]{:S(2)}, u32[]{:S(2)}) collective-permute-start(bf16[8,117,234]{2,0,1:T(8,128)(2,1)} %get-tuple-element.9), channel_id=1, source_target_pairs={{0,4},{4,8},{8,12},{1,5},{5,9},{9,13},{2,6},{6,10},{10,14},{3,7},{... | collective-permute-start | bytes 1314152 | tf_op jit(solution)/shard_map/ppermute | solution.py:106
  7.9 1.3 collective-permute-start.2
  9.1 5.3 %collective-permute-start.6 = (bf16[8,117,234]{2,0,1:T(8,128)(2,1)}, bf16[8,117,234]{2,0,1:T(8,128)(2,1)}, u32[]{:S(2)}, u32[]{:S(2)}) collective-permute-start(bf16[8,117,234]{2,0,1:T(8,128)(2,1)} %get-tuple-element.10), channel_id=1, source_target_pairs={{0,4},{4,8},{8,12},{1,5},{5,9},{9,13},{2,6},{6,10},{10,14},{3,7},{... | collective-permute-start | bytes 1314152 | tf_op jit(solution)/shard_map/ppermute | solution.py:106
  14.5 1.3 collective-permute-start.8
  15.8 1.1 pad_bitcast_fusion
  17.0 1.6 %copy.16 = bf16[8,13,64,13]{3,2,1,0:T(8,128)(2,1)S(1)} copy(bf16[8,13,64,13]{2,0,3,1:T(8,128)(2,1)S(1)} %pad_bitcast_fusion) | data formatting | bytes 346112 | tf_op jit(solution)/shard_map/transpose | solution.py:90
  18.6 3.0 %reshape.284 = bf16[104,832]{1,0:T(8,128)(2,1)S(1)} reshape(bf16[8,13,64,13]{3,2,1,0:T(8,128)(2,1)S(1)} %copy.16) | data formatting | bytes 346112 | tf_op jit(solution)/shard_map/reshape | solution.py:90
  21.8 4.6 %collective-permute-start.4 = (bf16[104,520]{1,0:T(8,128)(2,1)S(1)}, bf16[104,520]{1,0:T(8,128)(2,1)S(1)}, u32[]{:S(2)}, u32[]{:S(2)}) collective-permute-start(bf16[104,520]{1,0:T(8,128)(2,1)S(1)} %pad_select_fusion), channel_id=1, source_target_pairs={{12,8},{0,4},{13,9},{1,5},{14,10},{2,6},{15,11},{3,7},{28,24},{16,... | collective-permute-start | bytes 324488 | tf_op jit(solution)/shard_map/ppermute | solution.py:97
  58.7 6.4 %multiply_convert_fusion = bf16[8,36,13,2304]{3,0,2,1:T(8,128)(2,1)} fusion(f32[13,2304]{1,0:T(8,128)S(1)} %fusion.74, f32[8,36,2304]{2,0,1:T(8,128)S(1)} %copy.24), kind=kLoop, calls=%fused_computation | loop fusion | flops 25878528 | bytes 20026368 | tf_op jit(solution)/shard_map/convert_element_type | solution.py:41
  65.1 1.4 collective-permute-start.7
  66.9 2.1 %reshape.293 = bf16[468,2304,1]{1,0,2:T(8,128)(2,1)} reshape(bf16[36,13,2304]{2,1,0:T(8,128)(2,1)S(1)} %multiply_convert_fusion.1) | data formatting | bytes 4313088 | tf_op jit(solution)/shard_map/convert_element_type | solution.py:23
  69.0 1.5 collective-permute-start.1
  70.6 1.6 %reshape.285 = bf16[16,13,40,13]{3,2,1,0:T(8,128)(2,1)S(1)} reshape(bf16[208,520]{1,0:T(8,128)(2,1)S(1)} %pad_maximum_fusion) | data formatting | bytes 432640 | tf_op jit(solution)/shard_map/reshape | solution.py:99
  72.2 1.7 %copy.17 = bf16[16,13,40,13]{2,0,3,1:T(8,128)(2,1)S(1)} copy(bf16[16,13,40,13]{3,2,1,0:T(8,128)(2,1)S(1)} %reshape.285) | data formatting | bytes 432640 | tf_op jit(solution)/shard_map/reshape | solution.py:99
  75.5 1.1 constant_dynamic-update-slice_fusion.9
  76.5 1.1 constant_dynamic-update-slice_fusion.8
  78.7 1.1 constant_dynamic-update-slice_fusion.3
  79.8 1.1 constant_dynamic-update-slice_fusion.1
  82.1 1.3 collective-permute-start.5
  83.4 1.1 constant_dynamic-update-slice_fusion.6
  85.7 1.6 %collective-permute-start.10 = (bf16[8,117,234]{2,1,0:T(8,128)(2,1)S(1)}, bf16[8,117,234]{2,1,0:T(8,128)(2,1)S(1)}, u32[]{:S(2)}, u32[]{:S(2)}) collective-permute-start(bf16[8,117,234]{2,1,0:T(8,128)(2,1)S(1)} %copy.23), channel_id=1, source_target_pairs={{8,12},{4,0},{9,13},{5,1},{10,14},{6,2},{11,15},{7,3},{24,28},{20,... | collective-permute-start | bytes 1314152 | tf_op jit(solution)/shard_map/ppermute | solution.py:134
  87.5 15.3 %collective-permute-done.5 = bf16[8,117,234]{2,1,0:T(8,128)(2,1)S(1)} collective-permute-done((bf16[8,117,234]{2,1,0:T(8,128)(2,1)S(1)}, bf16[8,117,234]{2,1,0:T(8,128)(2,1)S(1)}, u32[]{:S(2)}, u32[]{:S(2)}) %collective-permute-start.5) | collective-permute-done | bytes 438080 | tf_op jit(solution)/shard_map/ppermute | solution.py:134
  103.3 9.2 %collective-permute-done.10 = bf16[8,117,234]{2,1,0:T(8,128)(2,1)S(1)} collective-permute-done((bf16[8,117,234]{2,1,0:T(8,128)(2,1)S(1)}, bf16[8,117,234]{2,1,0:T(8,128)(2,1)S(1)}, u32[]{:S(2)}, u32[]{:S(2)}) %collective-permute-start.10) | collective-permute-done | bytes 438080 | tf_op jit(solution)/shard_map/ppermute | solution.py:134
  113.0 12.9 %fusion.93 = bf16[8,468,468]{2,0,1:T(8,128)(2,1)S(1)} fusion(bf16[8,468,2304]{2,0,1:T(8,128)(2,1)} %bitcast.85, bf16[468,2304,1]{1,0,2:T(8,128)(2,1)S(1)} %copy-done.3), kind=kOutput, calls=%fused_computation.165 | convolution fusion | flops 8074100736 | bytes 22913280 | tf_op jit(solution)/shard_map/jk,qik->qji/dot_general | solution.py:123
  125.8 1.6 %collective-permute-start.13 = (bf16[8,117,234]{2,1,0:T(8,128)(2,1)S(1)}, bf16[8,117,234]{2,1,0:T(8,128)(2,1)S(1)}, u32[]{:S(2)}, u32[]{:S(2)}) collective-permute-start(bf16[8,117,234]{2,1,0:T(8,128)(2,1)S(1)} %fusion.24), channel_id=1, source_target_pairs={{0,2},{2,0},{1,3},{3,1},{4,6},{6,4},{5,7},{7,5},{8,10},{10,8},{9,1... | collective-permute-start | bytes 1314152 | tf_op jit(solution)/shard_map/ppermute | solution.py:138
  127.9 1.5 fusion.13
  129.5 1.5 fusion.14
  131.0 8.9 %collective-permute-done.13 = bf16[8,117,234]{2,1,0:T(8,128)(2,1)S(1)} collective-permute-done((bf16[8,117,234]{2,1,0:T(8,128)(2,1)S(1)}, bf16[8,117,234]{2,1,0:T(8,128)(2,1)S(1)}, u32[]{:S(2)}, u32[]{:S(2)}) %collective-permute-start.13) | collective-permute-done | bytes 438080 | tf_op jit(solution)/shard_map/ppermute | solution.py:138
  139.9 10.1 %collective-permute-done.14 = bf16[8,117,234]{2,1,0:T(8,128)(2,1)S(1)} collective-permute-done((bf16[8,117,234]{2,1,0:T(8,128)(2,1)S(1)}, bf16[8,117,234]{2,1,0:T(8,128)(2,1)S(1)}, u32[]{:S(2)}, u32[]{:S(2)}) %collective-permute-start.14) | collective-permute-done | bytes 438080 | tf_op jit(solution)/shard_map/ppermute | solution.py:138
  150.0 2.2 %add_convert_fusion = bf16[8,234,234]{2,1,0:T(8,128)(2,1)S(1)} fusion(bf16[8,117,234]{2,1,0:T(8,128)(2,1)S(1)} %fusion.22, bf16[8,117,234]{2,1,0:T(8,128)(2,1)S(1)} %fusion.24, bf16[8,117,234]{2,1,0:T(8,128)(2,1)S(1)} %collective-permute-done.14, bf16[8,117,234]{2,1,0:T(8,128)(2,1)S(1)} %collective-permute-done.13, bf16[8,117,468]{1,2,0:T(8,128)(2,1)S(1)} %fusion.14, ...), kind=kOutput, calls=%fused_computation.35 | convolution fusion | flops 423154368 | bytes 4380480 | tf_op jit(solution)/shard_map/qri,qic->qrc/dot_general | solution.py:148
  152.3 1.2 copy.26
  (79 shorter events, 13.8 us)
Async XLA Ops:
  2.2 66.8 %collective-permute-start = (bf16[8,117,234]{2,0,1:T(8,128)(2,1)}, bf16[8,117,234]{2,0,1:T(8,128)(2,1)}, u32[]{:S(2)}, u32[]{:S(2)}) collective-permute-start(bf16[8,117,234]{2,0,1:T(8,128)(2,1)} %get-tuple-element.9), channel_id=1, source_target_pairs={{0,4},{4,8},{8,12},{1,5},{5,9},{9,13},{2,6},{6,10},{10,14},{3,7},{... | collective-permute-start | bytes 1314152 | tf_op jit(solution)/shard_map/ppermute | solution.py:106
  7.9 66.1 %collective-permute-start.2 = (bf16[8,117,234]{2,0,1:T(8,128)(2,1)}, bf16[8,117,234]{2,0,1:T(8,128)(2,1)}, u32[]{:S(2)}, u32[]{:S(2)}) collective-permute-start(bf16[8,117,234]{2,0,1:T(8,128)(2,1)} %get-tuple-element.9), channel_id=1, source_target_pairs={{4,0},{8,4},{12,8},{5,1},{9,5},{13,9},{6,2},{10,6},{14,10},{7,3},{... | collective-permute-start | bytes 1314152 | tf_op jit(solution)/shard_map/ppermute | solution.py:107
  9.1 55.9 %collective-permute-start.6 = (bf16[8,117,234]{2,0,1:T(8,128)(2,1)}, bf16[8,117,234]{2,0,1:T(8,128)(2,1)}, u32[]{:S(2)}, u32[]{:S(2)}) collective-permute-start(bf16[8,117,234]{2,0,1:T(8,128)(2,1)} %get-tuple-element.10), channel_id=1, source_target_pairs={{0,4},{4,8},{8,12},{1,5},{5,9},{9,13},{2,6},{6,10},{10,14},{3,7},{... | collective-permute-start | bytes 1314152 | tf_op jit(solution)/shard_map/ppermute | solution.py:106
  14.5 60.3 %collective-permute-start.8 = (bf16[8,117,234]{2,0,1:T(8,128)(2,1)}, bf16[8,117,234]{2,0,1:T(8,128)(2,1)}, u32[]{:S(2)}, u32[]{:S(2)}) collective-permute-start(bf16[8,117,234]{2,0,1:T(8,128)(2,1)} %get-tuple-element.10), channel_id=1, source_target_pairs={{4,0},{8,4},{12,8},{5,1},{9,5},{13,9},{6,2},{10,6},{14,10},{7,3},{... | collective-permute-start | bytes 1314152 | tf_op jit(solution)/shard_map/ppermute | solution.py:107
  15.8 10.6 %copy-start.8 = (s32[32]{0:T(128)S(1)}, s32[32]{0:T(128)}, u32[]{:S(2)}) copy-start(s32[32]{0:T(128)} %param.12) | copy-start | bytes 388
  16.9 30.8 %copy-start.7 = (s32[13,2]{0,1:T(2,128)S(1)}, s32[13,2]{0,1:T(2,128)}, u32[]{:S(2)}) copy-start(s32[13,2]{0,1:T(2,128)} %param.13) | copy-start | bytes 316
  17.0 30.9 %copy-start.4 = (f32[36,2304]{1,0:T(8,128)S(1)}, f32[36,2304]{1,0:T(8,128)}, u32[]{:S(2)}) copy-start(f32[36,2304]{1,0:T(8,128)} %param.11) | copy-start | bytes 995332
  21.8 48.8 %collective-permute-start.4 = (bf16[104,520]{1,0:T(8,128)(2,1)S(1)}, bf16[104,520]{1,0:T(8,128)(2,1)S(1)}, u32[]{:S(2)}, u32[]{:S(2)}) collective-permute-start(bf16[104,520]{1,0:T(8,128)(2,1)S(1)} %pad_select_fusion), channel_id=1, source_target_pairs={{12,8},{0,4},{13,9},{1,5},{14,10},{2,6},{15,11},{3,7},{28,24},{16,... | collective-permute-start | bytes 324488 | tf_op jit(solution)/shard_map/ppermute | solution.py:97
  57.0 1.0 copy-start.5
  65.1 10.4 %collective-permute-start.7 = (bf16[8,117,234]{2,0,1:T(8,128)(2,1)}, bf16[8,117,234]{2,0,1:T(8,128)(2,1)}, u32[]{:S(2)}, u32[]{:S(2)}) collective-permute-start(bf16[8,117,234]{2,0,1:T(8,128)(2,1)} %collective-permute-done.6), channel_id=1, source_target_pairs={{4,8},{5,9},{6,10},{7,11},{20,24},{21,25},{22,26},{23,27}} | collective-permute-start | bytes 1314152 | tf_op jit(solution)/shard_map/ppermute | solution.py:108
  69.0 8.6 %collective-permute-start.1 = (bf16[8,117,234]{2,0,1:T(8,128)(2,1)}, bf16[8,117,234]{2,0,1:T(8,128)(2,1)}, u32[]{:S(2)}, u32[]{:S(2)}) collective-permute-start(bf16[8,117,234]{2,0,1:T(8,128)(2,1)} %collective-permute-done), channel_id=1, source_target_pairs={{4,8},{5,9},{6,10},{7,11},{20,24},{21,25},{22,26},{23,27}} | collective-permute-start | bytes 1314152 | tf_op jit(solution)/shard_map/ppermute | solution.py:108
  73.9 5.8 %copy-start.2 = (bf16[8,234,234]{2,0,1:T(8,128)(2,1)S(1)}, bf16[8,234,234]{2,0,1:T(8,128)(2,1)}, u32[]{:S(2)}) copy-start(bf16[8,234,234]{2,0,1:T(8,128)(2,1)} %param.8) | copy-start | bytes 2628292
  73.9 7.0 %collective-permute-start.3 = (bf16[8,117,234]{2,0,1:T(8,128)(2,1)}, bf16[8,117,234]{2,0,1:T(8,128)(2,1)S(1)}, u32[]{:S(2)}, u32[]{:S(2)}) collective-permute-start(bf16[8,117,234]{2,0,1:T(8,128)(2,1)} %collective-permute-done.2), channel_id=1, source_target_pairs={{8,4},{9,5},{10,6},{11,7},{24,20},{25,21},{26,22},{27,23}} | collective-permute-start | bytes 1314152 | tf_op jit(solution)/shard_map/ppermute | solution.py:109
  74.8 9.7 %collective-permute-start.9 = (bf16[8,117,234]{2,0,1:T(8,128)(2,1)}, bf16[8,117,234]{2,0,1:T(8,128)(2,1)S(1)}, u32[]{:S(2)}, u32[]{:S(2)}) collective-permute-start(bf16[8,117,234]{2,0,1:T(8,128)(2,1)} %collective-permute-done.8), channel_id=1, source_target_pairs={{8,4},{9,5},{10,6},{11,7},{24,20},{25,21},{26,22},{27,23}} | collective-permute-start | bytes 1314152 | tf_op jit(solution)/shard_map/ppermute | solution.py:109
  81.9 5.6 %copy-start.1 = (f32[16,9,13,234]{3,0,2,1:T(8,128)}, f32[16,9,13,234]{3,0,2,1:T(8,128)S(1)}, u32[]{:S(2)}) copy-start(f32[16,9,13,234]{3,0,2,1:T(8,128)S(1)} %convolution_bitcast_fusion.1) | copy-start | bytes 5256580
  82.1 20.7 %collective-permute-start.5 = (bf16[8,117,234]{2,1,0:T(8,128)(2,1)S(1)}, bf16[8,117,234]{2,1,0:T(8,128)(2,1)S(1)}, u32[]{:S(2)}, u32[]{:S(2)}) collective-permute-start(bf16[8,117,234]{2,1,0:T(8,128)(2,1)S(1)} %copy.19), channel_id=1, source_target_pairs={{8,12},{4,0},{9,13},{5,1},{10,14},{6,2},{11,15},{7,3},{24,28},{20,... | collective-permute-start | bytes 1314152 | tf_op jit(solution)/shard_map/ppermute | solution.py:134
  85.5 2.0 %copy-start = (f32[16,9,13,234]{3,0,2,1:T(8,128)}, f32[16,9,13,234]{3,0,2,1:T(8,128)S(1)}, u32[]{:S(2)}) copy-start(f32[16,9,13,234]{3,0,2,1:T(8,128)S(1)} %convolution_bitcast_fusion) | copy-start | bytes 5256580
  85.5 1.9 %copy-start.6 = (bf16[8,234,234]{2,0,1:T(8,128)(2,1)S(1)}, bf16[8,234,234]{2,0,1:T(8,128)(2,1)}, u32[]{:S(2)}) copy-start(bf16[8,234,234]{2,0,1:T(8,128)(2,1)} %param.7) | copy-start | bytes 2628292
  85.7 26.8 %collective-permute-start.10 = (bf16[8,117,234]{2,1,0:T(8,128)(2,1)S(1)}, bf16[8,117,234]{2,1,0:T(8,128)(2,1)S(1)}, u32[]{:S(2)}, u32[]{:S(2)}) collective-permute-start(bf16[8,117,234]{2,1,0:T(8,128)(2,1)S(1)} %copy.23), channel_id=1, source_target_pairs={{8,12},{4,0},{9,13},{5,1},{10,14},{6,2},{11,15},{7,3},{24,28},{20,... | collective-permute-start | bytes 1314152 | tf_op jit(solution)/shard_map/ppermute | solution.py:134
  87.5 15.3 %slice-start.1 = ((f32[16,9,13,234]{3,0,2,1:T(8,128)}), f32[8,9,13,234]{3,0,2,1:T(8,128)S(1)}, s32[]{:S(2)}) async-start(f32[16,9,13,234]{3,0,2,1:T(8,128)} %copy-done.1), calls=%async_computation.1 | async-start | bytes 1916928 | tf_op jit(solution)/shard_map/slice | solution.py:136
  87.5 25.0 %slice-start = ((f32[16,9,13,234]{3,0,2,1:T(8,128)}), f32[8,9,13,234]{3,0,2,1:T(8,128)S(1)}, s32[]{:S(2)}) async-start(f32[16,9,13,234]{3,0,2,1:T(8,128)} %copy-done), calls=%async_computation | async-start | bytes 1916928 | tf_op jit(solution)/shard_map/slice | solution.py:136
  102.8 10.2 %copy-start.3 = (bf16[468,2304,1]{1,0,2:T(8,128)(2,1)S(1)}, bf16[468,2304,1]{1,0,2:T(8,128)(2,1)}, u32[]{:S(2)}) copy-start(bf16[468,2304,1]{1,0,2:T(8,128)(2,1)} %reshape.293) | copy-start | bytes 6469636
  103.2 24.7 %collective-permute-start.11 = (bf16[8,117,234]{2,1,0:T(8,128)(2,1)S(1)}, bf16[8,117,234]{2,1,0:T(8,128)(2,1)S(1)}, u32[]{:S(2)}, u32[]{:S(2)}) collective-permute-start(bf16[8,117,234]{2,1,0:T(8,128)(2,1)S(1)} %fusion.24), channel_id=1, source_target_pairs={{0,1},{1,0},{2,3},{3,2},{4,5},{5,4},{6,7},{7,6},{8,9},{9,8},{10,11... | collective-permute-start | bytes 1314152 | tf_op jit(solution)/shard_map/ppermute | solution.py:139
  112.9 16.6 %collective-permute-start.12 = (bf16[8,117,234]{2,1,0:T(8,128)(2,1)S(1)}, bf16[8,117,234]{2,1,0:T(8,128)(2,1)S(1)}, u32[]{:S(2)}, u32[]{:S(2)}) collective-permute-start(bf16[8,117,234]{2,1,0:T(8,128)(2,1)S(1)} %fusion.22), channel_id=1, source_target_pairs={{0,1},{1,0},{2,3},{3,2},{4,5},{5,4},{6,7},{7,6},{8,9},{9,8},{10,11... | collective-permute-start | bytes 1314152 | tf_op jit(solution)/shard_map/ppermute | solution.py:139
  125.8 14.1 %collective-permute-start.13 = (bf16[8,117,234]{2,1,0:T(8,128)(2,1)S(1)}, bf16[8,117,234]{2,1,0:T(8,128)(2,1)S(1)}, u32[]{:S(2)}, u32[]{:S(2)}) collective-permute-start(bf16[8,117,234]{2,1,0:T(8,128)(2,1)S(1)} %fusion.24), channel_id=1, source_target_pairs={{0,2},{2,0},{1,3},{3,1},{4,6},{6,4},{5,7},{7,5},{8,10},{10,8},{9,1... | collective-permute-start | bytes 1314152 | tf_op jit(solution)/shard_map/ppermute | solution.py:138
  127.4 22.7 %collective-permute-start.14 = (bf16[8,117,234]{2,1,0:T(8,128)(2,1)S(1)}, bf16[8,117,234]{2,1,0:T(8,128)(2,1)S(1)}, u32[]{:S(2)}, u32[]{:S(2)}) collective-permute-start(bf16[8,117,234]{2,1,0:T(8,128)(2,1)S(1)} %fusion.22), channel_id=1, source_target_pairs={{0,2},{2,0},{1,3},{3,1},{4,6},{6,4},{5,7},{7,5},{8,10},{10,8},{9,1... | collective-permute-start | bytes 1314152 | tf_op jit(solution)/shard_map/ppermute | solution.py:138

commit v3 on v2

--- a/solution.py
+++ b/solution.py
@@ -3,6 +3,8 @@
 import jax
 import jax.numpy as jnp
 from jax import lax
+from jax.experimental import pallas as pl
+from jax.experimental.pallas import tpu as pltpu
 from jax.sharding import PartitionSpec as P
 
 LX = 48
@@ -73,6 +75,38 @@
     return (merged.astype(jnp.float32) + change).astype(jnp.bfloat16)
 
 
+def pick_kernel(window_ref, column_ref, green_ref, picked_ref):
+    qpoint = window_ref[pl.program_id(0)]
+    values = green_ref[...]
+    total_count = values.shape[1]
+    straight = pltpu.roll(values, lax.rem(total_count - qpoint, total_count), 1)
+    wrapped = pltpu.roll(values, lax.rem(total_count - qpoint + LX, total_count), 1)
+    stays = column_ref[...] + lax.rem(qpoint, LX) < LX
+    picked_ref[0] = jnp.where(stays, straight, wrapped)
+
+
+def pick_all(green, column, qpoints):
+    pairs, total_k = green.shape
+    points = qpoints.shape[0]
+    return pl.pallas_call(
+        pick_kernel,
+        grid=(points,),
+        out_shape=jax.ShapeDtypeStruct((points, pairs, total_k), jnp.float32),
+        in_specs=[
+            pl.BlockSpec(memory_space=pltpu.SMEM),
+            pl.BlockSpec((1, total_k), lambda i: (0, 0)),
+            pl.BlockSpec((pairs, total_k), lambda i: (0, 0)),
+        ],
+        out_specs=pl.BlockSpec((1, pairs, total_k), lambda i: (i, 0, 0)),
+        compiler_params=pltpu.CompilerParams(vmem_limit_bytes=8 * 1024 * 1024),
+        cost_estimate=pl.CostEstimate(
+            flops=4 * points * pairs * total_k,
+            bytes_accessed=8 * points * pairs * total_k,
+            transcendentals=0,
+        ),
+    )(qpoints, column, green)
+
+
 CHUNKS = 2
 ENDS = 4
 
@@ -105,9 +139,6 @@
     ]
     below = [lax.ppermute(piece, "mom", up) for piece in pieces]
     above = [lax.ppermute(piece, "mom", down) for piece in pieces]
-    far_below = [lax.ppermute(piece, "mom", [(1, 2)]) for piece in below]
-    far_above = [lax.ppermute(piece, "mom", [(2, 1)]) for piece in above]
-
     my_window = lax.dynamic_slice_in_dim(window, place * points, points, 0)
     momenta = jnp.arange(total_k, dtype=jnp.int32)
     form_table = form_factors(shifts, momenta)
@@ -119,10 +150,22 @@
         lax.axis_index("orb") == 0, green_right, jnp.roll(green_right, half_pairs, axis=0)
     )
     left_loop = loop_left(first_left, form_table)
-    right_loop = loop_right_all(first_right, form_table, momenta, my_window, total_k)
+    picked = pick_all(first_right, (momenta % LX)[None, :], my_window)
+    picked, below[0], above[0] = lax.optimization_barrier((picked, below[0], above[0]))
+    far_below = [lax.ppermute(below[0], "mom", [(1, 2)])]
+    far_above = [lax.ppermute(above[0], "mom", [(2, 1)])]
+    right_loop = picked[:, :, None, :] * form_table[None, None, :, :] * (1.0 / total_k)
+    right_loop = right_loop.reshape(points, -1, total_k).astype(jnp.bfloat16)
+    right_loop, *rest = lax.optimization_barrier((right_loop, *below[1:], *above[1:]))
+    below[1:], above[1:] = rest[: CHUNKS - 1], rest[CHUNKS - 1 :]
+    far_below += [lax.ppermute(piece, "mom", [(1, 2)]) for piece in below[1:]]
+    far_above += [lax.ppermute(piece, "mom", [(2, 1)]) for piece in above[1:]]
     bubble = jnp.einsum(
         "jk,qik->qji", left_loop, right_loop, preferred_element_type=jnp.float32
     ).astype(jnp.bfloat16)
+    bubble, far_below[0], far_above[0] = lax.optimization_barrier(
+        (bubble, far_below[0], far_above[0])
+    )
 
     merged, halves, across = [], [], []
     swap = [(0, 1), (1, 0)]

time: 155 us -> 152 us (0.981)
  between operations: 26.5 us -> 0.5 us
  local copies, waits for them, and re-layouts: 23.5 us -> 42.8 us
  Pallas kernels: 0 us -> 3.92 us
  matrix products: 20.1 us -> 23.5 us
  waiting for transfers between devices: 43.6 us -> 41 us
    mul x0 -> x4, local copies, waits for them, and re-layouts: none -> 17.9 us  [the longest x2 9.05 us: body_line(): picked[:, :, None, :] * form_table[None, None, :, :] * (1.0 / total_k)]
    convert_element_type x2 -> x1, other arithmetic: 6.71 us -> 11.1 us  [body_line(): right_loop = right_loop.reshape(points, -1, total_k).astype(jnp.bfloat16)]
    pallas_call x0 -> x1, Pallas kernels: none -> 3.92 us  [pick_all(): pl.pallas_call(pick_kernel, grid=(points,), out_shape=jax.ShapeDtypeStruc...]
    dot_general x1, matrix products: 12.9 us -> 16.8 us  [body_line(): jnp.einsum('jk,qik->qji', left_loop, right_loop, preferred_element_type=j...]
    dot_general x0 -> x1, local copies, waits for them, and re-layouts: none -> 3.4 us  [body_line(): jnp.einsum('jk,qik->qji', left_loop, right_loop, preferred_element_type=j...]
    unnamed x7 -> x0, other arithmetic: 3.26 us -> none
    ppermute x2, waiting for transfers between devices: 24.5 us -> 21.4 us  [body_line(): lax.ppermute(sums[points:].astype(jnp.bfloat16), 'mom', [(2, 3), (1, 0)])]
    reshape x2, local copies, waits for them, and re-layouts: 3.3 us -> 6.04 us  [body_line(): weights = weights.reshape(2 * points, form_count, 5 * points, form_count)]
  transfers between devices with their start and end apart: 15 -> 15, of which waited for: 4 -> 4; matrix products, arithmetic and copies ran while one was open for 33% -> 49% of each run, Pallas kernels for 0% -> 3%
where the time goes in v3:
time: 152 us; the launch traced here: 151 us
  local copies, waits for them, and re-layouts  42.8 us (28%)
  waiting for transfers between devices  41 us (27%)
  starting transfers between devices  26.4 us (17%)
  matrix products  23.5 us (15%)
  other arithmetic  12.9 us (8%)
  Pallas kernels  3.92 us (3%)
    ppermute x2, waiting for transfers between devices, body_line(): lax.ppermute(sums[points:].astype(jnp.bfloat16), 'mom', [(2, 3), (1, 0)])  21.4 us
    ppermute x2, waiting for transfers between devices, body_line(): across.append(lax.ppermute(mine, 'orb', swap))  19.6 us
    dot_general x1, matrix products, body_line(): jnp.einsum('jk,qik->qji', left_loop, right_loop, preferred_element_type=j...  16.8 us
    convert_element_type x1, other arithmetic, body_line(): right_loop = right_loop.reshape(points, -1, total_k).astype(jnp.bfloat16)  11.1 us
    ppermute x2, starting transfers between devices, body_line(): below = [lax.ppermute(piece, 'mom', up) for piece in pieces]  11.1 us
    mul x2, local copies, waits for them, and re-layouts, body_line(): picked[:, :, None, :] * form_table[None, None, :, :] * (1.0 / total_k)  9.05 us
    mul x2, local copies, waits for them, and re-layouts, loop_left(): loop_rows = green_part[:, None, :] * form_table[None, :, :]  8.85 us
    reshape x2, local copies, waits for them, and re-layouts, body_line(): weights = weights.reshape(2 * points, form_count, 5 * points, form_count)  6.04 us
  transfers between devices with their start and end apart: 15, of which 4 were waited for; matrix products, arithmetic and copies ran while one was open for 49% of the time, Pallas kernels for 3%

profile of v3, /device:TPU:0, one launch (start us, length us, event | category | flops | bytes accessed | tf_op | source)
XLA Modules:
  0.0 151.0 jit_solution(15418123596203992269)
XLA Ops:
  0.0 2.2 %fusion.50 = (bf16[8,117,234]{2,0,1:T(8,128)(2,1)}, bf16[8,117,234]{2,0,1:T(8,128)(2,1)}) fusion(bf16[8,234,234]{2,0,1:T(8,128)(2,1)} %param.8), kind=kLoop, calls=%fused_computation.84 | loop fusion | bytes 1752192 | tf_op jit(solution)/shard_map/slice | solution.py:138
  2.2 5.7 %collective-permute-start = (bf16[8,117,234]{2,0,1:T(8,128)(2,1)}, bf16[8,117,234]{2,0,1:T(8,128)(2,1)}, u32[]{:S(2)}, u32[]{:S(2)}) collective-permute-start(bf16[8,117,234]{2,0,1:T(8,128)(2,1)} %get-tuple-element.28), channel_id=1, source_target_pairs={{0,4},{4,8},{8,12},{1,5},{5,9},{9,13},{2,6},{6,10},{10,14},{3,7},{... | collective-permute-start | bytes 1314152 | tf_op jit(solution)/shard_map/ppermute | solution.py:140
  7.9 1.3 collective-permute-start.1
  9.2 5.3 %collective-permute-start.2 = (bf16[8,117,234]{2,0,1:T(8,128)(2,1)}, bf16[8,117,234]{2,0,1:T(8,128)(2,1)}, u32[]{:S(2)}, u32[]{:S(2)}) collective-permute-start(bf16[8,117,234]{2,0,1:T(8,128)(2,1)} %get-tuple-element.27), channel_id=1, source_target_pairs={{0,4},{4,8},{8,12},{1,5},{5,9},{9,13},{2,6},{6,10},{10,14},{3,7},{... | collective-permute-start | bytes 1314152 | tf_op jit(solution)/shard_map/ppermute | solution.py:140
  14.5 1.3 collective-permute-start.3
  15.8 1.2 pad_bitcast_fusion
  17.0 1.6 %copy.18 = bf16[8,13,64,13]{3,2,1,0:T(8,128)(2,1)S(1)} copy(bf16[8,13,64,13]{2,0,3,1:T(8,128)(2,1)S(1)} %pad_bitcast_fusion) | data formatting | bytes 346112 | tf_op jit(solution)/shard_map/transpose | solution.py:124
  18.6 3.0 %reshape.223 = bf16[104,832]{1,0:T(8,128)(2,1)S(1)} reshape(bf16[8,13,64,13]{3,2,1,0:T(8,128)(2,1)S(1)} %copy.18) | data formatting | bytes 346112 | tf_op jit(solution)/shard_map/reshape | solution.py:124
  21.8 4.6 %collective-permute-start.6 = (bf16[104,520]{1,0:T(8,128)(2,1)S(1)}, bf16[104,520]{1,0:T(8,128)(2,1)S(1)}, u32[]{:S(2)}, u32[]{:S(2)}) collective-permute-start(bf16[104,520]{1,0:T(8,128)(2,1)S(1)} %pad_select_fusion), channel_id=1, source_target_pairs={{12,8},{0,4},{13,9},{1,5},{14,10},{2,6},{15,11},{3,7},{28,24},{16,... | collective-permute-start | bytes 324488 | tf_op jit(solution)/shard_map/ppermute | solution.py:131
  27.2 3.0 %mul.141 = f32[36,13,2304]{2,1,0:T(8,128)} broadcast(f32[13,2304]{1,0:T(8,128)S(1)} %fusion.36), dimensions={1,2} | broadcast | bytes 4432896 | tf_op jit(solution)/shard_map/mul | solution.py:157
  30.1 6.1 %mul.142 = f32[468,2304]{1,0:T(8,128)} reshape(f32[36,13,2304]{2,1,0:T(8,128)} %mul.141) | data formatting | bytes 8626176 | tf_op jit(solution)/shard_map/mul | solution.py:157
  36.3 2.8 %mul.147 = f32[36,13,2304]{2,1,0:T(8,128)} broadcast(f32[36,2304]{1,0:T(8,128)S(1)} %maximum_select_fusion.1), dimensions={0,2} | broadcast | bytes 4644864 | tf_op jit(solution)/shard_map/mul | solution.py:24
  39.1 6.1 %mul.148 = f32[468,2304]{1,0:T(8,128)} reshape(f32[36,13,2304]{2,1,0:T(8,128)} %mul.147) | data formatting | bytes 8626176 | tf_op jit(solution)/shard_map/mul | solution.py:24
  45.3 3.9 %shard_map.73 = f32[8,36,2304]{2,1,0:T(8,128)S(1)} custom-call(s32[8]{0:T(128)S(1)} %dynamic_slice.6.window_ref, s32[1,2304]{1,0:T(1,128)S(1)} %and_select_fusion.column_ref, f32[36,2304]{1,0:T(8,128)S(1)} %maximum_select_fusion.green_ref), custom_call_target="tpu_custom_call" | custom-call | flops 2654208 | bytes 5308416 | tf_op jit(solution)/shard_map/pallas_call | solution.py:91
  49.4 2.6 %reshape.224 = bf16[16,13,40,13]{3,2,1,0:T(8,128)(2,1)} reshape(bf16[208,520]{1,0:T(8,128)(2,1)S(1)} %pad_maximum_fusion) | data formatting | bytes 432640 | tf_op jit(solution)/shard_map/reshape | solution.py:133
  52.0 3.5 %copy.19 = bf16[16,13,40,13]{2,0,3,1:T(8,128)(2,1)} copy(bf16[16,13,40,13]{3,2,1,0:T(8,128)(2,1)} %reshape.224) | data formatting | bytes 432640 | tf_op jit(solution)/shard_map/reshape | solution.py:133
  56.3 11.1 %fusion.1 = bf16[8,468,2304]{2,0,1:T(8,128)(2,1)} fusion(f32[468,2304]{1,0:T(8,128)} %mul.142, f32[8,36,2304]{2,0,1:T(8,128)S(1)} %copy.16), kind=kLoop, calls=%fused_computation.2 | loop fusion | flops 25878528 | bytes 24219648 | tf_op jit(solution)/shard_map/convert_element_type | solution.py:158
  69.8 16.8 %fusion.4 = bf16[8,468,468]{2,0,1:T(8,128)(2,1)} fusion(bf16[8,468,2304]{2,0,1:T(8,128)(2,1)} %fusion.1, f32[468,2304]{1,0:T(8,128)} %mul.148, f32[468,2304]{1,0:T(8,128)} %mul.142), kind=kOutput, calls=%fused_computation.7 | convolution fusion | flops 8076257280 | bytes 29382912 | tf_op jit(solution)/shard_map/jk,qik->qji/dot_general | solution.py:163
  86.5 3.4 %copy.50 = bf16[8,468,468]{2,1,0:T(8,128)(2,1)S(1)} copy(bf16[8,468,468]{2,0,1:T(8,128)(2,1)} %fusion.4) | data formatting | bytes 7008768 | tf_op jit(solution)/shard_map/jk,qik->qji/dot_general | solution.py:163
  91.9 1.1 constant_dynamic-update-slice_fusion.8
  93.2 1.1 constant_dynamic-update-slice_fusion.1
  95.4 1.3 collective-permute-start.7
  99.0 1.6 %collective-permute-start.10 = (bf16[8,117,234]{2,1,0:T(8,128)(2,1)S(1)}, bf16[8,117,234]{2,1,0:T(8,128)(2,1)S(1)}, u32[]{:S(2)}, u32[]{:S(2)}) collective-permute-start(bf16[8,117,234]{2,1,0:T(8,128)(2,1)S(1)} %copy.25), channel_id=1, source_target_pairs={{8,12},{4,0},{9,13},{5,1},{10,14},{6,2},{11,15},{7,3},{24,28},{20,... | collective-permute-start | bytes 1314152 | tf_op jit(solution)/shard_map/ppermute | solution.py:177
  100.9 14.1 %collective-permute-done.7 = bf16[8,117,234]{2,1,0:T(8,128)(2,1)S(1)} collective-permute-done((bf16[8,117,234]{2,1,0:T(8,128)(2,1)S(1)}, bf16[8,117,234]{2,1,0:T(8,128)(2,1)S(1)}, u32[]{:S(2)}, u32[]{:S(2)}) %collective-permute-start.7) | collective-permute-done | bytes 438080 | tf_op jit(solution)/shard_map/ppermute | solution.py:177
  115.5 7.3 %collective-permute-done.10 = bf16[8,117,234]{2,1,0:T(8,128)(2,1)S(1)} collective-permute-done((bf16[8,117,234]{2,1,0:T(8,128)(2,1)S(1)}, bf16[8,117,234]{2,1,0:T(8,128)(2,1)S(1)}, u32[]{:S(2)}, u32[]{:S(2)}) %collective-permute-start.10) | collective-permute-done | bytes 438080 | tf_op jit(solution)/shard_map/ppermute | solution.py:177
  123.3 1.6 %collective-permute-start.13 = (bf16[8,117,234]{2,1,0:T(8,128)(2,1)S(1)}, bf16[8,117,234]{2,1,0:T(8,128)(2,1)S(1)}, u32[]{:S(2)}, u32[]{:S(2)}) collective-permute-start(bf16[8,117,234]{2,1,0:T(8,128)(2,1)S(1)} %fusion.26), channel_id=1, source_target_pairs={{0,2},{2,0},{1,3},{3,1},{4,6},{6,4},{5,7},{7,5},{8,10},{10,8},{9,1... | collective-permute-start | bytes 1314152 | tf_op jit(solution)/shard_map/ppermute | solution.py:181
  125.4 1.2 convolution_convert_fusion.1
  126.7 1.3 convolution_convert_fusion
  128.0 9.5 %collective-permute-done.13 = bf16[8,117,234]{2,1,0:T(8,128)(2,1)S(1)} collective-permute-done((bf16[8,117,234]{2,1,0:T(8,128)(2,1)S(1)}, bf16[8,117,234]{2,1,0:T(8,128)(2,1)S(1)}, u32[]{:S(2)}, u32[]{:S(2)}) %collective-permute-start.13) | collective-permute-done | bytes 438080 | tf_op jit(solution)/shard_map/ppermute | solution.py:181
  137.4 10.1 %collective-permute-done.14 = bf16[8,117,234]{2,1,0:T(8,128)(2,1)S(1)} collective-permute-done((bf16[8,117,234]{2,1,0:T(8,128)(2,1)S(1)}, bf16[8,117,234]{2,1,0:T(8,128)(2,1)S(1)}, u32[]{:S(2)}, u32[]{:S(2)}) %collective-permute-start.14) | collective-permute-done | bytes 438080 | tf_op jit(solution)/shard_map/ppermute | solution.py:181
  147.5 2.2 %add_convert_fusion = bf16[8,234,234]{2,1,0:T(8,128)(2,1)S(1)} fusion(bf16[8,117,234]{2,1,0:T(8,128)(2,1)S(1)} %fusion.24, bf16[8,117,234]{2,1,0:T(8,128)(2,1)S(1)} %fusion.26, bf16[8,117,234]{2,1,0:T(8,128)(2,1)S(1)} %collective-permute-done.14, bf16[8,117,234]{2,1,0:T(8,128)(2,1)S(1)} %collective-permute-done.13, ...), kind=kOutput, calls=%fused_computation.8 | convolution fusion | flops 423154368 | bytes 4380480 | tf_op jit(solution)/shard_map/qri,qic->qrc/dot_general | solution.py:191
  149.8 1.2 copy.26
  (65 shorter events, 11.6 us)
Async XLA Ops:
  2.2 53.3 %collective-permute-start = (bf16[8,117,234]{2,0,1:T(8,128)(2,1)}, bf16[8,117,234]{2,0,1:T(8,128)(2,1)}, u32[]{:S(2)}, u32[]{:S(2)}) collective-permute-start(bf16[8,117,234]{2,0,1:T(8,128)(2,1)} %get-tuple-element.28), channel_id=1, source_target_pairs={{0,4},{4,8},{8,12},{1,5},{5,9},{9,13},{2,6},{6,10},{10,14},{3,7},{... | collective-permute-start | bytes 1314152 | tf_op jit(solution)/shard_map/ppermute | solution.py:140
  7.9 47.6 %collective-permute-start.1 = (bf16[8,117,234]{2,0,1:T(8,128)(2,1)}, bf16[8,117,234]{2,0,1:T(8,128)(2,1)}, u32[]{:S(2)}, u32[]{:S(2)}) collective-permute-start(bf16[8,117,234]{2,0,1:T(8,128)(2,1)} %get-tuple-element.28), channel_id=1, source_target_pairs={{4,0},{8,4},{12,8},{5,1},{9,5},{13,9},{6,2},{10,6},{14,10},{7,3},{... | collective-permute-start | bytes 1314152 | tf_op jit(solution)/shard_map/ppermute | solution.py:141
  9.2 58.3 %collective-permute-start.2 = (bf16[8,117,234]{2,0,1:T(8,128)(2,1)}, bf16[8,117,234]{2,0,1:T(8,128)(2,1)}, u32[]{:S(2)}, u32[]{:S(2)}) collective-permute-start(bf16[8,117,234]{2,0,1:T(8,128)(2,1)} %get-tuple-element.27), channel_id=1, source_target_pairs={{0,4},{4,8},{8,12},{1,5},{5,9},{9,13},{2,6},{6,10},{10,14},{3,7},{... | collective-permute-start | bytes 1314152 | tf_op jit(solution)/shard_map/ppermute | solution.py:140
  14.5 53.0 %collective-permute-start.3 = (bf16[8,117,234]{2,0,1:T(8,128)(2,1)}, bf16[8,117,234]{2,0,1:T(8,128)(2,1)}, u32[]{:S(2)}, u32[]{:S(2)}) collective-permute-start(bf16[8,117,234]{2,0,1:T(8,128)(2,1)} %get-tuple-element.27), channel_id=1, source_target_pairs={{4,0},{8,4},{12,8},{5,1},{9,5},{13,9},{6,2},{10,6},{14,10},{7,3},{... | collective-permute-start | bytes 1314152 | tf_op jit(solution)/shard_map/ppermute | solution.py:141
  15.8 10.6 %copy-start.5 = (s32[13,2]{0,1:T(2,128)S(1)}, s32[13,2]{0,1:T(2,128)}, u32[]{:S(2)}) copy-start(s32[13,2]{0,1:T(2,128)} %param.13) | copy-start | bytes 316
  15.8 10.6 %copy-start.2 = (f32[36,2304]{1,0:T(8,128)S(1)}, f32[36,2304]{1,0:T(8,128)}, u32[]{:S(2)}) copy-start(f32[36,2304]{1,0:T(8,128)} %param.11) | copy-start | bytes 995332
  21.8 27.6 %collective-permute-start.6 = (bf16[104,520]{1,0:T(8,128)(2,1)S(1)}, bf16[104,520]{1,0:T(8,128)(2,1)S(1)}, u32[]{:S(2)}, u32[]{:S(2)}) collective-permute-start(bf16[104,520]{1,0:T(8,128)(2,1)S(1)} %pad_select_fusion), channel_id=1, source_target_pairs={{12,8},{0,4},{13,9},{1,5},{14,10},{2,6},{15,11},{3,7},{28,24},{16,... | collective-permute-start | bytes 324488 | tf_op jit(solution)/shard_map/ppermute | solution.py:131
  30.1 6.1 %copy-start.1 = (f32[36,2304]{1,0:T(8,128)S(1)}, f32[36,2304]{1,0:T(8,128)}, u32[]{:S(2)}) copy-start(f32[36,2304]{1,0:T(8,128)} %param.10) | copy-start | bytes 995332
  39.1 6.1 %copy-start.6 = (s32[32]{0:T(128)S(1)}, s32[32]{0:T(128)}, u32[]{:S(2)}) copy-start(s32[32]{0:T(128)} %param.12) | copy-start | bytes 388
  67.5 23.3 %collective-permute-start.4 = (bf16[8,117,234]{2,0,1:T(8,128)(2,1)}, bf16[8,117,234]{2,0,1:T(8,128)(2,1)S(1)}, u32[]{:S(2)}, u32[]{:S(2)}) collective-permute-start(bf16[8,117,234]{2,0,1:T(8,128)(2,1)} %collective-permute-done), channel_id=1, source_target_pairs={{4,8},{5,9},{6,10},{7,11},{20,24},{21,25},{22,26},{23,27}} | collective-permute-start | bytes 1314152 | tf_op jit(solution)/shard_map/ppermute | solution.py:155
  68.2 22.6 %collective-permute-start.5 = (bf16[8,117,234]{2,0,1:T(8,128)(2,1)}, bf16[8,117,234]{2,0,1:T(8,128)(2,1)S(1)}, u32[]{:S(2)}, u32[]{:S(2)}) collective-permute-start(bf16[8,117,234]{2,0,1:T(8,128)(2,1)} %collective-permute-done.1), channel_id=1, source_target_pairs={{8,4},{9,5},{10,6},{11,7},{24,20},{25,21},{26,22},{27,23}} | collective-permute-start | bytes 1314152 | tf_op jit(solution)/shard_map/ppermute | solution.py:156
  68.9 23.0 %collective-permute-start.8 = (bf16[8,117,234]{2,0,1:T(8,128)(2,1)}, bf16[8,117,234]{2,0,1:T(8,128)(2,1)S(1)}, u32[]{:S(2)}, u32[]{:S(2)}) collective-permute-start(bf16[8,117,234]{2,0,1:T(8,128)(2,1)} %collective-permute-done.2), channel_id=1, source_target_pairs={{4,8},{5,9},{6,10},{7,11},{20,24},{21,25},{22,26},{23,27}} | collective-permute-start | bytes 1314152 | tf_op jit(solution)/shard_map/ppermute | solution.py:161
  89.9 3.2 %copy-start = (bf16[8,234,234]{2,0,1:T(8,128)(2,1)S(1)}, bf16[8,234,234]{2,0,1:T(8,128)(2,1)}, u32[]{:S(2)}) copy-start(bf16[8,234,234]{2,0,1:T(8,128)(2,1)} %param.8) | copy-start | bytes 2628292
  89.9 7.9 %collective-permute-start.9 = (bf16[8,117,234]{2,0,1:T(8,128)(2,1)}, bf16[8,117,234]{2,0,1:T(8,128)(2,1)S(1)}, u32[]{:S(2)}, u32[]{:S(2)}) collective-permute-start(bf16[8,117,234]{2,0,1:T(8,128)(2,1)} %collective-permute-done.3), channel_id=1, source_target_pairs={{8,4},{9,5},{10,6},{11,7},{24,20},{25,21},{26,22},{27,23}} | collective-permute-start | bytes 1314152 | tf_op jit(solution)/shard_map/ppermute | solution.py:162
  91.9 2.3 %copy-start.4 = (bf16[16,13,40,13]{2,0,3,1:T(8,128)(2,1)S(1)}, bf16[16,13,40,13]{2,0,3,1:T(8,128)(2,1)}, u32[]{:S(2)}) copy-start(bf16[16,13,40,13]{2,0,3,1:T(8,128)(2,1)} %copy.19) | copy-start | bytes 648964
  95.4 19.5 %collective-permute-start.7 = (bf16[8,117,234]{2,1,0:T(8,128)(2,1)S(1)}, bf16[8,117,234]{2,1,0:T(8,128)(2,1)S(1)}, u32[]{:S(2)}, u32[]{:S(2)}) collective-permute-start(bf16[8,117,234]{2,1,0:T(8,128)(2,1)S(1)} %copy.21), channel_id=1, source_target_pairs={{8,12},{4,0},{9,13},{5,1},{10,14},{6,2},{11,15},{7,3},{24,28},{20,... | collective-permute-start | bytes 1314152 | tf_op jit(solution)/shard_map/ppermute | solution.py:177
  98.9 1.8 %copy-start.3 = (bf16[8,234,234]{2,0,1:T(8,128)(2,1)S(1)}, bf16[8,234,234]{2,0,1:T(8,128)(2,1)}, u32[]{:S(2)}) copy-start(bf16[8,234,234]{2,0,1:T(8,128)(2,1)} %param.7) | copy-start | bytes 2628292
  99.0 23.8 %collective-permute-start.10 = (bf16[8,117,234]{2,1,0:T(8,128)(2,1)S(1)}, bf16[8,117,234]{2,1,0:T(8,128)(2,1)S(1)}, u32[]{:S(2)}, u32[]{:S(2)}) collective-permute-start(bf16[8,117,234]{2,1,0:T(8,128)(2,1)S(1)} %copy.25), channel_id=1, source_target_pairs={{8,12},{4,0},{9,13},{5,1},{10,14},{6,2},{11,15},{7,3},{24,28},{20,... | collective-permute-start | bytes 1314152 | tf_op jit(solution)/shard_map/ppermute | solution.py:177
  115.3 10.1 %collective-permute-start.11 = (bf16[8,117,234]{2,1,0:T(8,128)(2,1)S(1)}, bf16[8,117,234]{2,1,0:T(8,128)(2,1)S(1)}, u32[]{:S(2)}, u32[]{:S(2)}) collective-permute-start(bf16[8,117,234]{2,1,0:T(8,128)(2,1)S(1)} %fusion.26), channel_id=1, source_target_pairs={{0,1},{1,0},{2,3},{3,2},{4,5},{5,4},{6,7},{7,6},{8,9},{9,8},{10,11... | collective-permute-start | bytes 1314152 | tf_op jit(solution)/shard_map/ppermute | solution.py:182
  123.3 3.4 %collective-permute-start.12 = (bf16[8,117,234]{2,1,0:T(8,128)(2,1)S(1)}, bf16[8,117,234]{2,1,0:T(8,128)(2,1)S(1)}, u32[]{:S(2)}, u32[]{:S(2)}) collective-permute-start(bf16[8,117,234]{2,1,0:T(8,128)(2,1)S(1)} %fusion.24), channel_id=1, source_target_pairs={{0,1},{1,0},{2,3},{3,2},{4,5},{5,4},{6,7},{7,6},{8,9},{9,8},{10,11... | collective-permute-start | bytes 1314152 | tf_op jit(solution)/shard_map/ppermute | solution.py:182
  123.3 14.1 %collective-permute-start.13 = (bf16[8,117,234]{2,1,0:T(8,128)(2,1)S(1)}, bf16[8,117,234]{2,1,0:T(8,128)(2,1)S(1)}, u32[]{:S(2)}, u32[]{:S(2)}) collective-permute-start(bf16[8,117,234]{2,1,0:T(8,128)(2,1)S(1)} %fusion.26), channel_id=1, source_target_pairs={{0,2},{2,0},{1,3},{3,1},{4,6},{6,4},{5,7},{7,5},{8,10},{10,8},{9,1... | collective-permute-start | bytes 1314152 | tf_op jit(solution)/shard_map/ppermute | solution.py:181
  124.9 22.6 %collective-permute-start.14 = (bf16[8,117,234]{2,1,0:T(8,128)(2,1)S(1)}, bf16[8,117,234]{2,1,0:T(8,128)(2,1)S(1)}, u32[]{:S(2)}, u32[]{:S(2)}) collective-permute-start(bf16[8,117,234]{2,1,0:T(8,128)(2,1)S(1)} %fusion.24), channel_id=1, source_target_pairs={{0,2},{2,0},{1,3},{3,1},{4,6},{6,4},{5,7},{7,5},{8,10},{10,8},{9,1... | collective-permute-start | bytes 1314152 | tf_op jit(solution)/shard_map/ppermute | solution.py:181

commit v4 on v2

--- a/solution.py
+++ b/solution.py
@@ -3,6 +3,8 @@
 import jax
 import jax.numpy as jnp
 from jax import lax
+from jax.experimental import pallas as pl
+from jax.experimental.pallas import tpu as pltpu
 from jax.sharding import PartitionSpec as P
 
 LX = 48
@@ -73,6 +75,70 @@
     return (merged.astype(jnp.float32) + change).astype(jnp.bfloat16)
 
 
+def three_parts(values):
+    high = values.astype(jnp.bfloat16).astype(jnp.float32)
+    rest = values - high
+    middle = rest.astype(jnp.bfloat16).astype(jnp.float32)
+    return jnp.concatenate([high, middle, rest - middle], axis=0).astype(jnp.bfloat16)
+
+
+def spread(one_hot, values):
+    return jnp.dot(one_hot, three_parts(values), preferred_element_type=jnp.float32)
+
+
+def loop_kernel(
+    window_ref, column_ref, left_ref, right_ref, form_ref, rows_l, rows_r, rows_f, out_ref,
+    loop_l, form_all,
+):
+    @pl.when(pl.program_id(0) == 0)
+    def _():
+        form_all[...] = spread(rows_f[...], form_ref[...])
+        loop_l[...] = (spread(rows_l[...], left_ref[...]) * form_all[...]).astype(jnp.bfloat16)
+
+    qpoint = window_ref[pl.program_id(0)]
+    values = right_ref[...]
+    total_k = values.shape[1]
+    straight = pltpu.roll(values, lax.rem(total_k - qpoint, total_k), 1)
+    wrapped = pltpu.roll(values, lax.rem(total_k - qpoint + LX, total_k), 1)
+    stays = column_ref[...] + lax.rem(qpoint, LX) < LX
+    picked = spread(rows_r[...], jnp.where(stays, straight, wrapped))
+    loop_r = (picked * form_all[...] * (1.0 / total_k)).astype(jnp.bfloat16)
+    product = lax.dot_general(
+        loop_l[...], loop_r, (((1,), (1,)), ((), ())), preferred_element_type=jnp.float32
+    )
+    out_ref[0] = product.astype(jnp.bfloat16)
+
+
+def padded_rows(values, step):
+    return jnp.pad(values, ((0, -values.shape[0] % step), (0, 0)))
+
+
+def one_hot_rows(index, height):
+    places = jnp.arange(3 * height, dtype=jnp.int32) % height
+    return (index[:, None] == places[None, :]).astype(jnp.bfloat16)
+
+
+def loop_matrices(qpoints, column, left, right, form, rows_l, rows_r, rows_f):
+    points = qpoints.shape[0]
+    order = rows_l.shape[0]
+    total_k = left.shape[1]
+    whole = [column, left, right, form, rows_l, rows_r, rows_f]
+    return pl.pallas_call(
+        loop_kernel,
+        grid=(points,),
+        out_shape=jax.ShapeDtypeStruct((points, order, order), jnp.bfloat16),
+        in_specs=[pl.BlockSpec(memory_space=pltpu.SMEM)]
+        + [pl.BlockSpec(each.shape, lambda i: (0, 0)) for each in whole],
+        out_specs=pl.BlockSpec((1, order, order), lambda i: (i, 0, 0)),
+        scratch_shapes=[
+            pltpu.VMEM((order, total_k), jnp.bfloat16),
+            pltpu.VMEM((order, total_k), jnp.float32),
+        ],
+        compiler_params=pltpu.CompilerParams(vmem_limit_bytes=36 * 1024 * 1024),
+        cost_estimate=pl.CostEstimate(flops=1000, bytes_accessed=1000, transcendentals=0),
+    )(qpoints, *whole)
+
+
 CHUNKS = 2
 ENDS = 4
 
@@ -105,24 +171,35 @@
     ]
     below = [lax.ppermute(piece, "mom", up) for piece in pieces]
     above = [lax.ppermute(piece, "mom", down) for piece in pieces]
-    far_below = [lax.ppermute(piece, "mom", [(1, 2)]) for piece in below]
-    far_above = [lax.ppermute(piece, "mom", [(2, 1)]) for piece in above]
-
     my_window = lax.dynamic_slice_in_dim(window, place * points, points, 0)
     momenta = jnp.arange(total_k, dtype=jnp.int32)
     form_table = form_factors(shifts, momenta)
-    half_pairs = green_left.shape[0] // 2
-    first_left = jnp.where(
-        lax.axis_index("ff") == 0, green_left, jnp.roll(green_left, half_pairs, axis=0)
-    )
-    first_right = jnp.where(
-        lax.axis_index("orb") == 0, green_right, jnp.roll(green_right, half_pairs, axis=0)
-    )
-    left_loop = loop_left(first_left, form_table)
-    right_loop = loop_right_all(first_right, form_table, momenta, my_window, total_k)
-    bubble = jnp.einsum(
-        "jk,qik->qji", left_loop, right_loop, preferred_element_type=jnp.float32
-    ).astype(jnp.bfloat16)
+    all_pairs = green_left.shape[0]
+    left = padded_rows(green_left, 8)
+    right = padded_rows(green_right, 8)
+    form = padded_rows(form_table, 8)
+    order = jnp.arange(all_pairs * form_count, dtype=jnp.int32)
+    my_col = lax.axis_index("ff") * (all_pairs // 2)
+    my_row = lax.axis_index("orb") * (all_pairs // 2)
+    rows_l = one_hot_rows((order // form_count + my_col) % all_pairs, left.shape[0])
+    rows_r = one_hot_rows((order // form_count + my_row) % all_pairs, right.shape[0])
+    rows_f = one_hot_rows(order % form_count, form.shape[0])
+    column = (momenta % LX)[None, :]
+    cut = points // 2
+    tables = (left, right, form, rows_l, rows_r, rows_f)
+    right, below[0], above[0] = lax.optimization_barrier((right, below[0], above[0]))
+    far_below = [lax.ppermute(below[0], "mom", [(1, 2)])]
+    far_above = [lax.ppermute(above[0], "mom", [(2, 1)])]
+    first = loop_matrices(my_window[:cut], column, left, right, *tables[2:])
+    first, right, *rest = lax.optimization_barrier((first, right, *below[1:], *above[1:]))
+    below[1:], above[1:] = rest[: CHUNKS - 1], rest[CHUNKS - 1 :]
+    far_below += [lax.ppermute(piece, "mom", [(1, 2)]) for piece in below[1:]]
+    far_above += [lax.ppermute(piece, "mom", [(2, 1)]) for piece in above[1:]]
+    second = loop_matrices(my_window[cut:], column, left, right, *tables[2:])
+    first, second, far_below[0], far_above[0] = lax.optimization_barrier(
+        (first, second, far_below[0], far_above[0])
+    )
+    bubble = (first, second)
 
     merged, halves, across = [], [], []
     swap = [(0, 1), (1, 0)]
@@ -138,11 +215,11 @@
         across.append(lax.ppermute(mine, "orb", swap))
         beside = lax.ppermute(mine, "ff", swap)
         rows = jnp.concatenate([mine, beside], axis=2)
-        halves.append(
-            jnp.einsum(
-                "qrj,qji->qri", rows, bubble, preferred_element_type=jnp.float32
-            ).astype(jnp.bfloat16)
-        )
+        parts = [
+            jnp.einsum("qrj,qji->qri", part, loops, preferred_element_type=jnp.float32)
+            for part, loops in zip((rows[:cut], rows[cut:]), bubble)
+        ]
+        halves.append(jnp.concatenate(parts, axis=0).astype(jnp.bfloat16))
     half = jnp.concatenate(halves, axis=1)
     tall = jnp.concatenate(merged + across, axis=1)
     change = jnp.einsum("qri,qic->qrc", half, tall, preferred_element_type=jnp.float32)

time: 155 us -> 120 us (0.77)
  between operations: 26.5 us -> 0.54 us
  Pallas kernels: 0 us -> 22 us
  waiting for transfers between devices: 43.6 us -> 30.4 us
  matrix products: 20.1 us -> 8.87 us
  other arithmetic: 12.2 us -> 2.9 us
  starting transfers between devices: 27.7 us -> 30.2 us
    pallas_call x0 -> x2, Pallas kernels: none -> 22 us  [loop_matrices(): pl.pallas_call(loop_kernel, grid=(points,), out_shape=jax.ShapeDtypeStruc...]
    dot_general x3 -> x4, matrix products: 15.9 us -> 3.82 us  [body_line(): jnp.einsum('qrj,qji->qri', part, loops, preferred_element_type=jnp.float32)]
    ppermute x2, waiting for transfers between devices: 19.1 us -> 11 us  [body_line(): across.append(lax.ppermute(mine, 'orb', swap))]
    convert_element_type x2, other arithmetic: 6.71 us -> 0.32 us  [one_hot_rows(): return (index[:, None] == places[None, :]).astype(jnp.bfloat16)]
    ppermute x2, waiting for transfers between devices: 24.5 us -> 19.4 us  [body_line(): lax.ppermute(sums[points:].astype(jnp.bfloat16), 'mom', [(2, 3), (1, 0)])]
    unnamed x7 -> x0, other arithmetic: 3.26 us -> none
    reshape x2, local copies, waits for them, and re-layouts: 3.3 us -> 6.04 us  [body_line(): weights = weights.reshape(2 * points, form_count, 5 * points, form_count)]
    convert_element_type x1 -> x0, local copies, waits for them, and re-layouts: 2.05 us -> none  [loop_left(): return loop_rows.reshape(-1, form_table.shape[1]).astype(jnp.bfloat16)]
  transfers between devices with their start and end apart: 15 -> 15, of which waited for: 4 -> 4; matrix products, arithmetic and copies ran while one was open for 33% -> 25% of each run, Pallas kernels for 0% -> 18%
where the time goes in v4:
time: 120 us
  waiting for transfers between devices  30.4 us (25%)
  starting transfers between devices  30.2 us (25%)
  local copies, waits for them, and re-layouts  24.8 us (21%)
  Pallas kernels  22 us (18%)
  matrix products  8.87 us (7%)
  other arithmetic  2.9 us (2%)
    pallas_call x2, Pallas kernels, loop_matrices(): pl.pallas_call(loop_kernel, grid=(points,), out_shape=jax.ShapeDtypeStruc...  22 us
    ppermute x2, waiting for transfers between devices, body_line(): lax.ppermute(sums[points:].astype(jnp.bfloat16), 'mom', [(2, 3), (1, 0)])  19.4 us
    ppermute x2, starting transfers between devices, body_line(): below = [lax.ppermute(piece, 'mom', up) for piece in pieces]  11 us
    ppermute x2, waiting for transfers between devices, body_line(): across.append(lax.ppermute(mine, 'orb', swap))  11 us
    unnamed x25, local copies, waits for them, and re-layouts  6.61 us
    reshape x2, local copies, waits for them, and re-layouts, body_line(): weights = weights.reshape(2 * points, form_count, 5 * points, form_count)  6.04 us
    ppermute x1, starting transfers between devices, body_line(): lax.ppermute(jnp.where(place == 3, to_two, to_one), 'mom', [(3, 2), (0, 1)])  5.34 us
    dot_general x4, matrix products, body_line(): jnp.einsum('qrj,qji->qri', part, loops, preferred_element_type=jnp.float32)  3.82 us
  transfers between devices with their start and end apart: 15, of which 4 were waited for; matrix products, arithmetic and copies ran while one was open for 25% of the time, Pallas kernels for 18%

profile of v4, /device:TPU:0, one launch (start us, length us, event | category | flops | bytes accessed | tf_op | source)
XLA Modules:
  0.0 119.9 jit_solution(14613211540759099537)
XLA Ops:
  0.0 2.2 %fusion.51 = (bf16[8,117,234]{2,0,1:T(8,128)(2,1)}, bf16[8,117,234]{2,0,1:T(8,128)(2,1)}) fusion(bf16[8,234,234]{2,0,1:T(8,128)(2,1)} %param.8), kind=kLoop, calls=%fused_computation.98 | loop fusion | bytes 1752192 | tf_op jit(solution)/shard_map/slice | solution.py:170
  2.2 5.7 %collective-permute-start = (bf16[8,117,234]{2,0,1:T(8,128)(2,1)}, bf16[8,117,234]{2,0,1:T(8,128)(2,1)}, u32[]{:S(2)}, u32[]{:S(2)}) collective-permute-start(bf16[8,117,234]{2,0,1:T(8,128)(2,1)} %get-tuple-element.32), channel_id=1, source_target_pairs={{0,4},{4,8},{8,12},{1,5},{5,9},{9,13},{2,6},{6,10},{10,14},{3,7},{... | collective-permute-start | bytes 1314152 | tf_op jit(solution)/shard_map/ppermute | solution.py:172
  7.9 1.3 %collective-permute-start.1 = (bf16[8,117,234]{2,0,1:T(8,128)(2,1)}, bf16[8,117,234]{2,0,1:T(8,128)(2,1)}, u32[]{:S(2)}, u32[]{:S(2)}) collective-permute-start(bf16[8,117,234]{2,0,1:T(8,128)(2,1)} %get-tuple-element.32), channel_id=1, source_target_pairs={{4,0},{8,4},{12,8},{5,1},{9,5},{13,9},{6,2},{10,6},{14,10},{7,3},{... | collective-permute-start | bytes 1314152 | tf_op jit(solution)/shard_map/ppermute | solution.py:173
  9.2 5.3 %collective-permute-start.2 = (bf16[8,117,234]{2,0,1:T(8,128)(2,1)}, bf16[8,117,234]{2,0,1:T(8,128)(2,1)}, u32[]{:S(2)}, u32[]{:S(2)}) collective-permute-start(bf16[8,117,234]{2,0,1:T(8,128)(2,1)} %get-tuple-element.31), channel_id=1, source_target_pairs={{0,4},{4,8},{8,12},{1,5},{5,9},{9,13},{2,6},{6,10},{10,14},{3,7},{... | collective-permute-start | bytes 1314152 | tf_op jit(solution)/shard_map/ppermute | solution.py:172
  14.5 1.3 %collective-permute-start.3 = (bf16[8,117,234]{2,0,1:T(8,128)(2,1)}, bf16[8,117,234]{2,0,1:T(8,128)(2,1)}, u32[]{:S(2)}, u32[]{:S(2)}) collective-permute-start(bf16[8,117,234]{2,0,1:T(8,128)(2,1)} %get-tuple-element.31), channel_id=1, source_target_pairs={{4,0},{8,4},{12,8},{5,1},{9,5},{13,9},{6,2},{10,6},{14,10},{7,3},{... | collective-permute-start | bytes 1314152 | tf_op jit(solution)/shard_map/ppermute | solution.py:173
  15.8 1.1 pad_bitcast_fusion
  17.0 1.6 %copy.16 = bf16[8,13,64,13]{3,2,1,0:T(8,128)(2,1)S(1)} copy(bf16[8,13,64,13]{2,0,3,1:T(8,128)(2,1)S(1)} %pad_bitcast_fusion) | data formatting | bytes 346112 | tf_op jit(solution)/shard_map/transpose | solution.py:156
  18.6 3.0 %reshape.108 = bf16[104,832]{1,0:T(8,128)(2,1)S(1)} reshape(bf16[8,13,64,13]{3,2,1,0:T(8,128)(2,1)S(1)} %copy.16) | data formatting | bytes 346112 | tf_op jit(solution)/shard_map/reshape | solution.py:156
  21.8 5.3 %collective-permute-start.6 = (bf16[104,520]{1,0:T(8,128)(2,1)S(1)}, bf16[104,520]{1,0:T(8,128)(2,1)}, u32[]{:S(2)}, u32[]{:S(2)}) collective-permute-start(bf16[104,520]{1,0:T(8,128)(2,1)S(1)} %pad_select_fusion), channel_id=1, source_target_pairs={{12,8},{0,4},{13,9},{1,5},{14,10},{2,6},{15,11},{3,7},{28,24},{16,... | collective-permute-start | bytes 324488 | tf_op jit(solution)/shard_map/ppermute | solution.py:163
  29.5 1.5 %collective-permute-start.4 = (bf16[8,117,234]{2,0,1:T(8,128)(2,1)}, bf16[8,117,234]{2,0,1:T(8,128)(2,1)}, u32[]{:S(2)}, u32[]{:S(2)}) collective-permute-start(bf16[8,117,234]{2,0,1:T(8,128)(2,1)} %collective-permute-done), channel_id=1, source_target_pairs={{4,8},{5,9},{6,10},{7,11},{20,24},{21,25},{22,26},{23,27}} | collective-permute-start | bytes 1314152 | tf_op jit(solution)/shard_map/ppermute | solution.py:191
  31.0 1.5 %collective-permute-start.5 = (bf16[8,117,234]{2,0,1:T(8,128)(2,1)}, bf16[8,117,234]{2,0,1:T(8,128)(2,1)}, u32[]{:S(2)}, u32[]{:S(2)}) collective-permute-start(bf16[8,117,234]{2,0,1:T(8,128)(2,1)} %collective-permute-done.1), channel_id=1, source_target_pairs={{8,4},{9,5},{10,6},{11,7},{24,20},{25,21},{26,22},{27,23}} | collective-permute-start | bytes 1314152 | tf_op jit(solution)/shard_map/ppermute | solution.py:192
  32.5 11.0 %shard_map.73 = bf16[4,468,468]{2,1,0:T(8,128)(2,1)S(1)} custom-call(s32[4]{0:T(128)S(1)} %get-tuple-element.38.window_ref, s32[1,2304]{1,0:T(1,128)S(1)} %and_select_fusion.column_ref, f32[40,2304]{1,0:T(8,128)S(1)} %pad.17.left_ref, f32[40,2304]{1,0:T(8,128)S(1)} %pad.18.right_ref, f32[16,2304]{1,0:T(8,128)S(1)} %pad.19.form_ref, ...), custom_call_target="tpu_custom_call" | custom-call | flops 1000 | bytes 1000 | tf_op jit(solution)/shard_map/pallas_call | solution.py:126
  43.5 1.5 %collective-permute-start.8 = (bf16[8,117,234]{2,0,1:T(8,128)(2,1)}, bf16[8,117,234]{2,0,1:T(8,128)(2,1)}, u32[]{:S(2)}, u32[]{:S(2)}) collective-permute-start(bf16[8,117,234]{2,0,1:T(8,128)(2,1)} %collective-permute-done.2), channel_id=1, source_target_pairs={{4,8},{5,9},{6,10},{7,11},{20,24},{21,25},{22,26},{23,27}} | collective-permute-start | bytes 1314152 | tf_op jit(solution)/shard_map/ppermute | solution.py:196
  46.1 2.6 %reshape.109 = bf16[16,13,40,13]{3,2,1,0:T(8,128)(2,1)} reshape(bf16[208,520]{1,0:T(8,128)(2,1)S(1)} %pad_maximum_fusion.6) | data formatting | bytes 432640 | tf_op jit(solution)/shard_map/reshape | solution.py:165
  48.6 3.5 %copy.17 = bf16[16,13,40,13]{2,0,3,1:T(8,128)(2,1)} copy(bf16[16,13,40,13]{3,2,1,0:T(8,128)(2,1)} %reshape.109) | data formatting | bytes 432640 | tf_op jit(solution)/shard_map/reshape | solution.py:165
  53.0 11.0 %shard_map.74 = bf16[4,468,468]{2,1,0:T(8,128)(2,1)S(1)} custom-call(s32[4]{0:T(128)S(1)} %get-tuple-element.37.window_ref, s32[1,2304]{1,0:T(1,128)S(1)} %and_select_fusion.column_ref, f32[40,2304]{1,0:T(8,128)S(1)} %pad.17.left_ref, f32[40,2304]{1,0:T(8,128)S(1)} %pad.18.right_ref, f32[16,2304]{1,0:T(8,128)S(1)} %pad.19.form_ref, ...), custom_call_target="tpu_custom_call" | custom-call | flops 1000 | bytes 1000 | tf_op jit(solution)/shard_map/pallas_call | solution.py:126
  64.0 1.1 constant_dynamic-update-slice_fusion.4
  65.2 1.1 constant_dynamic-update-slice_fusion.3
  66.2 1.1 constant_dynamic-update-slice_fusion.9
  67.3 1.1 constant_dynamic-update-slice_fusion.8
  68.5 1.1 constant_dynamic-update-slice_fusion.1
  69.6 1.1 constant_dynamic-update-slice_fusion
  71.8 1.3 %collective-permute-start.7 = (bf16[8,117,234]{2,1,0:T(8,128)(2,1)S(1)}, bf16[8,117,234]{2,1,0:T(8,128)(2,1)S(1)}, u32[]{:S(2)}, u32[]{:S(2)}) collective-permute-start(bf16[8,117,234]{2,1,0:T(8,128)(2,1)S(1)} %copy.19), channel_id=1, source_target_pairs={{8,12},{4,0},{9,13},{5,1},{10,14},{6,2},{11,15},{7,3},{24,28},{20,... | collective-permute-start | bytes 1314152 | tf_op jit(solution)/shard_map/ppermute | solution.py:211
  73.1 1.1 constant_dynamic-update-slice_fusion.6
  75.4 1.5 %collective-permute-start.10 = (bf16[8,117,234]{2,1,0:T(8,128)(2,1)S(1)}, bf16[8,117,234]{2,1,0:T(8,128)(2,1)S(1)}, u32[]{:S(2)}, u32[]{:S(2)}) collective-permute-start(bf16[8,117,234]{2,1,0:T(8,128)(2,1)S(1)} %copy.23), channel_id=1, source_target_pairs={{8,12},{4,0},{9,13},{5,1},{10,14},{6,2},{11,15},{7,3},{24,28},{20,... | collective-permute-start | bytes 1314152 | tf_op jit(solution)/shard_map/ppermute | solution.py:211
  77.1 13.7 %collective-permute-done.7 = bf16[8,117,234]{2,1,0:T(8,128)(2,1)S(1)} collective-permute-done((bf16[8,117,234]{2,1,0:T(8,128)(2,1)S(1)}, bf16[8,117,234]{2,1,0:T(8,128)(2,1)S(1)}, u32[]{:S(2)}, u32[]{:S(2)}) %collective-permute-start.7) | collective-permute-done | bytes 438080 | tf_op jit(solution)/shard_map/ppermute | solution.py:211
  91.3 1.6 %collective-permute-start.13 = (bf16[8,117,234]{2,1,0:T(8,128)(2,1)S(1)}, bf16[8,117,234]{2,1,0:T(8,128)(2,1)S(1)}, u32[]{:S(2)}, u32[]{:S(2)}) collective-permute-start(bf16[8,117,234]{2,1,0:T(8,128)(2,1)S(1)} %fusion.18), channel_id=1, source_target_pairs={{0,2},{2,0},{1,3},{3,1},{4,6},{6,4},{5,7},{7,5},{8,10},{10,8},{9,1... | collective-permute-start | bytes 1314152 | tf_op jit(solution)/shard_map/ppermute | solution.py:215
  92.9 5.8 %collective-permute-done.10 = bf16[8,117,234]{2,1,0:T(8,128)(2,1)S(1)} collective-permute-done((bf16[8,117,234]{2,1,0:T(8,128)(2,1)S(1)}, bf16[8,117,234]{2,1,0:T(8,128)(2,1)S(1)}, u32[]{:S(2)}, u32[]{:S(2)}) %collective-permute-start.10) | collective-permute-done | bytes 438080 | tf_op jit(solution)/shard_map/ppermute | solution.py:211
  99.1 1.6 %collective-permute-start.14 = (bf16[8,117,234]{2,1,0:T(8,128)(2,1)S(1)}, bf16[8,117,234]{2,1,0:T(8,128)(2,1)S(1)}, u32[]{:S(2)}, u32[]{:S(2)}) collective-permute-start(bf16[8,117,234]{2,1,0:T(8,128)(2,1)S(1)} %fusion.16), channel_id=1, source_target_pairs={{0,2},{2,0},{1,3},{3,1},{4,6},{6,4},{5,7},{7,5},{8,10},{10,8},{9,1... | collective-permute-start | bytes 1314152 | tf_op jit(solution)/shard_map/ppermute | solution.py:215
  105.4 10.1 %collective-permute-done.14 = bf16[8,117,234]{2,1,0:T(8,128)(2,1)S(1)} collective-permute-done((bf16[8,117,234]{2,1,0:T(8,128)(2,1)S(1)}, bf16[8,117,234]{2,1,0:T(8,128)(2,1)S(1)}, u32[]{:S(2)}, u32[]{:S(2)}) %collective-permute-start.14) | collective-permute-done | bytes 438080 | tf_op jit(solution)/shard_map/ppermute | solution.py:215
  115.5 3.1 %add_convert_fusion = bf16[8,234,234]{2,1,0:T(8,128)(2,1)S(1)} fusion(bf16[8,117,234]{2,1,0:T(8,128)(2,1)S(1)} %fusion.16, bf16[8,117,234]{2,1,0:T(8,128)(2,1)S(1)} %fusion.18, bf16[8,117,234]{2,1,0:T(8,128)(2,1)S(1)} %collective-permute-done.14, bf16[8,117,234]{2,1,0:T(8,128)(2,1)S(1)} %collective-permute-done.13, ...), kind=kOutput, calls=%fused_computation | convolution fusion | flops 426658752 | bytes 4380480 | tf_op jit(solution)/shard_map/qri,qic->qrc/dot_general | solution.py:225
  118.6 1.3 %copy.24 = bf16[8,234,234]{2,0,1:T(8,128)(2,1)} copy(bf16[8,234,234]{2,1,0:T(8,128)(2,1)S(1)} %add_convert_fusion) | data formatting | bytes 1752192 | tf_op jit(solution)/shard_map/convert_element_type | solution.py:227
  (70 shorter events, 12.6 us)
Async XLA Ops:
  2.2 27.3 %collective-permute-start = (bf16[8,117,234]{2,0,1:T(8,128)(2,1)}, bf16[8,117,234]{2,0,1:T(8,128)(2,1)}, u32[]{:S(2)}, u32[]{:S(2)}) collective-permute-start(bf16[8,117,234]{2,0,1:T(8,128)(2,1)} %get-tuple-element.32), channel_id=1, source_target_pairs={{0,4},{4,8},{8,12},{1,5},{5,9},{9,13},{2,6},{6,10},{10,14},{3,7},{... | collective-permute-start | bytes 1314152 | tf_op jit(solution)/shard_map/ppermute | solution.py:172
  7.9 21.6 %collective-permute-start.1 = (bf16[8,117,234]{2,0,1:T(8,128)(2,1)}, bf16[8,117,234]{2,0,1:T(8,128)(2,1)}, u32[]{:S(2)}, u32[]{:S(2)}) collective-permute-start(bf16[8,117,234]{2,0,1:T(8,128)(2,1)} %get-tuple-element.32), channel_id=1, source_target_pairs={{4,0},{8,4},{12,8},{5,1},{9,5},{13,9},{6,2},{10,6},{14,10},{7,3},{... | collective-permute-start | bytes 1314152 | tf_op jit(solution)/shard_map/ppermute | solution.py:173
  9.2 34.3 %collective-permute-start.2 = (bf16[8,117,234]{2,0,1:T(8,128)(2,1)}, bf16[8,117,234]{2,0,1:T(8,128)(2,1)}, u32[]{:S(2)}, u32[]{:S(2)}) collective-permute-start(bf16[8,117,234]{2,0,1:T(8,128)(2,1)} %get-tuple-element.31), channel_id=1, source_target_pairs={{0,4},{4,8},{8,12},{1,5},{5,9},{9,13},{2,6},{6,10},{10,14},{3,7},{... | collective-permute-start | bytes 1314152 | tf_op jit(solution)/shard_map/ppermute | solution.py:172
  14.5 29.0 %collective-permute-start.3 = (bf16[8,117,234]{2,0,1:T(8,128)(2,1)}, bf16[8,117,234]{2,0,1:T(8,128)(2,1)}, u32[]{:S(2)}, u32[]{:S(2)}) collective-permute-start(bf16[8,117,234]{2,0,1:T(8,128)(2,1)} %get-tuple-element.31), channel_id=1, source_target_pairs={{4,0},{8,4},{12,8},{5,1},{9,5},{13,9},{6,2},{10,6},{14,10},{7,3},{... | collective-permute-start | bytes 1314152 | tf_op jit(solution)/shard_map/ppermute | solution.py:173
  15.8 11.4 %copy-start.7 = (s32[13,2]{0,1:T(2,128)S(1)}, s32[13,2]{0,1:T(2,128)}, u32[]{:S(2)}) copy-start(s32[13,2]{0,1:T(2,128)} %param.13) | copy-start | bytes 316
  17.0 10.3 %copy-start.5 = (f32[36,2304]{1,0:T(8,128)S(1)}, f32[36,2304]{1,0:T(8,128)}, u32[]{:S(2)}) copy-start(f32[36,2304]{1,0:T(8,128)} %param.11) | copy-start | bytes 995332
  17.0 11.0 %copy-start.6 = (f32[36,2304]{1,0:T(8,128)S(1)}, f32[36,2304]{1,0:T(8,128)}, u32[]{:S(2)}) copy-start(f32[36,2304]{1,0:T(8,128)} %param.10) | copy-start | bytes 995332
  21.6 6.5 %copy-start.3 = (bf16[8,234,234]{2,0,1:T(8,128)(2,1)S(1)}, bf16[8,234,234]{2,0,1:T(8,128)(2,1)}, u32[]{:S(2)}) copy-start(bf16[8,234,234]{2,0,1:T(8,128)(2,1)} %param.7) | copy-start | bytes 2628292
  21.6 7.5 %copy-start.8 = (s32[32]{0:T(128)S(1)}, s32[32]{0:T(128)}, u32[]{:S(2)}) copy-start(s32[32]{0:T(128)} %param.12) | copy-start | bytes 388
  21.8 23.3 %collective-permute-start.6 = (bf16[104,520]{1,0:T(8,128)(2,1)S(1)}, bf16[104,520]{1,0:T(8,128)(2,1)}, u32[]{:S(2)}, u32[]{:S(2)}) collective-permute-start(bf16[104,520]{1,0:T(8,128)(2,1)S(1)} %pad_select_fusion), channel_id=1, source_target_pairs={{12,8},{0,4},{13,9},{1,5},{14,10},{2,6},{15,11},{3,7},{28,24},{16,... | collective-permute-start | bytes 324488 | tf_op jit(solution)/shard_map/ppermute | solution.py:163
  29.5 34.5 %collective-permute-start.4 = (bf16[8,117,234]{2,0,1:T(8,128)(2,1)}, bf16[8,117,234]{2,0,1:T(8,128)(2,1)}, u32[]{:S(2)}, u32[]{:S(2)}) collective-permute-start(bf16[8,117,234]{2,0,1:T(8,128)(2,1)} %collective-permute-done), channel_id=1, source_target_pairs={{4,8},{5,9},{6,10},{7,11},{20,24},{21,25},{22,26},{23,27}} | collective-permute-start | bytes 1314152 | tf_op jit(solution)/shard_map/ppermute | solution.py:191
  31.0 33.0 %collective-permute-start.5 = (bf16[8,117,234]{2,0,1:T(8,128)(2,1)}, bf16[8,117,234]{2,0,1:T(8,128)(2,1)}, u32[]{:S(2)}, u32[]{:S(2)}) collective-permute-start(bf16[8,117,234]{2,0,1:T(8,128)(2,1)} %collective-permute-done.1), channel_id=1, source_target_pairs={{8,4},{9,5},{10,6},{11,7},{24,20},{25,21},{26,22},{27,23}} | collective-permute-start | bytes 1314152 | tf_op jit(solution)/shard_map/ppermute | solution.py:192
  43.5 22.7 %collective-permute-start.8 = (bf16[8,117,234]{2,0,1:T(8,128)(2,1)}, bf16[8,117,234]{2,0,1:T(8,128)(2,1)}, u32[]{:S(2)}, u32[]{:S(2)}) collective-permute-start(bf16[8,117,234]{2,0,1:T(8,128)(2,1)} %collective-permute-done.2), channel_id=1, source_target_pairs={{4,8},{5,9},{6,10},{7,11},{20,24},{21,25},{22,26},{23,27}} | collective-permute-start | bytes 1314152 | tf_op jit(solution)/shard_map/ppermute | solution.py:196
  52.1 22.1 %collective-permute-start.9 = (bf16[8,117,234]{2,0,1:T(8,128)(2,1)}, bf16[8,117,234]{2,0,1:T(8,128)(2,1)S(1)}, u32[]{:S(2)}, u32[]{:S(2)}) collective-permute-start(bf16[8,117,234]{2,0,1:T(8,128)(2,1)} %collective-permute-done.3), channel_id=1, source_target_pairs={{8,4},{9,5},{10,6},{11,7},{24,20},{25,21},{26,22},{27,23}} | collective-permute-start | bytes 1314152 | tf_op jit(solution)/shard_map/ppermute | solution.py:197
  64.0 4.5 %copy-start = (bf16[8,234,234]{2,0,1:T(8,128)(2,1)S(1)}, bf16[8,234,234]{2,0,1:T(8,128)(2,1)}, u32[]{:S(2)}) copy-start(bf16[8,234,234]{2,0,1:T(8,128)(2,1)} %param.8) | copy-start | bytes 2628292
  67.3 3.4 %copy-start.4 = (bf16[16,13,40,13]{2,0,3,1:T(8,128)(2,1)S(1)}, bf16[16,13,40,13]{2,0,3,1:T(8,128)(2,1)}, u32[]{:S(2)}) copy-start(bf16[16,13,40,13]{2,0,3,1:T(8,128)(2,1)} %copy.17) | copy-start | bytes 648964
  71.8 18.9 %collective-permute-start.7 = (bf16[8,117,234]{2,1,0:T(8,128)(2,1)S(1)}, bf16[8,117,234]{2,1,0:T(8,128)(2,1)S(1)}, u32[]{:S(2)}, u32[]{:S(2)}) collective-permute-start(bf16[8,117,234]{2,1,0:T(8,128)(2,1)S(1)} %copy.19), channel_id=1, source_target_pairs={{8,12},{4,0},{9,13},{5,1},{10,14},{6,2},{11,15},{7,3},{24,28},{20,... | collective-permute-start | bytes 1314152 | tf_op jit(solution)/shard_map/ppermute | solution.py:211
  75.2 15.5 %copy-start.2 = (bf16[8,117,234]{2,0,1:T(8,128)(2,1)S(1)}, bf16[8,117,234]{2,0,1:T(8,128)(2,1)}, u32[]{:S(2)}) copy-start(bf16[8,117,234]{2,0,1:T(8,128)(2,1)} %get-tuple-element.27) | copy-start | bytes 1314148
  75.4 23.2 %collective-permute-start.10 = (bf16[8,117,234]{2,1,0:T(8,128)(2,1)S(1)}, bf16[8,117,234]{2,1,0:T(8,128)(2,1)S(1)}, u32[]{:S(2)}, u32[]{:S(2)}) collective-permute-start(bf16[8,117,234]{2,1,0:T(8,128)(2,1)S(1)} %copy.23), channel_id=1, source_target_pairs={{8,12},{4,0},{9,13},{5,1},{10,14},{6,2},{11,15},{7,3},{24,28},{20,... | collective-permute-start | bytes 1314152 | tf_op jit(solution)/shard_map/ppermute | solution.py:211
  77.0 21.6 %copy-start.1 = (bf16[8,117,234]{2,0,1:T(8,128)(2,1)S(1)}, bf16[8,117,234]{2,0,1:T(8,128)(2,1)}, u32[]{:S(2)}) copy-start(bf16[8,117,234]{2,0,1:T(8,128)(2,1)} %get-tuple-element.28) | copy-start | bytes 1314148
  91.1 9.6 %collective-permute-start.11 = (bf16[8,117,234]{2,1,0:T(8,128)(2,1)S(1)}, bf16[8,117,234]{2,1,0:T(8,128)(2,1)S(1)}, u32[]{:S(2)}, u32[]{:S(2)}) collective-permute-start(bf16[8,117,234]{2,1,0:T(8,128)(2,1)S(1)} %fusion.18), channel_id=1, source_target_pairs={{0,1},{1,0},{2,3},{3,2},{4,5},{5,4},{6,7},{7,6},{8,9},{9,8},{10,11... | collective-permute-start | bytes 1314152 | tf_op jit(solution)/shard_map/ppermute | solution.py:216
  91.3 14.1 %collective-permute-start.13 = (bf16[8,117,234]{2,1,0:T(8,128)(2,1)S(1)}, bf16[8,117,234]{2,1,0:T(8,128)(2,1)S(1)}, u32[]{:S(2)}, u32[]{:S(2)}) collective-permute-start(bf16[8,117,234]{2,1,0:T(8,128)(2,1)S(1)} %fusion.18), channel_id=1, source_target_pairs={{0,2},{2,0},{1,3},{3,1},{4,6},{6,4},{5,7},{7,5},{8,10},{10,8},{9,1... | collective-permute-start | bytes 1314152 | tf_op jit(solution)/shard_map/ppermute | solution.py:215
  99.1 3.6 %collective-permute-start.12 = (bf16[8,117,234]{2,1,0:T(8,128)(2,1)S(1)}, bf16[8,117,234]{2,1,0:T(8,128)(2,1)S(1)}, u32[]{:S(2)}, u32[]{:S(2)}) collective-permute-start(bf16[8,117,234]{2,1,0:T(8,128)(2,1)S(1)} %fusion.16), channel_id=1, source_target_pairs={{0,1},{1,0},{2,3},{3,2},{4,5},{5,4},{6,7},{7,6},{8,9},{9,8},{10,11... | collective-permute-start | bytes 1314152 | tf_op jit(solution)/shard_map/ppermute | solution.py:216
  99.1 16.4 %collective-permute-start.14 = (bf16[8,117,234]{2,1,0:T(8,128)(2,1)S(1)}, bf16[8,117,234]{2,1,0:T(8,128)(2,1)S(1)}, u32[]{:S(2)}, u32[]{:S(2)}) collective-permute-start(bf16[8,117,234]{2,1,0:T(8,128)(2,1)S(1)} %fusion.16), channel_id=1, source_target_pairs={{0,2},{2,0},{1,3},{3,1},{4,6},{6,4},{5,7},{7,5},{8,10},{10,8},{9,1... | collective-permute-start | bytes 1314152 | tf_op jit(solution)/shard_map/ppermute | solution.py:215

commit v5 on v4

--- a/solution.py
+++ b/solution.py
@@ -153,16 +153,12 @@
     chunk_rows = chunk_pairs * form_count
 
     padded = jnp.pad(project_coeff, ((0, 0), (2 * points, 2 * points), (0, 0), (0, 0)))
-    padded = padded.transpose(0, 2, 1, 3).reshape(points * form_count, -1)
-    wide = points * form_count
-    own_coeff = lax.dynamic_slice_in_dim(padded, place * wide, 5 * wide, 1)
-    straight = padded[:, 2 * wide : 6 * wide]
-    zero = jnp.zeros((wide, wide), straight.dtype)
-    to_two = jnp.concatenate([straight[:, : 2 * wide], zero, zero, zero], axis=1)
-    to_one = jnp.concatenate([zero, zero, zero, straight[:, 2 * wide :]], axis=1)
+    own_coeff = lax.dynamic_slice_in_dim(padded, place * points, 5 * points, 1)
+    near = 2 * points
+    to_two = jnp.pad(project_coeff[:, :near], ((0, 0), (0, 3 * points), (0, 0), (0, 0)))
+    to_one = jnp.pad(project_coeff[:, near:], ((0, 0), (3 * points, 0), (0, 0), (0, 0)))
     end_coeff = lax.ppermute(jnp.where(place == 3, to_two, to_one), "mom", [(3, 2), (0, 1)])
     weights = jnp.concatenate([own_coeff, end_coeff], axis=0)
-    weights = weights.reshape(2 * points, form_count, 5 * points, form_count)
 
     up = [(i, i + 1) for i in range(ENDS - 1)]
     down = [(i + 1, i) for i in range(ENDS - 1)]
@@ -185,41 +181,52 @@
     rows_r = one_hot_rows((order // form_count + my_row) % all_pairs, right.shape[0])
     rows_f = one_hot_rows(order % form_count, form.shape[0])
     column = (momenta % LX)[None, :]
-    cut = points // 2
-    tables = (left, right, form, rows_l, rows_r, rows_f)
-    right, below[0], above[0] = lax.optimization_barrier((right, below[0], above[0]))
-    far_below = [lax.ppermute(below[0], "mom", [(1, 2)])]
-    far_above = [lax.ppermute(above[0], "mom", [(2, 1)])]
-    first = loop_matrices(my_window[:cut], column, left, right, *tables[2:])
-    first, right, *rest = lax.optimization_barrier((first, right, *below[1:], *above[1:]))
-    below[1:], above[1:] = rest[: CHUNKS - 1], rest[CHUNKS - 1 :]
-    far_below += [lax.ppermute(piece, "mom", [(1, 2)]) for piece in below[1:]]
-    far_above += [lax.ppermute(piece, "mom", [(2, 1)]) for piece in above[1:]]
-    second = loop_matrices(my_window[cut:], column, left, right, *tables[2:])
-    first, second, far_below[0], far_above[0] = lax.optimization_barrier(
-        (first, second, far_below[0], far_above[0])
-    )
-    bubble = (first, second)
-
-    merged, halves, across = [], [], []
-    swap = [(0, 1), (1, 0)]
+    tables = (form, rows_l, rows_r, rows_f)
+    bounds = [0, points // 2, points * 3 // 4, points]
+    spans = list(zip(bounds[:-1], bounds[1:]))
+    parts = [my_window[lo:hi] for lo, hi in spans]
+    right, below, above = lax.optimization_barrier((right, below, above))
+    far_below = [lax.ppermute(piece, "mom", [(1, 2)]) for piece in below]
+    far_above = [lax.ppermute(piece, "mom", [(2, 1)]) for piece in above]
+    loops = [loop_matrices(parts[0], column, left, right, *tables)]
+    weights, loops[0] = lax.optimization_barrier((weights, loops[0]))
+
+    sums, sent = [], []
     for i in range(CHUNKS):
         stack = jnp.concatenate([far_below[i], below[i], pieces[i], above[i], far_above[i]], axis=0)
         tiles = stack.reshape(5 * points, chunk_pairs, form_count, col_count)
-        sums = jnp.einsum("qlpm,pamc->qalc", weights, tiles, preferred_element_type=jnp.float32)
-        sums = sums.reshape(2 * points, chunk_rows, col_count)
-        outer = lax.ppermute(sums[points:].astype(jnp.bfloat16), "mom", [(2, 3), (1, 0)])
+        both = jnp.einsum("qplm,pamc->qalc", weights, tiles, preferred_element_type=jnp.float32)
+        both = both.reshape(2 * points, chunk_rows, col_count)
+        sums.append(both[:points])
+        sent.append(both[points:].astype(jnp.bfloat16))
+        if i + 1 < CHUNKS:
+            sent[i], far_below[i + 1], far_above[i + 1] = lax.optimization_barrier(
+                (sent[i], far_below[i + 1], far_above[i + 1])
+            )
+    sent[-1], right = lax.optimization_barrier((sent[-1], right))
+    outer = [lax.ppermute(each, "mom", [(2, 3), (1, 0)]) for each in sent]
+    loops.append(loop_matrices(parts[1], column, left, right, *tables))
+
+    merged, halves, across, beside = [], [], [], []
+    swap = [(0, 1), (1, 0)]
+    for i in range(CHUNKS):
         mine = vertex_own[:, i * chunk_rows : (i + 1) * chunk_rows].astype(jnp.float32)
-        mine = (mine + sums[:points] + outer.astype(jnp.float32)).astype(jnp.bfloat16)
+        if i == 0:
+            outer[0], loops[1] = lax.optimization_barrier((outer[0], loops[1]))
+        mine = (mine + sums[i] + outer[i].astype(jnp.float32)).astype(jnp.bfloat16)
+        if i == 0:
+            mine, right = lax.optimization_barrier((mine, right))
+            loops.append(loop_matrices(parts[2], column, left, right, *tables))
         merged.append(mine)
         across.append(lax.ppermute(mine, "orb", swap))
-        beside = lax.ppermute(mine, "ff", swap)
-        rows = jnp.concatenate([mine, beside], axis=2)
-        parts = [
-            jnp.einsum("qrj,qji->qri", part, loops, preferred_element_type=jnp.float32)
-            for part, loops in zip((rows[:cut], rows[cut:]), bubble)
+        beside.append(lax.ppermute(mine, "ff", swap))
+    for i in range(CHUNKS):
+        rows = jnp.concatenate([merged[i], beside[i]], axis=2)
+        terms = [
+            jnp.einsum("qrj,qji->qri", rows[lo:hi], loop, preferred_element_type=jnp.float32)
+            for (lo, hi), loop in zip(spans, loops)
         ]
-        halves.append(jnp.concatenate(parts, axis=0).astype(jnp.bfloat16))
+        halves.append(jnp.concatenate(terms, axis=0).astype(jnp.bfloat16))
     half = jnp.concatenate(halves, axis=1)
     tall = jnp.concatenate(merged + across, axis=1)
     change = jnp.einsum("qri,qic->qrc", half, tall, preferred_element_type=jnp.float32)

time: 120 us -> 122 us (1.017)
  waiting for transfers between devices: 30.4 us -> 44.1 us
  local copies, waits for them, and re-layouts: 24.8 us -> 11.4 us
  starting transfers between devices: 30.2 us -> 27.9 us
  Pallas kernels: 22 us -> 23.7 us
    ppermute x8, waiting for transfers between devices: 19.5 us -> 31.5 us  [the longest x2 31.5 us: body_line(): outer = [lax.ppermute(each, 'mom', [(2, 3), (1, 0)]) for each in sent]]
    reshape x3 -> x0, local copies, waits for them, and re-layouts: 9.03 us -> none  [the longest x2 6.04 us: body_line(): weights = weights.reshape(2 * points, form_count, 5 * points, form_count)]
    ppermute x2, waiting for transfers between devices: 11 us -> 4.02 us  [body_line(): across.append(lax.ppermute(mine, 'orb', swap))]
    ppermute x2, waiting for transfers between devices: 0.01 us -> 3.74 us  [body_line(): above = [lax.ppermute(piece, 'mom', down) for piece in pieces]]
    ppermute x2, waiting for transfers between devices: 0.01 us -> 3.31 us  [body_line(): below = [lax.ppermute(piece, 'mom', up) for piece in pieces]]
    transpose x2 -> x0, local copies, waits for them, and re-layouts: 2.74 us -> none  [body_line(): padded = padded.transpose(0, 2, 1, 3).reshape(points * form_count, -1)]
    ppermute x8, starting transfers between devices: 8.19 us -> 5.79 us  [the longest x2 2.9 us: body_line(): outer = [lax.ppermute(each, 'mom', [(2, 3), (1, 0)]) for each in sent]]
    pad x3, local copies, waits for them, and re-layouts: 0.07 us -> 2.04 us  [padded_rows(): return jnp.pad(values, ((0, -values.shape[0] % step), (0, 0)))]
  transfers between devices with their start and end apart: 15 -> 15, of which waited for: 4 -> 6; matrix products, arithmetic and copies ran while one was open for 25% -> 13% of each run, Pallas kernels for 18% -> 20%
where the time goes in v5:
time: 122 us
  waiting for transfers between devices  44.1 us (36%)
  starting transfers between devices  27.9 us (23%)
  Pallas kernels  23.7 us (19%)
  local copies, waits for them, and re-layouts  11.4 us (9%)
  matrix products  10 us (8%)
  other arithmetic  3.98 us (3%)
    ppermute x2, waiting for transfers between devices, body_line(): outer = [lax.ppermute(each, 'mom', [(2, 3), (1, 0)]) for each in sent]  31.5 us
    pallas_call x3, Pallas kernels, loop_matrices(): pl.pallas_call(loop_kernel, grid=(points,), out_shape=jax.ShapeDtypeStruc...  23.7 us
    ppermute x2, starting transfers between devices, body_line(): below = [lax.ppermute(piece, 'mom', up) for piece in pieces]  11.1 us
    ppermute x1, starting transfers between devices, body_line(): lax.ppermute(jnp.where(place == 3, to_two, to_one), 'mom', [(3, 2), (0, 1)])  5.41 us
    unnamed x20, local copies, waits for them, and re-layouts  4.76 us
    dot_general x6, matrix products, body_line(): jnp.einsum('qrj,qji->qri', rows[lo:hi], loop, preferred_element_type=jnp....  4.52 us
    ppermute x2, waiting for transfers between devices, body_line(): across.append(lax.ppermute(mine, 'orb', swap))  4.02 us
    ppermute x2, waiting for transfers between devices, body_line(): above = [lax.ppermute(piece, 'mom', down) for piece in pieces]  3.74 us
  transfers between devices with their start and end apart: 15, of which 6 were waited for; matrix products, arithmetic and copies ran while one was open for 13% of the time, Pallas kernels for 20%

profile of v5, /device:TPU:0, one launch (start us, length us, event | category | flops | bytes accessed | tf_op | source)
XLA Modules:
  0.0 121.7 jit_solution(7937741010878976538)
XLA Ops:
  0.0 2.3 %fusion.57 = (bf16[8,117,234]{2,0,1:T(8,128)(2,1)}, bf16[8,117,234]{2,0,1:T(8,128)(2,1)}) fusion(bf16[8,234,234]{2,0,1:T(8,128)(2,1)} %param.8), kind=kLoop, calls=%fused_computation.105 | loop fusion | bytes 1752192 | tf_op jit(solution)/shard_map/slice | solution.py:166
  2.3 5.7 %collective-permute-start = (bf16[8,117,234]{2,0,1:T(8,128)(2,1)}, bf16[8,117,234]{2,0,1:T(8,128)(2,1)}, u32[]{:S(2)}, u32[]{:S(2)}) collective-permute-start(bf16[8,117,234]{2,0,1:T(8,128)(2,1)} %get-tuple-element.40), channel_id=1, source_target_pairs={{0,4},{4,8},{8,12},{1,5},{5,9},{9,13},{2,6},{6,10},{10,14},{3,7},{... | collective-permute-start | bytes 1314152 | tf_op jit(solution)/shard_map/ppermute | solution.py:168
  8.0 1.3 %collective-permute-start.2 = (bf16[8,117,234]{2,0,1:T(8,128)(2,1)}, bf16[8,117,234]{2,0,1:T(8,128)(2,1)}, u32[]{:S(2)}, u32[]{:S(2)}) collective-permute-start(bf16[8,117,234]{2,0,1:T(8,128)(2,1)} %get-tuple-element.40), channel_id=1, source_target_pairs={{4,0},{8,4},{12,8},{5,1},{9,5},{13,9},{6,2},{10,6},{14,10},{7,3},{... | collective-permute-start | bytes 1314152 | tf_op jit(solution)/shard_map/ppermute | solution.py:169
  9.3 5.3 %collective-permute-start.1 = (bf16[8,117,234]{2,0,1:T(8,128)(2,1)}, bf16[8,117,234]{2,0,1:T(8,128)(2,1)}, u32[]{:S(2)}, u32[]{:S(2)}) collective-permute-start(bf16[8,117,234]{2,0,1:T(8,128)(2,1)} %get-tuple-element.39), channel_id=1, source_target_pairs={{0,4},{4,8},{8,12},{1,5},{5,9},{9,13},{2,6},{6,10},{10,14},{3,7},{... | collective-permute-start | bytes 1314152 | tf_op jit(solution)/shard_map/ppermute | solution.py:168
  14.6 1.3 %collective-permute-start.3 = (bf16[8,117,234]{2,0,1:T(8,128)(2,1)}, bf16[8,117,234]{2,0,1:T(8,128)(2,1)}, u32[]{:S(2)}, u32[]{:S(2)}) collective-permute-start(bf16[8,117,234]{2,0,1:T(8,128)(2,1)} %get-tuple-element.39), channel_id=1, source_target_pairs={{4,0},{8,4},{12,8},{5,1},{9,5},{13,9},{6,2},{10,6},{14,10},{7,3},{... | collective-permute-start | bytes 1314152 | tf_op jit(solution)/shard_map/ppermute | solution.py:169
  17.0 5.4 %collective-permute-start.6 = (bf16[8,40,13,13]{1,0,3,2:T(8,128)(2,1)}, bf16[8,40,13,13]{1,0,3,2:T(8,128)(2,1)}, u32[]{:S(2)}, u32[]{:S(2)}) collective-permute-start(bf16[8,40,13,13]{1,0,3,2:T(8,128)(2,1)} %pad_select_fusion), channel_id=1, source_target_pairs={{12,8},{0,4},{13,9},{1,5},{14,10},{2,6},{15,11},{3,7},{28,24},{16,... | collective-permute-start | bytes 324488 | tf_op jit(solution)/shard_map/ppermute | solution.py:160
  23.6 1.0 pad.23.right_ref
  24.7 1.0 pad.27.left_ref
  25.8 3.3 %collective-permute-done.1 = bf16[8,117,234]{2,0,1:T(8,128)(2,1)} collective-permute-done((bf16[8,117,234]{2,0,1:T(8,128)(2,1)}, bf16[8,117,234]{2,0,1:T(8,128)(2,1)}, u32[]{:S(2)}, u32[]{:S(2)}) %collective-permute-start.1) | collective-permute-done | bytes 438080 | tf_op jit(solution)/shard_map/ppermute | solution.py:168
  29.1 3.7 %collective-permute-done.3 = bf16[8,117,234]{2,0,1:T(8,128)(2,1)} collective-permute-done((bf16[8,117,234]{2,0,1:T(8,128)(2,1)}, bf16[8,117,234]{2,0,1:T(8,128)(2,1)}, u32[]{:S(2)}, u32[]{:S(2)}) %collective-permute-start.3) | collective-permute-done | bytes 438080 | tf_op jit(solution)/shard_map/ppermute | solution.py:169
  33.9 1.5 %collective-permute-done.6 = bf16[8,40,13,13]{1,0,3,2:T(8,128)(2,1)} collective-permute-done((bf16[8,40,13,13]{1,0,3,2:T(8,128)(2,1)}, bf16[8,40,13,13]{1,0,3,2:T(8,128)(2,1)}, u32[]{:S(2)}, u32[]{:S(2)}) %collective-permute-start.6) | collective-permute-done | bytes 108192 | tf_op jit(solution)/shard_map/ppermute | solution.py:160
  35.4 1.1 pad_maximum_fusion.2
  36.6 11.0 %shard_map.73 = bf16[4,468,468]{2,1,0:T(8,128)(2,1)S(1)} custom-call(s32[4]{0:T(128)S(1)} %bitcast.44, s32[1,2304]{1,0:T(1,128)S(1)} %and_select_fusion.column_ref, f32[40,2304]{1,0:T(8,128)S(1)} %pad.27.left_ref, f32[40,2304]{1,0:T(8,128)S(1)} %pad.23.right_ref, f32[16,2304]{1,0:T(8,128)S(1)} %pad.28.form_ref, ...), custom_call_target="tpu_custom_call" | custom-call | flops 1000 | bytes 1000 | tf_op jit(solution)/shard_map/pallas_call | solution.py:126
  49.7 1.1 constant_dynamic-update-slice_fusion.3
  50.8 1.1 constant_dynamic-update-slice_fusion.1
  51.9 1.0 convolution_bitcast_fusion.1
  53.0 1.4 %constant_dynamic-update-slice_fusion.8 = bf16[40,117,234]{2,0,1:T(8,128)(2,1)S(1)} fusion(bf16[40,117,234]{2,0,1:T(8,128)(2,1)S(1)} %constant_dynamic-update-slice_fusion.9, bf16[8,117,234]{2,0,1:T(8,128)(2,1)} %collective-permute-done.1), kind=kLoop, calls=%fused_computation.64 | loop fusion | bytes 917280
  54.5 1.1 constant_dynamic-update-slice_fusion.6
  55.7 1.3 %collective-permute-start.9 = (bf16[8,117,234]{2,1,0:T(8,128)(2,1)S(1)}, bf16[8,117,234]{2,1,0:T(8,128)(2,1)S(1)}, u32[]{:S(2)}, u32[]{:S(2)}) collective-permute-start(bf16[8,117,234]{2,1,0:T(8,128)(2,1)S(1)} %copy.10), channel_id=1, source_target_pairs={{8,12},{4,0},{9,13},{5,1},{10,14},{6,2},{11,15},{7,3},{24,28},{20,... | collective-permute-start | bytes 1314152 | tf_op jit(solution)/shard_map/ppermute | solution.py:207
  57.0 1.0 convolution_bitcast_fusion
  58.2 1.6 %collective-permute-start.10 = (bf16[8,117,234]{2,1,0:T(8,128)(2,1)S(1)}, bf16[8,117,234]{2,1,0:T(8,128)(2,1)S(1)}, u32[]{:S(2)}, u32[]{:S(2)}) collective-permute-start(bf16[8,117,234]{2,1,0:T(8,128)(2,1)S(1)} %copy.13), channel_id=1, source_target_pairs={{8,12},{4,0},{9,13},{5,1},{10,14},{6,2},{11,15},{7,3},{24,28},{20,... | collective-permute-start | bytes 1314152 | tf_op jit(solution)/shard_map/ppermute | solution.py:207
  59.8 6.4 %shard_map.74 = bf16[2,468,468]{2,1,0:T(8,128)(2,1)S(1)} custom-call(s32[2]{0:T(128)S(1)} %get-tuple-element.46.window_ref, s32[1,2304]{1,0:T(1,128)S(1)} %and_select_fusion.column_ref, f32[40,2304]{1,0:T(8,128)S(1)} %pad.27.left_ref, f32[40,2304]{1,0:T(8,128)S(1)} %pad.23.right_ref, f32[16,2304]{1,0:T(8,128)S(1)} %pad.28.form_ref, ...), custom_call_target="tpu_custom_call" | custom-call | flops 1000 | bytes 1000 | tf_op jit(solution)/shard_map/pallas_call | solution.py:126
  66.2 25.8 %collective-permute-done.9 = bf16[8,117,234]{2,1,0:T(8,128)(2,1)S(1)} collective-permute-done((bf16[8,117,234]{2,1,0:T(8,128)(2,1)S(1)}, bf16[8,117,234]{2,1,0:T(8,128)(2,1)S(1)}, u32[]{:S(2)}, u32[]{:S(2)}) %collective-permute-start.9) | collective-permute-done | bytes 438080 | tf_op jit(solution)/shard_map/ppermute | solution.py:207
  92.7 1.6 %collective-permute-start.13 = (bf16[8,117,234]{2,1,0:T(8,128)(2,1)S(1)}, bf16[8,117,234]{2,1,0:T(8,128)(2,1)S(1)}, u32[]{:S(2)}, u32[]{:S(2)}) collective-permute-start(bf16[8,117,234]{2,1,0:T(8,128)(2,1)S(1)} %fusion.22), channel_id=1, source_target_pairs={{0,2},{2,0},{1,3},{3,1},{4,6},{6,4},{5,7},{7,5},{8,10},{10,8},{9,1... | collective-permute-start | bytes 1314152 | tf_op jit(solution)/shard_map/ppermute | solution.py:221
  94.2 5.6 %collective-permute-done.10 = bf16[8,117,234]{2,1,0:T(8,128)(2,1)S(1)} collective-permute-done((bf16[8,117,234]{2,1,0:T(8,128)(2,1)S(1)}, bf16[8,117,234]{2,1,0:T(8,128)(2,1)S(1)}, u32[]{:S(2)}, u32[]{:S(2)}) %collective-permute-start.10) | collective-permute-done | bytes 438080 | tf_op jit(solution)/shard_map/ppermute | solution.py:207
  100.3 1.5 %collective-permute-start.14 = (bf16[8,117,234]{2,1,0:T(8,128)(2,1)S(1)}, bf16[8,117,234]{2,1,0:T(8,128)(2,1)S(1)}, u32[]{:S(2)}, u32[]{:S(2)}) collective-permute-start(bf16[8,117,234]{2,1,0:T(8,128)(2,1)S(1)} %fusion.20), channel_id=1, source_target_pairs={{0,2},{2,0},{1,3},{3,1},{4,6},{6,4},{5,7},{7,5},{8,10},{10,8},{9,1... | collective-permute-start | bytes 1314152 | tf_op jit(solution)/shard_map/ppermute | solution.py:221
  101.9 6.4 %shard_map.75 = bf16[2,468,468]{2,1,0:T(8,128)(2,1)S(1)} custom-call(s32[2]{0:T(128)S(1)} %get-tuple-element.45.window_ref, s32[1,2304]{1,0:T(1,128)S(1)} %and_select_fusion.column_ref, f32[40,2304]{1,0:T(8,128)S(1)} %pad.27.left_ref, f32[40,2304]{1,0:T(8,128)S(1)} %pad.23.right_ref, f32[16,2304]{1,0:T(8,128)S(1)} %pad.28.form_ref, ...), custom_call_target="tpu_custom_call" | custom-call | flops 1000 | bytes 1000 | tf_op jit(solution)/shard_map/pallas_call | solution.py:126
  109.6 1.0 convolution_convert_fusion.1
  111.9 1.0 convolution_convert_fusion
  112.9 4.0 %collective-permute-done.14 = bf16[8,117,234]{2,1,0:T(8,128)(2,1)S(1)} collective-permute-done((bf16[8,117,234]{2,1,0:T(8,128)(2,1)S(1)}, bf16[8,117,234]{2,1,0:T(8,128)(2,1)S(1)}, u32[]{:S(2)}, u32[]{:S(2)}) %collective-permute-start.14) | collective-permute-done | bytes 438080 | tf_op jit(solution)/shard_map/ppermute | solution.py:221
  116.9 3.5 %add_convert_fusion = bf16[8,234,234]{2,1,0:T(8,128)(2,1)S(1)} fusion(bf16[8,117,234]{2,1,0:T(8,128)(2,1)S(1)} %fusion.20, bf16[8,117,234]{2,1,0:T(8,128)(2,1)S(1)} %fusion.22, bf16[8,117,234]{2,1,0:T(8,128)(2,1)S(1)} %collective-permute-done.14, bf16[8,117,234]{2,1,0:T(8,128)(2,1)S(1)} %collective-permute-done.13, ...), kind=kOutput, calls=%fused_computation | convolution fusion | flops 430163136 | bytes 4380480 | tf_op jit(solution)/shard_map/qri,qic->qrc/dot_general | solution.py:232
  120.4 1.2 %copy.14 = bf16[8,234,234]{2,0,1:T(8,128)(2,1)} copy(bf16[8,234,234]{2,1,0:T(8,128)(2,1)S(1)} %add_convert_fusion) | data formatting | bytes 1752192 | tf_op jit(solution)/shard_map/convert_element_type | solution.py:234
  (64 shorter events, 9.6 us)
Async XLA Ops:
  0.0 15.9 %copy-start.2 = (bf16[8,32,13,13]{1,0,3,2:T(8,128)(2,1)S(1)}, bf16[8,32,13,13]{1,0,3,2:T(8,128)(2,1)}, u32[]{:S(2)}) copy-start(bf16[8,32,13,13]{1,0,3,2:T(8,128)(2,1)} %param.9) | copy-start | bytes 259588
  0.0 22.5 %copy-start.4 = (s32[13,2]{0,1:T(2,128)S(1)}, s32[13,2]{0,1:T(2,128)}, u32[]{:S(2)}) copy-start(s32[13,2]{0,1:T(2,128)} %param.13) | copy-start | bytes 316
  0.0 22.5 %copy-start.3 = (bf16[8,234,234]{2,0,1:T(8,128)(2,1)S(1)}, bf16[8,234,234]{2,0,1:T(8,128)(2,1)}, u32[]{:S(2)}) copy-start(bf16[8,234,234]{2,0,1:T(8,128)(2,1)} %param.7) | copy-start | bytes 2628292
  2.3 23.5 %collective-permute-start = (bf16[8,117,234]{2,0,1:T(8,128)(2,1)}, bf16[8,117,234]{2,0,1:T(8,128)(2,1)}, u32[]{:S(2)}, u32[]{:S(2)}) collective-permute-start(bf16[8,117,234]{2,0,1:T(8,128)(2,1)} %get-tuple-element.40), channel_id=1, source_target_pairs={{0,4},{4,8},{8,12},{1,5},{5,9},{9,13},{2,6},{6,10},{10,14},{3,7},{... | collective-permute-start | bytes 1314152 | tf_op jit(solution)/shard_map/ppermute | solution.py:168
  8.0 21.1 %collective-permute-start.2 = (bf16[8,117,234]{2,0,1:T(8,128)(2,1)}, bf16[8,117,234]{2,0,1:T(8,128)(2,1)}, u32[]{:S(2)}, u32[]{:S(2)}) collective-permute-start(bf16[8,117,234]{2,0,1:T(8,128)(2,1)} %get-tuple-element.40), channel_id=1, source_target_pairs={{4,0},{8,4},{12,8},{5,1},{9,5},{13,9},{6,2},{10,6},{14,10},{7,3},{... | collective-permute-start | bytes 1314152 | tf_op jit(solution)/shard_map/ppermute | solution.py:169
  9.3 19.9 %collective-permute-start.1 = (bf16[8,117,234]{2,0,1:T(8,128)(2,1)}, bf16[8,117,234]{2,0,1:T(8,128)(2,1)}, u32[]{:S(2)}, u32[]{:S(2)}) collective-permute-start(bf16[8,117,234]{2,0,1:T(8,128)(2,1)} %get-tuple-element.39), channel_id=1, source_target_pairs={{0,4},{4,8},{8,12},{1,5},{5,9},{9,13},{2,6},{6,10},{10,14},{3,7},{... | collective-permute-start | bytes 1314152 | tf_op jit(solution)/shard_map/ppermute | solution.py:168
  14.6 18.3 %collective-permute-start.3 = (bf16[8,117,234]{2,0,1:T(8,128)(2,1)}, bf16[8,117,234]{2,0,1:T(8,128)(2,1)}, u32[]{:S(2)}, u32[]{:S(2)}) collective-permute-start(bf16[8,117,234]{2,0,1:T(8,128)(2,1)} %get-tuple-element.39), channel_id=1, source_target_pairs={{4,0},{8,4},{12,8},{5,1},{9,5},{13,9},{6,2},{10,6},{14,10},{7,3},{... | collective-permute-start | bytes 1314152 | tf_op jit(solution)/shard_map/ppermute | solution.py:169
  17.0 8.7 %copy-start.5 = (s32[32]{0:T(128)S(1)}, s32[32]{0:T(128)}, u32[]{:S(2)}) copy-start(s32[32]{0:T(128)} %param.12) | copy-start | bytes 388
  17.0 18.4 %collective-permute-start.6 = (bf16[8,40,13,13]{1,0,3,2:T(8,128)(2,1)}, bf16[8,40,13,13]{1,0,3,2:T(8,128)(2,1)}, u32[]{:S(2)}, u32[]{:S(2)}) collective-permute-start(bf16[8,40,13,13]{1,0,3,2:T(8,128)(2,1)} %pad_select_fusion), channel_id=1, source_target_pairs={{12,8},{0,4},{13,9},{1,5},{14,10},{2,6},{15,11},{3,7},{28,24},{16,... | collective-permute-start | bytes 324488 | tf_op jit(solution)/shard_map/ppermute | solution.py:160
  32.9 16.8 %collective-permute-start.4 = (bf16[8,117,234]{2,0,1:T(8,128)(2,1)}, bf16[8,117,234]{2,0,1:T(8,128)(2,1)S(1)}, u32[]{:S(2)}, u32[]{:S(2)}) collective-permute-start(bf16[8,117,234]{2,0,1:T(8,128)(2,1)} %collective-permute-done), channel_id=1, source_target_pairs={{4,8},{5,9},{6,10},{7,11},{20,24},{21,25},{22,26},{23,27}} | collective-permute-start | bytes 1314152 | tf_op jit(solution)/shard_map/ppermute | solution.py:189
  36.6 14.2 %copy-start.1 = (bf16[8,234,234]{2,0,1:T(8,128)(2,1)S(1)}, bf16[8,234,234]{2,0,1:T(8,128)(2,1)}, u32[]{:S(2)}) copy-start(bf16[8,234,234]{2,0,1:T(8,128)(2,1)} %param.8) | copy-start | bytes 2628292
  47.5 4.3 %collective-permute-start.5 = (bf16[8,117,234]{2,0,1:T(8,128)(2,1)}, bf16[8,117,234]{2,0,1:T(8,128)(2,1)S(1)}, u32[]{:S(2)}, u32[]{:S(2)}) collective-permute-start(bf16[8,117,234]{2,0,1:T(8,128)(2,1)} %collective-permute-done.2), channel_id=1, source_target_pairs={{8,4},{9,5},{10,6},{11,7},{24,20},{25,21},{26,22},{27,23}} | collective-permute-start | bytes 1314152 | tf_op jit(solution)/shard_map/ppermute | solution.py:190
  48.2 4.8 %collective-permute-start.7 = (bf16[8,117,234]{2,0,1:T(8,128)(2,1)}, bf16[8,117,234]{2,0,1:T(8,128)(2,1)S(1)}, u32[]{:S(2)}, u32[]{:S(2)}) collective-permute-start(bf16[8,117,234]{2,0,1:T(8,128)(2,1)} %collective-permute-done.1), channel_id=1, source_target_pairs={{4,8},{5,9},{6,10},{7,11},{20,24},{21,25},{22,26},{23,27}} | collective-permute-start | bytes 1314152 | tf_op jit(solution)/shard_map/ppermute | solution.py:189
  48.9 4.1 %collective-permute-start.8 = (bf16[8,117,234]{2,0,1:T(8,128)(2,1)}, bf16[8,117,234]{2,0,1:T(8,128)(2,1)S(1)}, u32[]{:S(2)}, u32[]{:S(2)}) collective-permute-start(bf16[8,117,234]{2,0,1:T(8,128)(2,1)} %collective-permute-done.3), channel_id=1, source_target_pairs={{8,4},{9,5},{10,6},{11,7},{24,20},{25,21},{26,22},{27,23}} | collective-permute-start | bytes 1314152 | tf_op jit(solution)/shard_map/ppermute | solution.py:190
  52.9 1.6 %copy-start = (f32[16,9,13,234]{3,0,2,1:T(8,128)}, f32[16,9,13,234]{3,0,2,1:T(8,128)S(1)}, u32[]{:S(2)}) copy-start(f32[16,9,13,234]{3,0,2,1:T(8,128)S(1)} %convolution_bitcast_fusion.1) | copy-start | bytes 5256580
  55.7 36.4 %collective-permute-start.9 = (bf16[8,117,234]{2,1,0:T(8,128)(2,1)S(1)}, bf16[8,117,234]{2,1,0:T(8,128)(2,1)S(1)}, u32[]{:S(2)}, u32[]{:S(2)}) collective-permute-start(bf16[8,117,234]{2,1,0:T(8,128)(2,1)S(1)} %copy.10), channel_id=1, source_target_pairs={{8,12},{4,0},{9,13},{5,1},{10,14},{6,2},{11,15},{7,3},{24,28},{20,... | collective-permute-start | bytes 1314152 | tf_op jit(solution)/shard_map/ppermute | solution.py:207
  58.0 34.0 %slice-start = ((f32[16,9,13,234]{3,0,2,1:T(8,128)}), f32[8,9,13,234]{3,0,2,1:T(8,128)S(1)}, s32[]{:S(2)}) async-start(f32[16,9,13,234]{3,0,2,1:T(8,128)} %copy-done), calls=%async_computation | async-start | bytes 1916928 | tf_op jit(solution)/shard_map/slice | solution.py:200
  58.2 41.6 %collective-permute-start.10 = (bf16[8,117,234]{2,1,0:T(8,128)(2,1)S(1)}, bf16[8,117,234]{2,1,0:T(8,128)(2,1)S(1)}, u32[]{:S(2)}, u32[]{:S(2)}) collective-permute-start(bf16[8,117,234]{2,1,0:T(8,128)(2,1)S(1)} %copy.13), channel_id=1, source_target_pairs={{8,12},{4,0},{9,13},{5,1},{10,14},{6,2},{11,15},{7,3},{24,28},{20,... | collective-permute-start | bytes 1314152 | tf_op jit(solution)/shard_map/ppermute | solution.py:207
  92.5 15.8 %collective-permute-start.11 = (bf16[8,117,234]{2,1,0:T(8,128)(2,1)S(1)}, bf16[8,117,234]{2,1,0:T(8,128)(2,1)S(1)}, u32[]{:S(2)}, u32[]{:S(2)}) collective-permute-start(bf16[8,117,234]{2,1,0:T(8,128)(2,1)S(1)} %fusion.22), channel_id=1, source_target_pairs={{0,1},{1,0},{2,3},{3,2},{4,5},{5,4},{6,7},{7,6},{8,9},{9,8},{10,11... | collective-permute-start | bytes 1314152 | tf_op jit(solution)/shard_map/ppermute | solution.py:222
  92.7 20.2 %collective-permute-start.13 = (bf16[8,117,234]{2,1,0:T(8,128)(2,1)S(1)}, bf16[8,117,234]{2,1,0:T(8,128)(2,1)S(1)}, u32[]{:S(2)}, u32[]{:S(2)}) collective-permute-start(bf16[8,117,234]{2,1,0:T(8,128)(2,1)S(1)} %fusion.22), channel_id=1, source_target_pairs={{0,2},{2,0},{1,3},{3,1},{4,6},{6,4},{5,7},{7,5},{8,10},{10,8},{9,1... | collective-permute-start | bytes 1314152 | tf_op jit(solution)/shard_map/ppermute | solution.py:221
  100.3 10.3 %collective-permute-start.12 = (bf16[8,117,234]{2,1,0:T(8,128)(2,1)S(1)}, bf16[8,117,234]{2,1,0:T(8,128)(2,1)S(1)}, u32[]{:S(2)}, u32[]{:S(2)}) collective-permute-start(bf16[8,117,234]{2,1,0:T(8,128)(2,1)S(1)} %fusion.20), channel_id=1, source_target_pairs={{0,1},{1,0},{2,3},{3,2},{4,5},{5,4},{6,7},{7,6},{8,9},{9,8},{10,11... | collective-permute-start | bytes 1314152 | tf_op jit(solution)/shard_map/ppermute | solution.py:222
  100.3 16.5 %collective-permute-start.14 = (bf16[8,117,234]{2,1,0:T(8,128)(2,1)S(1)}, bf16[8,117,234]{2,1,0:T(8,128)(2,1)S(1)}, u32[]{:S(2)}, u32[]{:S(2)}) collective-permute-start(bf16[8,117,234]{2,1,0:T(8,128)(2,1)S(1)} %fusion.20), channel_id=1, source_target_pairs={{0,2},{2,0},{1,3},{3,1},{4,6},{6,4},{5,7},{7,5},{8,10},{10,8},{9,1... | collective-permute-start | bytes 1314152 | tf_op jit(solution)/shard_map/ppermute | solution.py:221

commit v6 on v5

--- a/solution.py
+++ b/solution.py
@@ -185,11 +185,10 @@
     bounds = [0, points // 2, points * 3 // 4, points]
     spans = list(zip(bounds[:-1], bounds[1:]))
     parts = [my_window[lo:hi] for lo, hi in spans]
-    right, below, above = lax.optimization_barrier((right, below, above))
+    loops = [loop_matrices(parts[0], column, left, right, *tables)]
+    loops, right, below, above = lax.optimization_barrier((loops, right, below, above))
     far_below = [lax.ppermute(piece, "mom", [(1, 2)]) for piece in below]
     far_above = [lax.ppermute(piece, "mom", [(2, 1)]) for piece in above]
-    loops = [loop_matrices(parts[0], column, left, right, *tables)]
-    weights, loops[0] = lax.optimization_barrier((weights, loops[0]))
 
     sums, sent = [], []
     for i in range(CHUNKS):
@@ -199,10 +198,6 @@
         both = both.reshape(2 * points, chunk_rows, col_count)
         sums.append(both[:points])
         sent.append(both[points:].astype(jnp.bfloat16))
-        if i + 1 < CHUNKS:
-            sent[i], far_below[i + 1], far_above[i + 1] = lax.optimization_barrier(
-                (sent[i], far_below[i + 1], far_above[i + 1])
-            )
     sent[-1], right = lax.optimization_barrier((sent[-1], right))
     outer = [lax.ppermute(each, "mom", [(2, 3), (1, 0)]) for each in sent]
     loops.append(loop_matrices(parts[1], column, left, right, *tables))

time: 122 us -> 105 us (0.86)
  waiting for transfers between devices: 44.1 us -> 26.8 us
  matrix products: 10 us -> 12 us
    ppermute x2, waiting for transfers between devices: 31.5 us -> 21.1 us  [body_line(): outer = [lax.ppermute(each, 'mom', [(2, 3), (1, 0)]) for each in sent]]
    ppermute x2, waiting for transfers between devices: 3.74 us -> 0.01 us  [body_line(): above = [lax.ppermute(piece, 'mom', down) for piece in pieces]]
    ppermute x2, waiting for transfers between devices: 3.31 us -> 0.01 us  [body_line(): below = [lax.ppermute(piece, 'mom', up) for piece in pieces]]
    pad x3, local copies, waits for them, and re-layouts: 2.04 us -> 0.07 us  [padded_rows(): return jnp.pad(values, ((0, -values.shape[0] % step), (0, 0)))]
    dot_general x2, matrix products: 1.96 us -> 3.93 us  [body_line(): jnp.einsum('qplm,pamc->qalc', weights, tiles, preferred_element_type=jnp....]
    ppermute x2, waiting for transfers between devices: 4.02 us -> 5.76 us  [body_line(): across.append(lax.ppermute(mine, 'orb', swap))]
    ppermute x1, waiting for transfers between devices: 1.54 us -> 0.01 us  [body_line(): lax.ppermute(jnp.where(place == 3, to_two, to_one), 'mom', [(3, 2), (0, 1)])]
    unnamed x20 -> x21, local copies, waits for them, and re-layouts: 4.76 us -> 4.4 us
  transfers between devices with their start and end apart: 15 -> 15, of which waited for: 6 -> 3; matrix products, arithmetic and copies ran while one was open for 13% -> 17% of each run, Pallas kernels for 20% -> 23%
where the time goes in v6:
time: 105 us; the launch traced here: 104 us
  starting transfers between devices  28.1 us (27%)
  waiting for transfers between devices  26.8 us (26%)
  Pallas kernels  23.8 us (23%)
  matrix products  12 us (11%)
  local copies, waits for them, and re-layouts  10.2 us (10%)
  other arithmetic  2.85 us (3%)
    pallas_call x3, Pallas kernels, loop_matrices(): pl.pallas_call(loop_kernel, grid=(points,), out_shape=jax.ShapeDtypeStruc...  23.8 us
    ppermute x2, waiting for transfers between devices, body_line(): outer = [lax.ppermute(each, 'mom', [(2, 3), (1, 0)]) for each in sent]  21.1 us
    ppermute x2, starting transfers between devices, body_line(): below = [lax.ppermute(piece, 'mom', up) for piece in pieces]  11.2 us
    ppermute x2, waiting for transfers between devices, body_line(): across.append(lax.ppermute(mine, 'orb', swap))  5.76 us
    ppermute x1, starting transfers between devices, body_line(): lax.ppermute(jnp.where(place == 3, to_two, to_one), 'mom', [(3, 2), (0, 1)])  5.28 us
    dot_general x6, matrix products, body_line(): jnp.einsum('qrj,qji->qri', rows[lo:hi], loop, preferred_element_type=jnp....  4.49 us
    unnamed x21, local copies, waits for them, and re-layouts  4.4 us
    dot_general x2, matrix products, body_line(): jnp.einsum('qplm,pamc->qalc', weights, tiles, preferred_element_type=jnp....  3.93 us
  transfers between devices with their start and end apart: 15, of which 3 were waited for; matrix products, arithmetic and copies ran while one was open for 17% of the time, Pallas kernels for 23%

profile of v6, /device:TPU:0, one launch (start us, length us, event | category | flops | bytes accessed | tf_op | source)
XLA Modules:
  0.0 104.4 jit_solution(15917269236125118884)
XLA Ops:
  0.0 2.2 %fusion.57 = (bf16[8,117,234]{2,0,1:T(8,128)(2,1)}, bf16[8,117,234]{2,0,1:T(8,128)(2,1)}) fusion(bf16[8,234,234]{2,0,1:T(8,128)(2,1)} %param.8), kind=kLoop, calls=%fused_computation.105 | loop fusion | bytes 1752192 | tf_op jit(solution)/shard_map/slice | solution.py:166
  2.2 5.9 %collective-permute-start = (bf16[8,117,234]{2,0,1:T(8,128)(2,1)}, bf16[8,117,234]{2,0,1:T(8,128)(2,1)}, u32[]{:S(2)}, u32[]{:S(2)}) collective-permute-start(bf16[8,117,234]{2,0,1:T(8,128)(2,1)} %get-tuple-element.34), channel_id=1, source_target_pairs={{0,4},{4,8},{8,12},{1,5},{5,9},{9,13},{2,6},{6,10},{10,14},{3,7},{... | collective-permute-start | bytes 1314152 | tf_op jit(solution)/shard_map/ppermute | solution.py:168
  8.1 1.3 %collective-permute-start.2 = (bf16[8,117,234]{2,0,1:T(8,128)(2,1)}, bf16[8,117,234]{2,0,1:T(8,128)(2,1)}, u32[]{:S(2)}, u32[]{:S(2)}) collective-permute-start(bf16[8,117,234]{2,0,1:T(8,128)(2,1)} %get-tuple-element.34), channel_id=1, source_target_pairs={{4,0},{8,4},{12,8},{5,1},{9,5},{13,9},{6,2},{10,6},{14,10},{7,3},{... | collective-permute-start | bytes 1314152 | tf_op jit(solution)/shard_map/ppermute | solution.py:169
  9.4 5.4 %collective-permute-start.1 = (bf16[8,117,234]{2,0,1:T(8,128)(2,1)}, bf16[8,117,234]{2,0,1:T(8,128)(2,1)}, u32[]{:S(2)}, u32[]{:S(2)}) collective-permute-start(bf16[8,117,234]{2,0,1:T(8,128)(2,1)} %get-tuple-element.33), channel_id=1, source_target_pairs={{0,4},{4,8},{8,12},{1,5},{5,9},{9,13},{2,6},{6,10},{10,14},{3,7},{... | collective-permute-start | bytes 1314152 | tf_op jit(solution)/shard_map/ppermute | solution.py:168
  14.7 1.3 %collective-permute-start.3 = (bf16[8,117,234]{2,0,1:T(8,128)(2,1)}, bf16[8,117,234]{2,0,1:T(8,128)(2,1)}, u32[]{:S(2)}, u32[]{:S(2)}) collective-permute-start(bf16[8,117,234]{2,0,1:T(8,128)(2,1)} %get-tuple-element.33), channel_id=1, source_target_pairs={{4,0},{8,4},{12,8},{5,1},{9,5},{13,9},{6,2},{10,6},{14,10},{7,3},{... | collective-permute-start | bytes 1314152 | tf_op jit(solution)/shard_map/ppermute | solution.py:169
  16.2 1.0 pad_select_fusion
  17.2 5.3 %collective-permute-start.6 = (bf16[8,40,13,13]{1,0,3,2:T(8,128)(2,1)}, bf16[8,40,13,13]{1,0,3,2:T(8,128)(2,1)}, u32[]{:S(2)}, u32[]{:S(2)}) collective-permute-start(bf16[8,40,13,13]{1,0,3,2:T(8,128)(2,1)} %pad_select_fusion), channel_id=1, source_target_pairs={{12,8},{0,4},{13,9},{1,5},{14,10},{2,6},{15,11},{3,7},{28,24},{16,... | collective-permute-start | bytes 324488 | tf_op jit(solution)/shard_map/ppermute | solution.py:160
  23.8 11.0 %shard_map.73 = bf16[4,468,468]{2,1,0:T(8,128)(2,1)S(1)} custom-call(s32[4]{0:T(128)S(1)} %bitcast.43, s32[1,2304]{1,0:T(1,128)S(1)} %and_select_fusion.column_ref, f32[40,2304]{1,0:T(8,128)S(1)} %pad.23.left_ref, f32[40,2304]{1,0:T(8,128)S(1)} %pad.24.right_ref, f32[16,2304]{1,0:T(8,128)S(1)} %pad.25.form_ref, ...), custom_call_target="tpu_custom_call" | custom-call | flops 1000 | bytes 1000 | tf_op jit(solution)/shard_map/pallas_call | solution.py:126
  35.1 0.7 collective-permute-start.8
  35.8 1.2 %fusion.56 = (bf16[8,117,234]{2,0,1:T(8,128)(2,1)S(1)}, bf16[8,117,234]{2,0,1:T(8,128)(2,1)S(1)}) fusion(bf16[8,234,234]{2,0,1:T(8,128)(2,1)} %param.7), kind=kLoop, calls=%fused_computation.104 | loop fusion | bytes 1752192 | tf_op jit(solution)/shard_map/slice | solution.py:208
  37.1 0.8 collective-permute-start.4
  38.0 0.7 collective-permute-start.5
  38.6 0.7 collective-permute-start.9
  39.4 1.1 %constant_dynamic-update-slice_fusion.8 = bf16[40,117,234]{2,0,1:T(8,128)(2,1)S(1)} fusion(bf16[40,117,234]{2,0,1:T(8,128)(2,1)S(1)} %constant_dynamic-update-slice_fusion.9, bf16[8,117,234]{2,0,1:T(8,128)(2,1)} %collective-permute-done.1), kind=kLoop, calls=%fused_computation.62 | loop fusion | bytes 917280
  40.5 1.1 %constant_dynamic-update-slice_fusion.3 = bf16[40,117,234]{2,0,1:T(8,128)(2,1)S(1)} fusion(bf16[40,117,234]{2,0,1:T(8,128)(2,1)S(1)} %constant_dynamic-update-slice_fusion.4, bf16[8,117,234]{2,0,1:T(8,128)(2,1)} %collective-permute-done), kind=kLoop, calls=%fused_computation.57 | loop fusion | bytes 917280
  41.7 1.1 %constant_dynamic-update-slice_fusion.1 = bf16[40,117,234]{2,0,1:T(8,128)(2,1)S(1)} fusion(bf16[40,117,234]{2,0,1:T(8,128)(2,1)S(1)} %get-tuple-element.31, bf16[8,117,234]{2,0,1:T(8,128)(2,1)} %collective-permute-done.2), kind=kLoop, calls=%fused_computation.55 | loop fusion | bytes 917280
  42.8 2.0 %convolution_bitcast_fusion.1 = f32[16,9,13,234]{3,0,2,1:T(8,128)S(1)} fusion(bf16[40,9,13,234,1]{3,0,2,4,1:T(8,128)(2,1)S(1)} %bitcast.49, bf16[8,40,13,13]{1,0,3,2:T(8,128)(2,1)} %collective-permute-done.6, bf16[8,40,13,13]{1,0,3,2:T(8,128)(2,1)S(1)} %pad_dynamic-slice_fusion), kind=kOutput, calls=%fused_computation.21 | convolution fusion | flops 456002560 | bytes 4158752 | tf_op jit(solution)/shard_map/qplm,pamc->qalc/dot_general | solution.py:197
  44.9 1.3 %collective-permute-start.7 = (bf16[8,117,234]{2,1,0:T(8,128)(2,1)S(1)}, bf16[8,117,234]{2,1,0:T(8,128)(2,1)S(1)}, u32[]{:S(2)}, u32[]{:S(2)}) collective-permute-start(bf16[8,117,234]{2,1,0:T(8,128)(2,1)S(1)} %copy.10), channel_id=1, source_target_pairs={{8,12},{4,0},{9,13},{5,1},{10,14},{6,2},{11,15},{7,3},{24,28},{20,... | collective-permute-start | bytes 1314152 | tf_op jit(solution)/shard_map/ppermute | solution.py:202
  46.2 1.1 %constant_dynamic-update-slice_fusion.6 = bf16[40,117,234]{2,0,1:T(8,128)(2,1)S(1)} fusion(bf16[40,117,234]{2,0,1:T(8,128)(2,1)S(1)} %get-tuple-element.32, bf16[8,117,234]{2,0,1:T(8,128)(2,1)} %collective-permute-done.3), kind=kLoop, calls=%fused_computation.60 | loop fusion | bytes 917280
  47.4 2.0 %convolution_bitcast_fusion = f32[16,9,13,234]{3,0,2,1:T(8,128)S(1)} fusion(bf16[40,9,13,234,1]{3,0,2,4,1:T(8,128)(2,1)S(1)} %bitcast.48, bf16[8,40,13,13]{1,0,3,2:T(8,128)(2,1)} %collective-permute-done.6, bf16[8,40,13,13]{1,0,3,2:T(8,128)(2,1)S(1)} %pad_dynamic-slice_fusion), kind=kOutput, calls=%fused_computation.20 | convolution fusion | flops 456002560 | bytes 4158752 | tf_op jit(solution)/shard_map/qplm,pamc->qalc/dot_general | solution.py:197
  49.5 1.6 %collective-permute-start.10 = (bf16[8,117,234]{2,1,0:T(8,128)(2,1)S(1)}, bf16[8,117,234]{2,1,0:T(8,128)(2,1)S(1)}, u32[]{:S(2)}, u32[]{:S(2)}) collective-permute-start(bf16[8,117,234]{2,1,0:T(8,128)(2,1)S(1)} %copy.13), channel_id=1, source_target_pairs={{8,12},{4,0},{9,13},{5,1},{10,14},{6,2},{11,15},{7,3},{24,28},{20,... | collective-permute-start | bytes 1314152 | tf_op jit(solution)/shard_map/ppermute | solution.py:202
  51.1 6.4 %shard_map.74 = bf16[2,468,468]{2,1,0:T(8,128)(2,1)S(1)} custom-call(s32[2]{0:T(128)S(1)} %get-tuple-element.40.window_ref, s32[1,2304]{1,0:T(1,128)S(1)} %and_select_fusion.column_ref, f32[40,2304]{1,0:T(8,128)S(1)} %pad.23.left_ref, f32[40,2304]{1,0:T(8,128)S(1)} %pad.24.right_ref, f32[16,2304]{1,0:T(8,128)S(1)} %pad.25.form_ref, ...), custom_call_target="tpu_custom_call" | custom-call | flops 1000 | bytes 1000 | tf_op jit(solution)/shard_map/pallas_call | solution.py:126
  57.6 17.2 %collective-permute-done.7 = bf16[8,117,234]{2,1,0:T(8,128)(2,1)S(1)} collective-permute-done((bf16[8,117,234]{2,1,0:T(8,128)(2,1)S(1)}, bf16[8,117,234]{2,1,0:T(8,128)(2,1)S(1)}, u32[]{:S(2)}, u32[]{:S(2)}) %collective-permute-start.7) | collective-permute-done | bytes 438080 | tf_op jit(solution)/shard_map/ppermute | solution.py:202
  75.3 1.6 %collective-permute-start.13 = (bf16[8,117,234]{2,1,0:T(8,128)(2,1)S(1)}, bf16[8,117,234]{2,1,0:T(8,128)(2,1)S(1)}, u32[]{:S(2)}, u32[]{:S(2)}) collective-permute-start(bf16[8,117,234]{2,1,0:T(8,128)(2,1)S(1)} %fusion.22), channel_id=1, source_target_pairs={{0,2},{2,0},{1,3},{3,1},{4,6},{6,4},{5,7},{7,5},{8,10},{10,8},{9,1... | collective-permute-start | bytes 1314152 | tf_op jit(solution)/shard_map/ppermute | solution.py:216
  76.9 3.9 %collective-permute-done.10 = bf16[8,117,234]{2,1,0:T(8,128)(2,1)S(1)} collective-permute-done((bf16[8,117,234]{2,1,0:T(8,128)(2,1)S(1)}, bf16[8,117,234]{2,1,0:T(8,128)(2,1)S(1)}, u32[]{:S(2)}, u32[]{:S(2)}) %collective-permute-start.10) | collective-permute-done | bytes 438080 | tf_op jit(solution)/shard_map/ppermute | solution.py:202
  81.3 1.6 %collective-permute-start.14 = (bf16[8,117,234]{2,1,0:T(8,128)(2,1)S(1)}, bf16[8,117,234]{2,1,0:T(8,128)(2,1)S(1)}, u32[]{:S(2)}, u32[]{:S(2)}) collective-permute-start(bf16[8,117,234]{2,1,0:T(8,128)(2,1)S(1)} %fusion.20), channel_id=1, source_target_pairs={{0,2},{2,0},{1,3},{3,1},{4,6},{6,4},{5,7},{7,5},{8,10},{10,8},{9,1... | collective-permute-start | bytes 1314152 | tf_op jit(solution)/shard_map/ppermute | solution.py:216
  82.8 6.4 %shard_map.75 = bf16[2,468,468]{2,1,0:T(8,128)(2,1)S(1)} custom-call(s32[2]{0:T(128)S(1)} %get-tuple-element.39.window_ref, s32[1,2304]{1,0:T(1,128)S(1)} %and_select_fusion.column_ref, f32[40,2304]{1,0:T(8,128)S(1)} %pad.23.left_ref, f32[40,2304]{1,0:T(8,128)S(1)} %pad.24.right_ref, f32[16,2304]{1,0:T(8,128)S(1)} %pad.25.form_ref, ...), custom_call_target="tpu_custom_call" | custom-call | flops 1000 | bytes 1000 | tf_op jit(solution)/shard_map/pallas_call | solution.py:126
  90.5 1.0 convolution_convert_fusion.1
  92.8 1.0 convolution_convert_fusion
  93.8 5.8 %collective-permute-done.14 = bf16[8,117,234]{2,1,0:T(8,128)(2,1)S(1)} collective-permute-done((bf16[8,117,234]{2,1,0:T(8,128)(2,1)S(1)}, bf16[8,117,234]{2,1,0:T(8,128)(2,1)S(1)}, u32[]{:S(2)}, u32[]{:S(2)}) %collective-permute-start.14) | collective-permute-done | bytes 438080 | tf_op jit(solution)/shard_map/ppermute | solution.py:216
  99.6 3.6 %add_convert_fusion = bf16[8,234,234]{2,1,0:T(8,128)(2,1)S(1)} fusion(bf16[8,117,234]{2,1,0:T(8,128)(2,1)S(1)} %fusion.20, bf16[8,117,234]{2,1,0:T(8,128)(2,1)S(1)} %fusion.22, bf16[8,117,234]{2,1,0:T(8,128)(2,1)S(1)} %collective-permute-done.14, bf16[8,117,234]{2,1,0:T(8,128)(2,1)S(1)} %collective-permute-done.13, ...), kind=kOutput, calls=%fused_computation | convolution fusion | flops 430163136 | bytes 4380480 | tf_op jit(solution)/shard_map/qri,qic->qrc/dot_general | solution.py:227
  103.1 1.2 %copy.14 = bf16[8,234,234]{2,0,1:T(8,128)(2,1)} copy(bf16[8,234,234]{2,1,0:T(8,128)(2,1)S(1)} %add_convert_fusion) | data formatting | bytes 1752192 | tf_op jit(solution)/shard_map/convert_element_type | solution.py:229
  (64 shorter events, 5.9 us)
Async XLA Ops:
  0.0 16.0 %copy-start.2 = (bf16[8,32,13,13]{1,0,3,2:T(8,128)(2,1)S(1)}, bf16[8,32,13,13]{1,0,3,2:T(8,128)(2,1)}, u32[]{:S(2)}) copy-start(bf16[8,32,13,13]{1,0,3,2:T(8,128)(2,1)} %param.9) | copy-start | bytes 259588
  0.0 22.5 %copy-start.5 = (s32[13,2]{0,1:T(2,128)S(1)}, s32[13,2]{0,1:T(2,128)}, u32[]{:S(2)}) copy-start(s32[13,2]{0,1:T(2,128)} %param.13) | copy-start | bytes 316
  0.0 23.2 %copy-start.3 = (f32[36,2304]{1,0:T(8,128)S(1)}, f32[36,2304]{1,0:T(8,128)}, u32[]{:S(2)}) copy-start(f32[36,2304]{1,0:T(8,128)} %param.10) | copy-start | bytes 995332
  2.2 21.0 %copy-start.4 = (f32[36,2304]{1,0:T(8,128)S(1)}, f32[36,2304]{1,0:T(8,128)}, u32[]{:S(2)}) copy-start(f32[36,2304]{1,0:T(8,128)} %param.11) | copy-start | bytes 995332
  2.2 32.8 %collective-permute-start = (bf16[8,117,234]{2,0,1:T(8,128)(2,1)}, bf16[8,117,234]{2,0,1:T(8,128)(2,1)}, u32[]{:S(2)}, u32[]{:S(2)}) collective-permute-start(bf16[8,117,234]{2,0,1:T(8,128)(2,1)} %get-tuple-element.34), channel_id=1, source_target_pairs={{0,4},{4,8},{8,12},{1,5},{5,9},{9,13},{2,6},{6,10},{10,14},{3,7},{... | collective-permute-start | bytes 1314152 | tf_op jit(solution)/shard_map/ppermute | solution.py:168
  8.1 27.0 %collective-permute-start.2 = (bf16[8,117,234]{2,0,1:T(8,128)(2,1)}, bf16[8,117,234]{2,0,1:T(8,128)(2,1)}, u32[]{:S(2)}, u32[]{:S(2)}) collective-permute-start(bf16[8,117,234]{2,0,1:T(8,128)(2,1)} %get-tuple-element.34), channel_id=1, source_target_pairs={{4,0},{8,4},{12,8},{5,1},{9,5},{13,9},{6,2},{10,6},{14,10},{7,3},{... | collective-permute-start | bytes 1314152 | tf_op jit(solution)/shard_map/ppermute | solution.py:169
  9.4 25.7 %collective-permute-start.1 = (bf16[8,117,234]{2,0,1:T(8,128)(2,1)}, bf16[8,117,234]{2,0,1:T(8,128)(2,1)}, u32[]{:S(2)}, u32[]{:S(2)}) collective-permute-start(bf16[8,117,234]{2,0,1:T(8,128)(2,1)} %get-tuple-element.33), channel_id=1, source_target_pairs={{0,4},{4,8},{8,12},{1,5},{5,9},{9,13},{2,6},{6,10},{10,14},{3,7},{... | collective-permute-start | bytes 1314152 | tf_op jit(solution)/shard_map/ppermute | solution.py:168
  14.7 20.4 %collective-permute-start.3 = (bf16[8,117,234]{2,0,1:T(8,128)(2,1)}, bf16[8,117,234]{2,0,1:T(8,128)(2,1)}, u32[]{:S(2)}, u32[]{:S(2)}) collective-permute-start(bf16[8,117,234]{2,0,1:T(8,128)(2,1)} %get-tuple-element.33), channel_id=1, source_target_pairs={{4,0},{8,4},{12,8},{5,1},{9,5},{13,9},{6,2},{10,6},{14,10},{7,3},{... | collective-permute-start | bytes 1314152 | tf_op jit(solution)/shard_map/ppermute | solution.py:169
  16.0 7.3 %copy-start.6 = (s32[32]{0:T(128)S(1)}, s32[32]{0:T(128)}, u32[]{:S(2)}) copy-start(s32[32]{0:T(128)} %param.12) | copy-start | bytes 388
  17.2 25.6 %collective-permute-start.6 = (bf16[8,40,13,13]{1,0,3,2:T(8,128)(2,1)}, bf16[8,40,13,13]{1,0,3,2:T(8,128)(2,1)}, u32[]{:S(2)}, u32[]{:S(2)}) collective-permute-start(bf16[8,40,13,13]{1,0,3,2:T(8,128)(2,1)} %pad_select_fusion), channel_id=1, source_target_pairs={{12,8},{0,4},{13,9},{1,5},{14,10},{2,6},{15,11},{3,7},{28,24},{16,... | collective-permute-start | bytes 324488 | tf_op jit(solution)/shard_map/ppermute | solution.py:160
  35.1 4.2 %collective-permute-start.8 = (bf16[8,117,234]{2,0,1:T(8,128)(2,1)}, bf16[8,117,234]{2,0,1:T(8,128)(2,1)S(1)}, u32[]{:S(2)}, u32[]{:S(2)}) collective-permute-start(bf16[8,117,234]{2,0,1:T(8,128)(2,1)} %collective-permute-done.1), channel_id=1, source_target_pairs={{4,8},{5,9},{6,10},{7,11},{20,24},{21,25},{22,26},{23,27}} | collective-permute-start | bytes 1314152 | tf_op jit(solution)/shard_map/ppermute | solution.py:190
  37.0 4.5 %copy-start.1 = (bf16[8,234,234]{2,0,1:T(8,128)(2,1)S(1)}, bf16[8,234,234]{2,0,1:T(8,128)(2,1)}, u32[]{:S(2)}) copy-start(bf16[8,234,234]{2,0,1:T(8,128)(2,1)} %param.8) | copy-start | bytes 2628292
  37.1 3.4 %collective-permute-start.4 = (bf16[8,117,234]{2,0,1:T(8,128)(2,1)}, bf16[8,117,234]{2,0,1:T(8,128)(2,1)S(1)}, u32[]{:S(2)}, u32[]{:S(2)}) collective-permute-start(bf16[8,117,234]{2,0,1:T(8,128)(2,1)} %collective-permute-done), channel_id=1, source_target_pairs={{4,8},{5,9},{6,10},{7,11},{20,24},{21,25},{22,26},{23,27}} | collective-permute-start | bytes 1314152 | tf_op jit(solution)/shard_map/ppermute | solution.py:190
  38.0 4.8 %collective-permute-start.5 = (bf16[8,117,234]{2,0,1:T(8,128)(2,1)}, bf16[8,117,234]{2,0,1:T(8,128)(2,1)S(1)}, u32[]{:S(2)}, u32[]{:S(2)}) collective-permute-start(bf16[8,117,234]{2,0,1:T(8,128)(2,1)} %collective-permute-done.2), channel_id=1, source_target_pairs={{8,4},{9,5},{10,6},{11,7},{24,20},{25,21},{26,22},{27,23}} | collective-permute-start | bytes 1314152 | tf_op jit(solution)/shard_map/ppermute | solution.py:191
  38.6 8.7 %collective-permute-start.9 = (bf16[8,117,234]{2,0,1:T(8,128)(2,1)}, bf16[8,117,234]{2,0,1:T(8,128)(2,1)S(1)}, u32[]{:S(2)}, u32[]{:S(2)}) collective-permute-start(bf16[8,117,234]{2,0,1:T(8,128)(2,1)} %collective-permute-done.3), channel_id=1, source_target_pairs={{8,4},{9,5},{10,6},{11,7},{24,20},{25,21},{26,22},{27,23}} | collective-permute-start | bytes 1314152 | tf_op jit(solution)/shard_map/ppermute | solution.py:191
  44.8 2.5 %copy-start = (f32[16,9,13,234]{3,0,2,1:T(8,128)}, f32[16,9,13,234]{3,0,2,1:T(8,128)S(1)}, u32[]{:S(2)}) copy-start(f32[16,9,13,234]{3,0,2,1:T(8,128)S(1)} %convolution_bitcast_fusion.1) | copy-start | bytes 5256580
  44.9 29.8 %collective-permute-start.7 = (bf16[8,117,234]{2,1,0:T(8,128)(2,1)S(1)}, bf16[8,117,234]{2,1,0:T(8,128)(2,1)S(1)}, u32[]{:S(2)}, u32[]{:S(2)}) collective-permute-start(bf16[8,117,234]{2,1,0:T(8,128)(2,1)S(1)} %copy.10), channel_id=1, source_target_pairs={{8,12},{4,0},{9,13},{5,1},{10,14},{6,2},{11,15},{7,3},{24,28},{20,... | collective-permute-start | bytes 1314152 | tf_op jit(solution)/shard_map/ppermute | solution.py:202
  49.3 25.4 %slice-start = ((f32[16,9,13,234]{3,0,2,1:T(8,128)}), f32[8,9,13,234]{3,0,2,1:T(8,128)S(1)}, s32[]{:S(2)}) async-start(f32[16,9,13,234]{3,0,2,1:T(8,128)} %copy-done), calls=%async_computation | async-start | bytes 1916928 | tf_op jit(solution)/shard_map/slice | solution.py:199
  49.5 31.3 %collective-permute-start.10 = (bf16[8,117,234]{2,1,0:T(8,128)(2,1)S(1)}, bf16[8,117,234]{2,1,0:T(8,128)(2,1)S(1)}, u32[]{:S(2)}, u32[]{:S(2)}) collective-permute-start(bf16[8,117,234]{2,1,0:T(8,128)(2,1)S(1)} %copy.13), channel_id=1, source_target_pairs={{8,12},{4,0},{9,13},{5,1},{10,14},{6,2},{11,15},{7,3},{24,28},{20,... | collective-permute-start | bytes 1314152 | tf_op jit(solution)/shard_map/ppermute | solution.py:202
  75.2 14.1 %collective-permute-start.11 = (bf16[8,117,234]{2,1,0:T(8,128)(2,1)S(1)}, bf16[8,117,234]{2,1,0:T(8,128)(2,1)S(1)}, u32[]{:S(2)}, u32[]{:S(2)}) collective-permute-start(bf16[8,117,234]{2,1,0:T(8,128)(2,1)S(1)} %fusion.22), channel_id=1, source_target_pairs={{0,1},{1,0},{2,3},{3,2},{4,5},{5,4},{6,7},{7,6},{8,9},{9,8},{10,11... | collective-permute-start | bytes 1314152 | tf_op jit(solution)/shard_map/ppermute | solution.py:217
  75.3 18.4 %collective-permute-start.13 = (bf16[8,117,234]{2,1,0:T(8,128)(2,1)S(1)}, bf16[8,117,234]{2,1,0:T(8,128)(2,1)S(1)}, u32[]{:S(2)}, u32[]{:S(2)}) collective-permute-start(bf16[8,117,234]{2,1,0:T(8,128)(2,1)S(1)} %fusion.22), channel_id=1, source_target_pairs={{0,2},{2,0},{1,3},{3,1},{4,6},{6,4},{5,7},{7,5},{8,10},{10,8},{9,1... | collective-permute-start | bytes 1314152 | tf_op jit(solution)/shard_map/ppermute | solution.py:216
  81.2 10.3 %collective-permute-start.12 = (bf16[8,117,234]{2,1,0:T(8,128)(2,1)S(1)}, bf16[8,117,234]{2,1,0:T(8,128)(2,1)S(1)}, u32[]{:S(2)}, u32[]{:S(2)}) collective-permute-start(bf16[8,117,234]{2,1,0:T(8,128)(2,1)S(1)} %fusion.20), channel_id=1, source_target_pairs={{0,1},{1,0},{2,3},{3,2},{4,5},{5,4},{6,7},{7,6},{8,9},{9,8},{10,11... | collective-permute-start | bytes 1314152 | tf_op jit(solution)/shard_map/ppermute | solution.py:217
  81.3 18.3 %collective-permute-start.14 = (bf16[8,117,234]{2,1,0:T(8,128)(2,1)S(1)}, bf16[8,117,234]{2,1,0:T(8,128)(2,1)S(1)}, u32[]{:S(2)}, u32[]{:S(2)}) collective-permute-start(bf16[8,117,234]{2,1,0:T(8,128)(2,1)S(1)} %fusion.20), channel_id=1, source_target_pairs={{0,2},{2,0},{1,3},{3,1},{4,6},{6,4},{5,7},{7,5},{8,10},{10,8},{9,1... | collective-permute-start | bytes 1314152 | tf_op jit(solution)/shard_map/ppermute | solution.py:216

commit v7 on v6

--- a/solution.py
+++ b/solution.py
@@ -139,7 +139,7 @@
     )(qpoints, *whole)
 
 
-CHUNKS = 2
+CHUNKS = 3
 ENDS = 4
 
 

time: 105 us -> 128 us (1.22)
  local copies, waits for them, and re-layouts: 10.2 us -> 21.1 us
  matrix products: 12 us -> 21.2 us
  starting transfers between devices: 28.1 us -> 36.1 us
  waiting for transfers between devices: 26.8 us -> 21 us
    dot_general x6 -> x9, matrix products: 4.49 us -> 13.1 us  [body_line(): jnp.einsum('qrj,qji->qri', rows[lo:hi], loop, preferred_element_type=jnp....]
    concatenate x0 -> x1, local copies, waits for them, and re-layouts: none -> 7.36 us  [body_line(): tall = jnp.concatenate(merged + across, axis=1)]
    ppermute x2 -> x3, waiting for transfers between devices: 5.76 us -> 0.01 us  [body_line(): across.append(lax.ppermute(mine, 'orb', swap))]
    ppermute x2 -> x3, starting transfers between devices: 11.2 us -> 15.5 us  [body_line(): below = [lax.ppermute(piece, 'mom', up) for piece in pieces]]
    unnamed x21 -> x46, local copies, waits for them, and re-layouts: 4.4 us -> 7.94 us
    dot_general x1, matrix products: 3.58 us -> 5.87 us  [body_line(): jnp.einsum('qri,qic->qrc', half, tall, preferred_element_type=jnp.float32)]
    dot_general x2 -> x3, matrix products: 3.93 us -> 2.2 us  [body_line(): jnp.einsum('qplm,pamc->qalc', weights, tiles, preferred_element_type=jnp....]
    ppermute x2 -> x3, starting transfers between devices: 2.56 us -> 3.86 us  [body_line(): above = [lax.ppermute(piece, 'mom', down) for piece in pieces]]
  transfers between devices with their start and end apart: 15 -> 22, of which waited for: 3 -> 3; matrix products, arithmetic and copies ran while one was open for 17% -> 20% of each run, Pallas kernels for 23% -> 19%
where the time goes in v7:
time: 128 us; the launch traced here: 127 us
  starting transfers between devices  36.1 us (28%)
  Pallas kernels  24 us (19%)
  matrix products  21.2 us (17%)
  local copies, waits for them, and re-layouts  21.1 us (16%)
  waiting for transfers between devices  21 us (16%)
  other arithmetic  2.79 us (2%)
    pallas_call x3, Pallas kernels, loop_matrices(): pl.pallas_call(loop_kernel, grid=(points,), out_shape=jax.ShapeDtypeStruc...  24 us
    ppermute x3, waiting for transfers between devices, body_line(): outer = [lax.ppermute(each, 'mom', [(2, 3), (1, 0)]) for each in sent]  20.9 us
    ppermute x3, starting transfers between devices, body_line(): below = [lax.ppermute(piece, 'mom', up) for piece in pieces]  15.5 us
    dot_general x9, matrix products, body_line(): jnp.einsum('qrj,qji->qri', rows[lo:hi], loop, preferred_element_type=jnp....  13.1 us
    unnamed x46, local copies, waits for them, and re-layouts  7.94 us
    concatenate x1, local copies, waits for them, and re-layouts, body_line(): tall = jnp.concatenate(merged + across, axis=1)  7.36 us
    dot_general x1, matrix products, body_line(): jnp.einsum('qri,qic->qrc', half, tall, preferred_element_type=jnp.float32)  5.87 us
    ppermute x1, starting transfers between devices, body_line(): lax.ppermute(jnp.where(place == 3, to_two, to_one), 'mom', [(3, 2), (0, 1)])  4.57 us
  transfers between devices with their start and end apart: 22, of which 3 were waited for; matrix products, arithmetic and copies ran while one was open for 20% of the time, Pallas kernels for 19%

profile of v7, /device:TPU:0, one launch (start us, length us, event | category | flops | bytes accessed | tf_op | source)
XLA Modules:
  0.0 126.8 jit_solution(2749819135274838321)
XLA Ops:
  0.0 2.2 %fusion.60 = (bf16[8,78,234]{2,0,1:T(8,128)(2,1)}, bf16[8,78,234]{2,0,1:T(8,128)(2,1)}, bf16[8,78,234]{2,0,1:T(8,128)(2,1)}) fusion(bf16[8,234,234]{2,0,1:T(8,128)(2,1)} %param.8), kind=kLoop, calls=%fused_computation.122 | loop fusion | bytes 1752192 | tf_op jit(solution)/shard_map/slice | solution.py:166
  2.2 4.9 %collective-permute-start = (bf16[8,78,234]{2,0,1:T(8,128)(2,1)}, bf16[8,78,234]{2,0,1:T(8,128)(2,1)S(1)}, u32[]{:S(2)}, u32[]{:S(2)}) collective-permute-start(bf16[8,78,234]{2,0,1:T(8,128)(2,1)} %get-tuple-element.40), channel_id=1, source_target_pairs={{0,4},{4,8},{8,12},{1,5},{5,9},{9,13},{2,6},{6,10},{10,14},{3,7},{... | collective-permute-start | bytes 876104 | tf_op jit(solution)/shard_map/ppermute | solution.py:168
  7.2 1.3 %collective-permute-start.3 = (bf16[8,78,234]{2,0,1:T(8,128)(2,1)}, bf16[8,78,234]{2,0,1:T(8,128)(2,1)}, u32[]{:S(2)}, u32[]{:S(2)}) collective-permute-start(bf16[8,78,234]{2,0,1:T(8,128)(2,1)} %get-tuple-element.40), channel_id=1, source_target_pairs={{4,0},{8,4},{12,8},{5,1},{9,5},{13,9},{6,2},{10,6},{14,10},{7,3},{... | collective-permute-start | bytes 876104 | tf_op jit(solution)/shard_map/ppermute | solution.py:169
  8.5 5.3 %collective-permute-start.1 = (bf16[8,78,234]{2,0,1:T(8,128)(2,1)}, bf16[8,78,234]{2,0,1:T(8,128)(2,1)}, u32[]{:S(2)}, u32[]{:S(2)}) collective-permute-start(bf16[8,78,234]{2,0,1:T(8,128)(2,1)} %get-tuple-element.41), channel_id=1, source_target_pairs={{0,4},{4,8},{8,12},{1,5},{5,9},{9,13},{2,6},{6,10},{10,14},{3,7},{... | collective-permute-start | bytes 876104 | tf_op jit(solution)/shard_map/ppermute | solution.py:168
  13.7 1.3 %collective-permute-start.4 = (bf16[8,78,234]{2,0,1:T(8,128)(2,1)}, bf16[8,78,234]{2,0,1:T(8,128)(2,1)}, u32[]{:S(2)}, u32[]{:S(2)}) collective-permute-start(bf16[8,78,234]{2,0,1:T(8,128)(2,1)} %get-tuple-element.41), channel_id=1, source_target_pairs={{4,0},{8,4},{12,8},{5,1},{9,5},{13,9},{6,2},{10,6},{14,10},{7,3},{... | collective-permute-start | bytes 876104 | tf_op jit(solution)/shard_map/ppermute | solution.py:169
  15.0 5.3 %collective-permute-start.2 = (bf16[8,78,234]{2,0,1:T(8,128)(2,1)}, bf16[8,78,234]{2,0,1:T(8,128)(2,1)}, u32[]{:S(2)}, u32[]{:S(2)}) collective-permute-start(bf16[8,78,234]{2,0,1:T(8,128)(2,1)} %get-tuple-element.39), channel_id=1, source_target_pairs={{0,4},{4,8},{8,12},{1,5},{5,9},{9,13},{2,6},{6,10},{10,14},{3,7},{... | collective-permute-start | bytes 876104 | tf_op jit(solution)/shard_map/ppermute | solution.py:168
  21.7 1.3 %collective-permute-start.5 = (bf16[8,78,234]{2,0,1:T(8,128)(2,1)}, bf16[8,78,234]{2,0,1:T(8,128)(2,1)}, u32[]{:S(2)}, u32[]{:S(2)}) collective-permute-start(bf16[8,78,234]{2,0,1:T(8,128)(2,1)} %get-tuple-element.39), channel_id=1, source_target_pairs={{4,0},{8,4},{12,8},{5,1},{9,5},{13,9},{6,2},{10,6},{14,10},{7,3},{... | collective-permute-start | bytes 876104 | tf_op jit(solution)/shard_map/ppermute | solution.py:169
  24.1 10.9 %shard_map.73 = bf16[4,468,468]{2,1,0:T(8,128)(2,1)S(1)} custom-call(s32[4]{0:T(128)S(1)} %bitcast.61, s32[1,2304]{1,0:T(1,128)S(1)} %and_select_fusion.column_ref, f32[40,2304]{1,0:T(8,128)S(1)} %pad.23.left_ref, f32[40,2304]{1,0:T(8,128)S(1)} %pad.24.right_ref, f32[16,2304]{1,0:T(8,128)S(1)} %pad.25.form_ref, ...), custom_call_target="tpu_custom_call" | custom-call | flops 1000 | bytes 1000 | tf_op jit(solution)/shard_map/pallas_call | solution.py:126
  35.1 1.3 %fusion.59 = (bf16[8,78,234]{2,0,1:T(8,128)(2,1)S(1)}, bf16[8,78,234]{2,0,1:T(8,128)(2,1)S(1)}, bf16[8,78,234]{2,0,1:T(8,128)(2,1)S(1)}) fusion(bf16[8,234,234]{2,0,1:T(8,128)(2,1)} %param.7), kind=kLoop, calls=%fused_computation.121 | loop fusion | bytes 1752192 | tf_op jit(solution)/shard_map/slice | solution.py:208
  36.4 4.6 %collective-permute-start.8 = (bf16[8,40,13,13]{1,0,3,2:T(8,128)(2,1)S(1)}, bf16[8,40,13,13]{1,0,3,2:T(8,128)(2,1)S(1)}, u32[]{:S(2)}, u32[]{:S(2)}) collective-permute-start(bf16[8,40,13,13]{1,0,3,2:T(8,128)(2,1)S(1)} %copy-done.11), channel_id=1, source_target_pairs={{12,8},{0,4},{13,9},{1,5},{14,10},{2,6},{15,11},{3,7},{28,24},{16,... | collective-permute-start | bytes 324488 | tf_op jit(solution)/shard_map/ppermute | solution.py:160
  51.8 1.3 %collective-permute-start.9 = (bf16[8,78,234]{2,1,0:T(8,128)(2,1)S(1)}, bf16[8,78,234]{2,1,0:T(8,128)(2,1)S(1)}, u32[]{:S(2)}, u32[]{:S(2)}) collective-permute-start(bf16[8,78,234]{2,1,0:T(8,128)(2,1)S(1)} %copy.10), channel_id=1, source_target_pairs={{8,12},{4,0},{9,13},{5,1},{10,14},{6,2},{11,15},{7,3},{24,28},{20,... | collective-permute-start | bytes 876104 | tf_op jit(solution)/shard_map/ppermute | solution.py:202
  53.2 1.3 %collective-permute-start.15 = (bf16[8,78,234]{2,1,0:T(8,128)(2,1)S(1)}, bf16[8,78,234]{2,1,0:T(8,128)(2,1)S(1)}, u32[]{:S(2)}, u32[]{:S(2)}) collective-permute-start(bf16[8,78,234]{2,1,0:T(8,128)(2,1)S(1)} %copy.16), channel_id=1, source_target_pairs={{8,12},{4,0},{9,13},{5,1},{10,14},{6,2},{11,15},{7,3},{24,28},{20,... | collective-permute-start | bytes 876104 | tf_op jit(solution)/shard_map/ppermute | solution.py:202
  57.4 1.6 %collective-permute-start.14 = (bf16[8,78,234]{2,1,0:T(8,128)(2,1)S(1)}, bf16[8,78,234]{2,1,0:T(8,128)(2,1)S(1)}, u32[]{:S(2)}, u32[]{:S(2)}) collective-permute-start(bf16[8,78,234]{2,1,0:T(8,128)(2,1)S(1)} %copy.13), channel_id=1, source_target_pairs={{8,12},{4,0},{9,13},{5,1},{10,14},{6,2},{11,15},{7,3},{24,28},{20,... | collective-permute-start | bytes 876104 | tf_op jit(solution)/shard_map/ppermute | solution.py:202
  59.0 6.4 %shard_map.74 = bf16[2,468,468]{2,1,0:T(8,128)(2,1)S(1)} custom-call(s32[2]{0:T(128)S(1)} %get-tuple-element.47.window_ref, s32[1,2304]{1,0:T(1,128)S(1)} %and_select_fusion.column_ref, f32[40,2304]{1,0:T(8,128)S(1)} %pad.23.left_ref, f32[40,2304]{1,0:T(8,128)S(1)} %pad.24.right_ref, f32[16,2304]{1,0:T(8,128)S(1)} %pad.25.form_ref, ...), custom_call_target="tpu_custom_call" | custom-call | flops 1000 | bytes 1000 | tf_op jit(solution)/shard_map/pallas_call | solution.py:126
  65.4 12.4 %collective-permute-done.9 = bf16[8,78,234]{2,1,0:T(8,128)(2,1)S(1)} collective-permute-done((bf16[8,78,234]{2,1,0:T(8,128)(2,1)S(1)}, bf16[8,78,234]{2,1,0:T(8,128)(2,1)S(1)}, u32[]{:S(2)}, u32[]{:S(2)}) %collective-permute-start.9) | collective-permute-done | bytes 292064 | tf_op jit(solution)/shard_map/ppermute | solution.py:202
  78.2 6.7 %collective-permute-done.15 = bf16[8,78,234]{2,1,0:T(8,128)(2,1)S(1)} collective-permute-done((bf16[8,78,234]{2,1,0:T(8,128)(2,1)S(1)}, bf16[8,78,234]{2,1,0:T(8,128)(2,1)S(1)}, u32[]{:S(2)}, u32[]{:S(2)}) %collective-permute-start.15) | collective-permute-done | bytes 292064 | tf_op jit(solution)/shard_map/ppermute | solution.py:202
  85.2 1.6 %collective-permute-start.21 = (bf16[8,78,234]{2,1,0:T(8,128)(2,1)S(1)}, bf16[8,78,234]{2,1,0:T(8,128)(2,1)S(1)}, u32[]{:S(2)}, u32[]{:S(2)}) collective-permute-start(bf16[8,78,234]{2,1,0:T(8,128)(2,1)S(1)} %fusion.21), channel_id=1, source_target_pairs={{0,2},{2,0},{1,3},{3,1},{4,6},{6,4},{5,7},{7,5},{8,10},{10,8},{9,1... | collective-permute-start | bytes 876104 | tf_op jit(solution)/shard_map/ppermute | solution.py:216
  86.8 1.8 %collective-permute-done.14 = bf16[8,78,234]{2,1,0:T(8,128)(2,1)S(1)} collective-permute-done((bf16[8,78,234]{2,1,0:T(8,128)(2,1)S(1)}, bf16[8,78,234]{2,1,0:T(8,128)(2,1)S(1)}, u32[]{:S(2)}, u32[]{:S(2)}) %collective-permute-start.14) | collective-permute-done | bytes 292064 | tf_op jit(solution)/shard_map/ppermute | solution.py:202
  89.0 1.6 %collective-permute-start.20 = (bf16[8,78,234]{2,1,0:T(8,128)(2,1)S(1)}, bf16[8,78,234]{2,1,0:T(8,128)(2,1)S(1)}, u32[]{:S(2)}, u32[]{:S(2)}) collective-permute-start(bf16[8,78,234]{2,1,0:T(8,128)(2,1)S(1)} %fusion.23), channel_id=1, source_target_pairs={{0,2},{2,0},{1,3},{3,1},{4,6},{6,4},{5,7},{7,5},{8,10},{10,8},{9,1... | collective-permute-start | bytes 876104 | tf_op jit(solution)/shard_map/ppermute | solution.py:216
  90.5 6.6 %shard_map.75 = bf16[2,468,468]{2,1,0:T(8,128)(2,1)S(1)} custom-call(s32[2]{0:T(128)S(1)} %get-tuple-element.46.window_ref, s32[1,2304]{1,0:T(1,128)S(1)} %and_select_fusion.column_ref, f32[40,2304]{1,0:T(8,128)S(1)} %pad.23.left_ref, f32[40,2304]{1,0:T(8,128)S(1)} %pad.24.right_ref, f32[16,2304]{1,0:T(8,128)S(1)} %pad.25.form_ref, ...), custom_call_target="tpu_custom_call" | custom-call | flops 1000 | bytes 1000 | tf_op jit(solution)/shard_map/pallas_call | solution.py:126
  97.7 1.8 %convolution_convert_fusion.2 = bf16[4,78,468]{1,2,0:T(8,128)(2,1)} fusion(bf16[4,468,468]{2,1,0:T(8,128)(2,1)S(1)} %shard_map.73, bf16[8,78,234]{2,1,0:T(8,128)(2,1)S(1)} %collective-permute-done.16, bf16[8,78,234]{2,1,0:T(8,128)(2,1)S(1)} %fusion.25), kind=kOutput, calls=%fused_computation.24 | convolution fusion | flops 137985120 | bytes 2628288 | tf_op jit(solution)/shard_map/qrj,qji->qri/dot_general | solution.py:221
  99.5 1.3 %convolution_convert_fusion.8 = bf16[2,78,468]{1,2,0:T(8,128)(2,1)} fusion(bf16[2,468,468]{2,1,0:T(8,128)(2,1)S(1)} %shard_map.74, bf16[8,78,234]{2,1,0:T(8,128)(2,1)S(1)} %collective-permute-done.16, bf16[8,78,234]{2,1,0:T(8,128)(2,1)S(1)} %fusion.25), kind=kOutput, calls=%fused_computation.30 | convolution fusion | flops 69576624 | bytes 1606176 | tf_op jit(solution)/shard_map/qrj,qji->qri/dot_general | solution.py:221
  100.8 1.8 %convolution_convert_fusion.1 = bf16[4,78,468]{1,2,0:T(8,128)(2,1)} fusion(bf16[4,468,468]{2,1,0:T(8,128)(2,1)S(1)} %shard_map.73, bf16[8,78,234]{2,1,0:T(8,128)(2,1)S(1)} %collective-permute-done.17, bf16[8,78,234]{2,1,0:T(8,128)(2,1)S(1)} %fusion.23), kind=kOutput, calls=%fused_computation.23 | convolution fusion | flops 137985120 | bytes 2628288 | tf_op jit(solution)/shard_map/qrj,qji->qri/dot_general | solution.py:221
  102.6 1.3 %convolution_convert_fusion.6 = bf16[2,78,468]{1,2,0:T(8,128)(2,1)} fusion(bf16[2,468,468]{2,1,0:T(8,128)(2,1)S(1)} %shard_map.74, bf16[8,78,234]{2,1,0:T(8,128)(2,1)S(1)} %collective-permute-done.17, bf16[8,78,234]{2,1,0:T(8,128)(2,1)S(1)} %fusion.23), kind=kOutput, calls=%fused_computation.28 | convolution fusion | flops 69576624 | bytes 1606176 | tf_op jit(solution)/shard_map/qrj,qji->qri/dot_general | solution.py:221
  103.9 1.3 %convolution_convert_fusion.7 = bf16[2,78,468]{1,2,0:T(8,128)(2,1)} fusion(bf16[2,468,468]{2,1,0:T(8,128)(2,1)S(1)} %shard_map.75, bf16[8,78,234]{2,1,0:T(8,128)(2,1)S(1)} %collective-permute-done.16, bf16[8,78,234]{2,1,0:T(8,128)(2,1)S(1)} %fusion.25), kind=kOutput, calls=%fused_computation.29 | convolution fusion | flops 69576624 | bytes 1606176 | tf_op jit(solution)/shard_map/qrj,qji->qri/dot_general | solution.py:221
  105.2 1.3 %convolution_convert_fusion.5 = bf16[2,78,468]{1,2,0:T(8,128)(2,1)} fusion(bf16[2,468,468]{2,1,0:T(8,128)(2,1)S(1)} %shard_map.75, bf16[8,78,234]{2,1,0:T(8,128)(2,1)S(1)} %collective-permute-done.17, bf16[8,78,234]{2,1,0:T(8,128)(2,1)S(1)} %fusion.23), kind=kOutput, calls=%fused_computation.27 | convolution fusion | flops 69576624 | bytes 1606176 | tf_op jit(solution)/shard_map/qrj,qji->qri/dot_general | solution.py:221
  106.5 1.8 %convolution_convert_fusion = bf16[4,78,468]{1,2,0:T(8,128)(2,1)} fusion(bf16[4,468,468]{2,1,0:T(8,128)(2,1)S(1)} %shard_map.73, bf16[8,78,234]{2,1,0:T(8,128)(2,1)S(1)} %collective-permute-done.18, bf16[8,78,234]{2,1,0:T(8,128)(2,1)S(1)} %fusion.21), kind=kOutput, calls=%fused_computation.22 | convolution fusion | flops 137985120 | bytes 2628288 | tf_op jit(solution)/shard_map/qrj,qji->qri/dot_general | solution.py:221
  108.3 1.3 %convolution_convert_fusion.4 = bf16[2,78,468]{1,2,0:T(8,128)(2,1)} fusion(bf16[2,468,468]{2,1,0:T(8,128)(2,1)S(1)} %shard_map.74, bf16[8,78,234]{2,1,0:T(8,128)(2,1)S(1)} %collective-permute-done.18, bf16[8,78,234]{2,1,0:T(8,128)(2,1)S(1)} %fusion.21), kind=kOutput, calls=%fused_computation.26 | convolution fusion | flops 69576624 | bytes 1606176 | tf_op jit(solution)/shard_map/qrj,qji->qri/dot_general | solution.py:221
  109.6 1.3 %convolution_convert_fusion.3 = bf16[2,78,468]{1,2,0:T(8,128)(2,1)} fusion(bf16[2,468,468]{2,1,0:T(8,128)(2,1)S(1)} %shard_map.75, bf16[8,78,234]{2,1,0:T(8,128)(2,1)S(1)} %collective-permute-done.18, bf16[8,78,234]{2,1,0:T(8,128)(2,1)S(1)} %fusion.21), kind=kOutput, calls=%fused_computation.25 | convolution fusion | flops 69576624 | bytes 1606176 | tf_op jit(solution)/shard_map/qrj,qji->qri/dot_general | solution.py:221
  112.3 7.4 %concatenate.54 = bf16[8,468,234]{2,1,0:T(8,128)(2,1)S(1)} concatenate(bf16[8,78,234]{2,1,0:T(8,128)(2,1)S(1)} %fusion.25, bf16[8,78,234]{2,1,0:T(8,128)(2,1)S(1)} %copy-done.8, bf16[8,78,234]{2,1,0:T(8,128)(2,1)} %copy-done.5, bf16[8,78,234]{2,1,0:T(8,128)(2,1)S(1)} %collective-permute-done.19, bf16[8,78,234]{2,1,0:T(8,128)(2,1)} %copy-done.13, bf16[8,78,234]{2,1,0:T(8,128)(2,1)} %copy-done.12), dimensions={1} | concatenate | bytes 3504384 | tf_op jit(solution)/shard_map/concatenate | solution.py:226
  119.7 5.9 %add_convert_fusion = bf16[8,234,234]{2,1,0:T(8,128)(2,1)S(1)} fusion(bf16[8,468,234]{2,1,0:T(8,128)(2,1)S(1)} %concatenate.54, bf16[2,78,468]{1,2,0:T(8,128)(2,1)} %convolution_convert_fusion.3, bf16[2,78,468]{1,2,0:T(8,128)(2,1)} %convolution_convert_fusion.4, bf16[4,78,468]{1,2,0:T(8,128)(2,1)} %convolution_convert_fusion, ...), kind=kOutput, calls=%fused_computation | convolution fusion | flops 429287040 | bytes 5256576 | tf_op jit(solution)/shard_map/qri,qic->qrc/dot_general | solution.py:227
  125.6 1.2 copy.17
  (115 shorter events, 18.9 us)
Async XLA Ops:
  0.0 20.3 %copy-start.16 = (s32[13,2]{0,1:T(2,128)S(1)}, s32[13,2]{0,1:T(2,128)}, u32[]{:S(2)}) copy-start(s32[13,2]{0,1:T(2,128)} %param.13) | copy-start | bytes 316
  0.0 21.5 %copy-start.1 = (bf16[8,32,13,13]{1,0,3,2:T(8,128)(2,1)S(1)}, bf16[8,32,13,13]{1,0,3,2:T(8,128)(2,1)}, u32[]{:S(2)}) copy-start(bf16[8,32,13,13]{1,0,3,2:T(8,128)(2,1)} %param.9) | copy-start | bytes 259588
  2.2 19.4 %collective-permute-start = (bf16[8,78,234]{2,0,1:T(8,128)(2,1)}, bf16[8,78,234]{2,0,1:T(8,128)(2,1)S(1)}, u32[]{:S(2)}, u32[]{:S(2)}) collective-permute-start(bf16[8,78,234]{2,0,1:T(8,128)(2,1)} %get-tuple-element.40), channel_id=1, source_target_pairs={{0,4},{4,8},{8,12},{1,5},{5,9},{9,13},{2,6},{6,10},{10,14},{3,7},{... | collective-permute-start | bytes 876104 | tf_op jit(solution)/shard_map/ppermute | solution.py:168
  7.2 33.8 %collective-permute-start.3 = (bf16[8,78,234]{2,0,1:T(8,128)(2,1)}, bf16[8,78,234]{2,0,1:T(8,128)(2,1)}, u32[]{:S(2)}, u32[]{:S(2)}) collective-permute-start(bf16[8,78,234]{2,0,1:T(8,128)(2,1)} %get-tuple-element.40), channel_id=1, source_target_pairs={{4,0},{8,4},{12,8},{5,1},{9,5},{13,9},{6,2},{10,6},{14,10},{7,3},{... | collective-permute-start | bytes 876104 | tf_op jit(solution)/shard_map/ppermute | solution.py:169
  8.5 27.9 %collective-permute-start.1 = (bf16[8,78,234]{2,0,1:T(8,128)(2,1)}, bf16[8,78,234]{2,0,1:T(8,128)(2,1)}, u32[]{:S(2)}, u32[]{:S(2)}) collective-permute-start(bf16[8,78,234]{2,0,1:T(8,128)(2,1)} %get-tuple-element.41), channel_id=1, source_target_pairs={{0,4},{4,8},{8,12},{1,5},{5,9},{9,13},{2,6},{6,10},{10,14},{3,7},{... | collective-permute-start | bytes 876104 | tf_op jit(solution)/shard_map/ppermute | solution.py:168
  13.7 27.3 %collective-permute-start.4 = (bf16[8,78,234]{2,0,1:T(8,128)(2,1)}, bf16[8,78,234]{2,0,1:T(8,128)(2,1)}, u32[]{:S(2)}, u32[]{:S(2)}) collective-permute-start(bf16[8,78,234]{2,0,1:T(8,128)(2,1)} %get-tuple-element.41), channel_id=1, source_target_pairs={{4,0},{8,4},{12,8},{5,1},{9,5},{13,9},{6,2},{10,6},{14,10},{7,3},{... | collective-permute-start | bytes 876104 | tf_op jit(solution)/shard_map/ppermute | solution.py:169
  15.0 26.0 %collective-permute-start.2 = (bf16[8,78,234]{2,0,1:T(8,128)(2,1)}, bf16[8,78,234]{2,0,1:T(8,128)(2,1)}, u32[]{:S(2)}, u32[]{:S(2)}) collective-permute-start(bf16[8,78,234]{2,0,1:T(8,128)(2,1)} %get-tuple-element.39), channel_id=1, source_target_pairs={{0,4},{4,8},{8,12},{1,5},{5,9},{9,13},{2,6},{6,10},{10,14},{3,7},{... | collective-permute-start | bytes 876104 | tf_op jit(solution)/shard_map/ppermute | solution.py:168
  21.7 19.3 %collective-permute-start.5 = (bf16[8,78,234]{2,0,1:T(8,128)(2,1)}, bf16[8,78,234]{2,0,1:T(8,128)(2,1)}, u32[]{:S(2)}, u32[]{:S(2)}) collective-permute-start(bf16[8,78,234]{2,0,1:T(8,128)(2,1)} %get-tuple-element.39), channel_id=1, source_target_pairs={{4,0},{8,4},{12,8},{5,1},{9,5},{13,9},{6,2},{10,6},{14,10},{7,3},{... | collective-permute-start | bytes 876104 | tf_op jit(solution)/shard_map/ppermute | solution.py:169
  35.1 6.7 %copy-start.15 = (bf16[8,78,234]{2,0,1:T(8,128)(2,1)S(1)}, bf16[8,78,234]{2,0,1:T(8,128)(2,1)}, u32[]{:S(2)}) copy-start(bf16[8,78,234]{2,0,1:T(8,128)(2,1)} %copy-done.14) | copy-start | bytes 876100
  36.4 12.4 %collective-permute-start.8 = (bf16[8,40,13,13]{1,0,3,2:T(8,128)(2,1)S(1)}, bf16[8,40,13,13]{1,0,3,2:T(8,128)(2,1)S(1)}, u32[]{:S(2)}, u32[]{:S(2)}) collective-permute-start(bf16[8,40,13,13]{1,0,3,2:T(8,128)(2,1)S(1)} %copy-done.11), channel_id=1, source_target_pairs={{12,8},{0,4},{13,9},{1,5},{14,10},{2,6},{15,11},{3,7},{28,24},{16,... | collective-permute-start | bytes 324488 | tf_op jit(solution)/shard_map/ppermute | solution.py:160
  41.0 3.1 %collective-permute-start.10 = (bf16[8,78,234]{2,0,1:T(8,128)(2,1)}, bf16[8,78,234]{2,0,1:T(8,128)(2,1)S(1)}, u32[]{:S(2)}, u32[]{:S(2)}) collective-permute-start(bf16[8,78,234]{2,0,1:T(8,128)(2,1)} %collective-permute-done.2), channel_id=1, source_target_pairs={{4,8},{5,9},{6,10},{7,11},{20,24},{21,25},{22,26},{23,27}} | collective-permute-start | bytes 876104 | tf_op jit(solution)/shard_map/ppermute | solution.py:190
  41.8 4.1 %collective-permute-start.6 = (bf16[8,78,234]{2,0,1:T(8,128)(2,1)S(1)}, bf16[8,78,234]{2,0,1:T(8,128)(2,1)S(1)}, u32[]{:S(2)}, u32[]{:S(2)}) collective-permute-start(bf16[8,78,234]{2,0,1:T(8,128)(2,1)S(1)} %copy-done.15), channel_id=1, source_target_pairs={{4,8},{5,9},{6,10},{7,11},{20,24},{21,25},{22,26},{23,27}} | collective-permute-start | bytes 876104 | tf_op jit(solution)/shard_map/ppermute | solution.py:190
  42.7 4.0 %collective-permute-start.12 = (bf16[8,78,234]{2,0,1:T(8,128)(2,1)}, bf16[8,78,234]{2,0,1:T(8,128)(2,1)S(1)}, u32[]{:S(2)}, u32[]{:S(2)}) collective-permute-start(bf16[8,78,234]{2,0,1:T(8,128)(2,1)} %collective-permute-done.1), channel_id=1, source_target_pairs={{4,8},{5,9},{6,10},{7,11},{20,24},{21,25},{22,26},{23,27}} | collective-permute-start | bytes 876104 | tf_op jit(solution)/shard_map/ppermute | solution.py:190
  43.4 5.4 %collective-permute-start.11 = (bf16[8,78,234]{2,0,1:T(8,128)(2,1)}, bf16[8,78,234]{2,0,1:T(8,128)(2,1)S(1)}, u32[]{:S(2)}, u32[]{:S(2)}) collective-permute-start(bf16[8,78,234]{2,0,1:T(8,128)(2,1)} %collective-permute-done.5), channel_id=1, source_target_pairs={{8,4},{9,5},{10,6},{11,7},{24,20},{25,21},{26,22},{27,23}} | collective-permute-start | bytes 876104 | tf_op jit(solution)/shard_map/ppermute | solution.py:191
  44.1 6.8 %collective-permute-start.7 = (bf16[8,78,234]{2,0,1:T(8,128)(2,1)}, bf16[8,78,234]{2,0,1:T(8,128)(2,1)S(1)}, u32[]{:S(2)}, u32[]{:S(2)}) collective-permute-start(bf16[8,78,234]{2,0,1:T(8,128)(2,1)} %collective-permute-done.3), channel_id=1, source_target_pairs={{8,4},{9,5},{10,6},{11,7},{24,20},{25,21},{26,22},{27,23}} | collective-permute-start | bytes 876104 | tf_op jit(solution)/shard_map/ppermute | solution.py:191
  45.9 9.5 %collective-permute-start.13 = (bf16[8,78,234]{2,0,1:T(8,128)(2,1)}, bf16[8,78,234]{2,0,1:T(8,128)(2,1)S(1)}, u32[]{:S(2)}, u32[]{:S(2)}) collective-permute-start(bf16[8,78,234]{2,0,1:T(8,128)(2,1)} %collective-permute-done.4), channel_id=1, source_target_pairs={{8,4},{9,5},{10,6},{11,7},{24,20},{25,21},{26,22},{27,23}} | collective-permute-start | bytes 876104 | tf_op jit(solution)/shard_map/ppermute | solution.py:191
  49.6 6.7 %copy-start.3 = (f32[16,6,13,234]{3,0,2,1:T(8,128)}, f32[16,6,13,234]{3,0,2,1:T(8,128)S(1)}, u32[]{:S(2)}) copy-start(f32[16,6,13,234]{3,0,2,1:T(8,128)S(1)} %convolution_bitcast_fusion.1) | copy-start | bytes 3504388
  51.8 26.0 %collective-permute-start.9 = (bf16[8,78,234]{2,1,0:T(8,128)(2,1)S(1)}, bf16[8,78,234]{2,1,0:T(8,128)(2,1)S(1)}, u32[]{:S(2)}, u32[]{:S(2)}) collective-permute-start(bf16[8,78,234]{2,1,0:T(8,128)(2,1)S(1)} %copy.10), channel_id=1, source_target_pairs={{8,12},{4,0},{9,13},{5,1},{10,14},{6,2},{11,15},{7,3},{24,28},{20,... | collective-permute-start | bytes 876104 | tf_op jit(solution)/shard_map/ppermute | solution.py:202
  53.2 31.7 %collective-permute-start.15 = (bf16[8,78,234]{2,1,0:T(8,128)(2,1)S(1)}, bf16[8,78,234]{2,1,0:T(8,128)(2,1)S(1)}, u32[]{:S(2)}, u32[]{:S(2)}) collective-permute-start(bf16[8,78,234]{2,1,0:T(8,128)(2,1)S(1)} %copy.16), channel_id=1, source_target_pairs={{8,12},{4,0},{9,13},{5,1},{10,14},{6,2},{11,15},{7,3},{24,28},{20,... | collective-permute-start | bytes 876104 | tf_op jit(solution)/shard_map/ppermute | solution.py:202
  57.3 20.5 %slice-start.2 = ((f32[16,6,13,234]{3,0,2,1:T(8,128)}), f32[8,6,13,234]{3,0,2,1:T(8,128)S(1)}, s32[]{:S(2)}) async-start(f32[16,6,13,234]{3,0,2,1:T(8,128)} %copy-done.4), calls=%async_computation.2 | async-start | bytes 1277952 | tf_op jit(solution)/shard_map/slice | solution.py:199
  57.4 31.2 %collective-permute-start.14 = (bf16[8,78,234]{2,1,0:T(8,128)(2,1)S(1)}, bf16[8,78,234]{2,1,0:T(8,128)(2,1)S(1)}, u32[]{:S(2)}, u32[]{:S(2)}) collective-permute-start(bf16[8,78,234]{2,1,0:T(8,128)(2,1)S(1)} %copy.13), channel_id=1, source_target_pairs={{8,12},{4,0},{9,13},{5,1},{10,14},{6,2},{11,15},{7,3},{24,28},{20,... | collective-permute-start | bytes 876104 | tf_op jit(solution)/shard_map/ppermute | solution.py:202
  59.0 25.9 %slice-start.1 = ((f32[16,6,13,234]{3,0,2,1:T(8,128)}), f32[8,6,13,234]{3,0,2,1:T(8,128)S(1)}, s32[]{:S(2)}) async-start(f32[16,6,13,234]{3,0,2,1:T(8,128)} %copy-done.3), calls=%async_computation.1 | async-start | bytes 1277952 | tf_op jit(solution)/shard_map/slice | solution.py:199
  77.8 10.8 %slice-start = ((f32[16,6,13,234]{3,0,2,1:T(8,128)}), f32[8,6,13,234]{3,0,2,1:T(8,128)S(1)}, s32[]{:S(2)}) async-start(f32[16,6,13,234]{3,0,2,1:T(8,128)} %copy-done.2), calls=%async_computation | async-start | bytes 1277952 | tf_op jit(solution)/shard_map/slice | solution.py:199
  78.1 19.1 %collective-permute-start.16 = (bf16[8,78,234]{2,1,0:T(8,128)(2,1)S(1)}, bf16[8,78,234]{2,1,0:T(8,128)(2,1)S(1)}, u32[]{:S(2)}, u32[]{:S(2)}) collective-permute-start(bf16[8,78,234]{2,1,0:T(8,128)(2,1)S(1)} %fusion.25), channel_id=1, source_target_pairs={{0,1},{1,0},{2,3},{3,2},{4,5},{5,4},{6,7},{7,6},{8,9},{9,8},{10,11... | collective-permute-start | bytes 876104 | tf_op jit(solution)/shard_map/ppermute | solution.py:217
  85.1 24.5 %copy-start.5 = (bf16[8,78,234]{2,1,0:T(8,128)(2,1)}, bf16[8,78,234]{2,1,0:T(8,128)(2,1)S(1)}, u32[]{:S(2)}) copy-start(bf16[8,78,234]{2,1,0:T(8,128)(2,1)S(1)} %fusion.21) | copy-start | bytes 876100
  85.1 21.4 %collective-permute-start.18 = (bf16[8,78,234]{2,1,0:T(8,128)(2,1)S(1)}, bf16[8,78,234]{2,1,0:T(8,128)(2,1)S(1)}, u32[]{:S(2)}, u32[]{:S(2)}) collective-permute-start(bf16[8,78,234]{2,1,0:T(8,128)(2,1)S(1)} %fusion.21), channel_id=1, source_target_pairs={{0,1},{1,0},{2,3},{3,2},{4,5},{5,4},{6,7},{7,6},{8,9},{9,8},{10,11... | collective-permute-start | bytes 876104 | tf_op jit(solution)/shard_map/ppermute | solution.py:217
  85.2 25.7 %collective-permute-start.21 = (bf16[8,78,234]{2,1,0:T(8,128)(2,1)S(1)}, bf16[8,78,234]{2,1,0:T(8,128)(2,1)S(1)}, u32[]{:S(2)}, u32[]{:S(2)}) collective-permute-start(bf16[8,78,234]{2,1,0:T(8,128)(2,1)S(1)} %fusion.21), channel_id=1, source_target_pairs={{0,2},{2,0},{1,3},{3,1},{4,6},{6,4},{5,7},{7,5},{8,10},{10,8},{9,1... | collective-permute-start | bytes 876104 | tf_op jit(solution)/shard_map/ppermute | solution.py:216
  88.9 16.3 %copy-start.7 = (bf16[8,78,234]{2,1,0:T(8,128)(2,1)}, bf16[8,78,234]{2,1,0:T(8,128)(2,1)S(1)}, u32[]{:S(2)}) copy-start(bf16[8,78,234]{2,1,0:T(8,128)(2,1)S(1)} %fusion.23) | copy-start | bytes 876100
  88.9 11.9 %collective-permute-start.17 = (bf16[8,78,234]{2,1,0:T(8,128)(2,1)S(1)}, bf16[8,78,234]{2,1,0:T(8,128)(2,1)S(1)}, u32[]{:S(2)}, u32[]{:S(2)}) collective-permute-start(bf16[8,78,234]{2,1,0:T(8,128)(2,1)S(1)} %fusion.23), channel_id=1, source_target_pairs={{0,1},{1,0},{2,3},{3,2},{4,5},{5,4},{6,7},{7,6},{8,9},{9,8},{10,11... | collective-permute-start | bytes 876104 | tf_op jit(solution)/shard_map/ppermute | solution.py:217
  89.0 21.9 %collective-permute-start.20 = (bf16[8,78,234]{2,1,0:T(8,128)(2,1)S(1)}, bf16[8,78,234]{2,1,0:T(8,128)(2,1)S(1)}, u32[]{:S(2)}, u32[]{:S(2)}) collective-permute-start(bf16[8,78,234]{2,1,0:T(8,128)(2,1)S(1)} %fusion.23), channel_id=1, source_target_pairs={{0,2},{2,0},{1,3},{3,1},{4,6},{6,4},{5,7},{7,5},{8,10},{10,8},{9,1... | collective-permute-start | bytes 876104 | tf_op jit(solution)/shard_map/ppermute | solution.py:216
  97.2 15.2 %collective-permute-start.19 = (bf16[8,78,234]{2,1,0:T(8,128)(2,1)S(1)}, bf16[8,78,234]{2,1,0:T(8,128)(2,1)S(1)}, u32[]{:S(2)}, u32[]{:S(2)}) collective-permute-start(bf16[8,78,234]{2,1,0:T(8,128)(2,1)S(1)} %fusion.25), channel_id=1, source_target_pairs={{0,2},{2,0},{1,3},{3,1},{4,6},{6,4},{5,7},{7,5},{8,10},{10,8},{9,1... | collective-permute-start | bytes 876104 | tf_op jit(solution)/shard_map/ppermute | solution.py:216
  110.9 8.8 %copy-start.6 = (bf16[8,78,234]{2,1,0:T(8,128)(2,1)S(1)}, bf16[8,78,234]{2,1,0:T(8,128)(2,1)}, u32[]{:S(2)}) copy-start(bf16[8,78,234]{2,1,0:T(8,128)(2,1)} %copy-done.5) | copy-start | bytes 876100
  (11 other events, 26.2 us)
